TPU v7x, 32 devices: a whole 2x2x4 slice. The times are simulated.
32 devices in a mesh: dp: 8 (over y, x, core), tensor: 4 (over z).
Axes of the slice: x: 2, y: 2, z: 4, core: 2. Of those that a mesh axis runs over, the one named last changes fastest.
Arguments:
- tokens: bfloat16 [8192, 2048], P(('dp', 'tensor')), may hold values from -6 to 6
- attn_gain: bfloat16 [2048], P(('dp', 'tensor')), may hold values from 0.25 to 1.75
- w_query: bfloat16 [2048, 2048], P('dp', 'tensor'), may hold values from -0.125 to 0.125
- w_key: bfloat16 [2048, 256], P(('dp', 'tensor')), may hold values from -0.125 to 0.125
- w_value: bfloat16 [2048, 256], P(('dp', 'tensor')), may hold values from -0.125 to 0.125
- w_out: bfloat16 [2048, 2048], P('tensor', 'dp'), may hold values from -0.5 to 0.5
- mlp_gain: bfloat16 [2048], P(('dp', 'tensor')), may hold values from 0.25 to 1.75
- w_gate: bfloat16 [2048, 5632], P('dp', 'tensor'), may hold values from -0.125 to 0.125
- w_up: bfloat16 [2048, 5632], P('dp', 'tensor'), may hold values from -0.125 to 0.125
- w_down: bfloat16 [5632, 2048], P('tensor', 'dp'), may hold values from -0.15625 to 0.15625
- cotangent: bfloat16 [8192, 2048], P(('dp', 'tensor')), may hold values from -6 to 6
Outputs:
- output: bfloat16 [8192, 2048], P(('dp', 'tensor'))
- grad_tokens: float32 [8192, 2048], P(('dp', 'tensor'))
- grad_attn_gain: float32 [2048], P(('dp', 'tensor'))
- grad_query: float32 [2048, 2048], P('dp', 'tensor')
- grad_key: float32 [2048, 256], P(('dp', 'tensor'))
- grad_value: float32 [2048, 256], P(('dp', 'tensor'))
- grad_out: float32 [2048, 2048], P('tensor', 'dp')
- grad_mlp_gain: float32 [2048], P(('dp', 'tensor'))
- grad_gate: float32 [2048, 5632], P('dp', 'tensor')
- grad_up: float32 [2048, 5632], P('dp', 'tensor')
- grad_down: float32 [5632, 2048], P('tensor', 'dp')
All inputs are finite; a program needn't handle non-finite values.
Results may differ from a plain program's by a relative error of at most 0.019.
Values may be sent and summed in bfloat16 or wider, within the bound.
A program may use at most 320 MiB of HBM per device.

v0:
```python
import jax
import jax.numpy as jnp
from jax import lax
from jax.sharding import PartitionSpec as P

HEADS = 32
KV_HEADS = 4
HEAD_DIM = 64
SEQLEN = 1024


epsilon = 1e-05
theta_base = 10000.0


def rope_tables(length, head_width):
    halved = head_width // 2
    freqs = theta_base ** (-2.0 * jnp.arange(halved, dtype=jnp.float32) / head_width)
    angles = jnp.arange(length, dtype=jnp.float32)[:, None] * freqs[None, :]
    return (jnp.cos(angles), jnp.sin(angles))


def rotate(values, cosines, sines):
    halved = values.shape[-1] // 2
    first_half = values[..., :halved]
    second_half = values[..., halved:]
    return jnp.concatenate(
        [first_half * cosines - second_half * sines, second_half * cosines + first_half * sines],
        axis=-1,
    )


def product(left, right):
    return jnp.dot(left, right, preferred_element_type=jnp.float32)


def product_left(left, right):
    return lax.dot_general(
        left, right, (((0,), (0,)), ((), ())), preferred_element_type=jnp.float32
    )


def product_right(left, right):
    return lax.dot_general(
        left, right, (((1,), (1,)), ((), ())), preferred_element_type=jnp.float32
    )


def flatten_heads(blocks):
    seq_count, head_count, length, head_width = blocks.shape
    return blocks.transpose(0, 2, 1, 3).reshape(seq_count * length, head_count * head_width)


def split_heads(flat, seq_count, head_count):
    return flat.reshape(seq_count, -1, head_count, flat.shape[1] // head_count).transpose(
        0, 2, 1, 3
    )


def masked_scores(query_seq, key_seq, causal):
    scores = jnp.einsum(
        "hqd,kd->hqk", query_seq, key_seq, preferred_element_type=jnp.float32
    ) * HEAD_DIM ** (-0.5)
    return jnp.where(causal[None], scores, -jnp.inf)


def norm_back(grad_normed, unit_rows, scale_rows, gain):
    scaled_grad = grad_normed * gain
    return scale_rows * (
        scaled_grad - unit_rows * jnp.mean(scaled_grad * unit_rows, axis=-1, keepdims=True)
    )


def on_device(
    tokens, attn_gain, w_query, w_key, w_value, w_out, mlp_gain, w_gate, w_up, w_down, cotangent
):
    tensor_index = lax.axis_index("tensor")
    head_count = w_query.shape[1] // HEAD_DIM
    kv_index = tensor_index * head_count // (HEADS // KV_HEADS)
    key_full, value_full, gain_first, gain_second = (
        lax.all_gather(w_key, ("dp", "tensor"), axis=0, tiled=True),
        lax.all_gather(w_value, ("dp", "tensor"), axis=0, tiled=True),
        lax.all_gather(attn_gain, ("dp", "tensor"), axis=0, tiled=True),
        lax.all_gather(mlp_gain, ("dp", "tensor"), axis=0, tiled=True),
    )
    query_full, gate_full, up_full, out_full, down_full = (
        lax.all_gather(w_query, "dp", axis=0, tiled=True),
        lax.all_gather(w_gate, "dp", axis=0, tiled=True),
        lax.all_gather(w_up, "dp", axis=0, tiled=True),
        lax.all_gather(w_out, "dp", axis=1, tiled=True),
        lax.all_gather(w_down, "dp", axis=1, tiled=True),
    )
    key_own = lax.dynamic_slice_in_dim(key_full, kv_index * HEAD_DIM, HEAD_DIM, 1)
    value_own = lax.dynamic_slice_in_dim(value_full, kv_index * HEAD_DIM, HEAD_DIM, 1)
    gain_first = gain_first.astype(jnp.float32)
    gain_second = gain_second.astype(jnp.float32)
    cosines, sines = rope_tables(SEQLEN, HEAD_DIM)
    causal = jnp.arange(SEQLEN)[:, None] >= jnp.arange(SEQLEN)[None, :]
    residual = tokens.astype(jnp.float32)
    scale_first = lax.rsqrt(jnp.mean(residual * residual, axis=-1, keepdims=True) + epsilon)
    unit_first = residual * scale_first
    normed_first = lax.all_gather(
        (unit_first * gain_first).astype(jnp.bfloat16), "tensor", axis=0, tiled=True
    )
    all_rows = normed_first.shape[0]
    seq_count = all_rows // SEQLEN
    queries = rotate(
        split_heads(product(normed_first, query_full), seq_count, head_count), cosines, sines
    ).astype(jnp.bfloat16)
    keys_own = rotate(
        product(normed_first, key_own).reshape(seq_count, SEQLEN, HEAD_DIM), cosines, sines
    ).astype(jnp.bfloat16)
    values_own = (
        product(normed_first, value_own).astype(jnp.bfloat16).reshape(seq_count, SEQLEN, HEAD_DIM)
    )

    def attend_forward(pieces):
        query_seq, key_seq, value_seq = pieces
        scores = masked_scores(query_seq, key_seq, causal)
        row_max = jnp.max(scores, axis=-1, keepdims=True)
        exponent = jnp.exp(scores - row_max)
        summed = jnp.sum(exponent, axis=-1, keepdims=True)
        weights_low = (exponent / summed).astype(jnp.bfloat16)
        context_seq = jnp.einsum(
            "hqk,kd->hqd", weights_low, value_seq, preferred_element_type=jnp.float32
        )
        return (context_seq.astype(jnp.bfloat16), row_max + jnp.log(summed))

    context, log_sums = lax.map(attend_forward, (queries, keys_own, values_own))
    context_flat = flatten_heads(context)
    attn_part = product(context_flat, out_full)
    attn_rows = lax.psum_scatter(attn_part, "tensor", scatter_dimension=0, tiled=True)
    middle = residual + attn_rows
    scale_second = lax.rsqrt(jnp.mean(middle * middle, axis=-1, keepdims=True) + epsilon)
    unit_second = middle * scale_second
    normed_second = lax.all_gather(
        (unit_second * gain_second).astype(jnp.bfloat16), "tensor", axis=0, tiled=True
    )
    gate_pre = product(normed_second, gate_full)
    upward = product(normed_second, up_full)
    sigmoid_gate = jax.nn.sigmoid(gate_pre)
    silu_gate = gate_pre * sigmoid_gate
    hidden = (silu_gate * upward).astype(jnp.bfloat16)
    mlp_rows = lax.psum_scatter(
        product(hidden, down_full).astype(jnp.bfloat16), "tensor", scatter_dimension=0, tiled=True
    ).astype(jnp.float32)
    output = (middle + mlp_rows).astype(jnp.bfloat16)
    cot_all = lax.all_gather(cotangent, "tensor", axis=0, tiled=True)
    grad_hidden = product_right(cot_all, down_full)
    grad_down_w = product_left(hidden, cot_all)
    grad_gate_pre = (
        grad_hidden * upward * sigmoid_gate * (1.0 + gate_pre * (1.0 - sigmoid_gate))
    ).astype(jnp.bfloat16)
    grad_upward = (grad_hidden * silu_gate).astype(jnp.bfloat16)
    grad_gate_w = product_left(normed_second, grad_gate_pre)
    grad_up_w = product_left(normed_second, grad_upward)
    back_second = lax.psum_scatter(
        product_right(grad_gate_pre, gate_full) + product_right(grad_upward, up_full),
        "tensor",
        scatter_dimension=0,
        tiled=True,
    )
    grad_gain_second = jnp.sum(back_second * unit_second, axis=0)
    grad_middle = cotangent.astype(jnp.float32) + norm_back(
        back_second, unit_second, scale_second, gain_second
    )
    middle_all = lax.all_gather(grad_middle.astype(jnp.bfloat16), "tensor", axis=0, tiled=True)
    grad_out_w = product_left(context_flat, middle_all)
    grad_context = split_heads(
        product_right(middle_all, out_full).astype(jnp.bfloat16), seq_count, head_count
    )

    def attend_back(pieces):
        query_seq, key_seq, value_seq, grad_seq, lse_seq = pieces
        softmaxed = jnp.exp(masked_scores(query_seq, key_seq, causal) - lse_seq)
        grad_soft = jnp.einsum(
            "hqd,kd->hqk", grad_seq, value_seq, preferred_element_type=jnp.float32
        )
        mixed_sum = jnp.sum(softmaxed * grad_soft, axis=-1, keepdims=True)
        grad_scores = (softmaxed * (grad_soft - mixed_sum)).astype(jnp.bfloat16)
        inv_root = HEAD_DIM ** (-0.5)
        grad_query_seq = (
            jnp.einsum("hqk,kd->hqd", grad_scores, key_seq, preferred_element_type=jnp.float32)
            * inv_root
        )
        grad_key_seq = (
            jnp.einsum("hqk,hqd->hkd", grad_scores, query_seq, preferred_element_type=jnp.float32)
            * inv_root
        )
        grad_value_seq = jnp.einsum(
            "hqk,hqd->hkd",
            softmaxed.astype(jnp.bfloat16),
            grad_seq,
            preferred_element_type=jnp.float32,
        )
        return (grad_query_seq, grad_key_seq, grad_value_seq)

    grad_queries, grad_keys, grad_values = lax.map(
        attend_back, (queries, keys_own, values_own, grad_context, log_sums)
    )
    grad_queries = flatten_heads(rotate(grad_queries, cosines, -sines).astype(jnp.bfloat16))
    grad_keys = flatten_heads(rotate(grad_keys, cosines, -sines).astype(jnp.bfloat16))
    grad_values = flatten_heads(grad_values.astype(jnp.bfloat16))
    width = normed_first.shape[1]
    grad_query_w = product_left(normed_first, grad_queries)
    key_terms = (
        product_left(normed_first, grad_keys).reshape(width, head_count, HEAD_DIM).sum(axis=1)
    )
    value_terms = (
        product_left(normed_first, grad_values).reshape(width, head_count, HEAD_DIM).sum(axis=1)
    )
    empty_grad = jnp.zeros(key_full.shape, jnp.float32)
    grad_key_w = lax.dynamic_update_slice_in_dim(empty_grad, key_terms, kv_index * HEAD_DIM, 1)
    grad_value_w = lax.dynamic_update_slice_in_dim(empty_grad, value_terms, kv_index * HEAD_DIM, 1)
    tiled_key = jnp.tile(key_own.T, (head_count, 1))
    tiled_value = jnp.tile(value_own.T, (head_count, 1))
    back_first = (
        product_right(grad_queries, query_full)
        + product(grad_keys, tiled_key)
        + product(grad_values, tiled_value)
    )
    back_first = lax.psum_scatter(
        back_first.astype(jnp.bfloat16), "tensor", scatter_dimension=0, tiled=True
    ).astype(jnp.float32)
    grad_gain_first = jnp.sum(back_first * unit_first, axis=0)
    grad_tokens = grad_middle + norm_back(back_first, unit_first, scale_first, gain_first)
    sum_query, sum_gate, sum_up, sum_out, sum_down = (
        lax.psum_scatter(
            grad_query_w.astype(jnp.bfloat16), "dp", scatter_dimension=0, tiled=True
        ).astype(jnp.float32),
        lax.psum_scatter(
            grad_gate_w.astype(jnp.bfloat16), "dp", scatter_dimension=0, tiled=True
        ).astype(jnp.float32),
        lax.psum_scatter(
            grad_up_w.astype(jnp.bfloat16), "dp", scatter_dimension=0, tiled=True
        ).astype(jnp.float32),
        lax.psum_scatter(
            grad_out_w.astype(jnp.bfloat16), "dp", scatter_dimension=1, tiled=True
        ).astype(jnp.float32),
        lax.psum_scatter(
            grad_down_w.astype(jnp.bfloat16), "dp", scatter_dimension=1, tiled=True
        ).astype(jnp.float32),
    )
    sum_key, sum_value, sum_gain_first, sum_gain_second = (
        lax.psum_scatter(grad_key_w, ("dp", "tensor"), scatter_dimension=0, tiled=True),
        lax.psum_scatter(grad_value_w, ("dp", "tensor"), scatter_dimension=0, tiled=True),
        lax.psum_scatter(grad_gain_first, ("dp", "tensor"), scatter_dimension=0, tiled=True),
        lax.psum_scatter(grad_gain_second, ("dp", "tensor"), scatter_dimension=0, tiled=True),
    )
    return (
        output,
        grad_tokens,
        sum_gain_first,
        sum_query,
        sum_key,
        sum_value,
        sum_out,
        sum_gain_second,
        sum_gate,
        sum_up,
        sum_down,
    )


def solution(mesh):
    placed = (
        P(("dp", "tensor"), None),
        P(("dp", "tensor")),
        P("dp", "tensor"),
        P(("dp", "tensor"), None),
        P(("dp", "tensor"), None),
        P("tensor", "dp"),
        P(("dp", "tensor")),
        P("dp", "tensor"),
        P("dp", "tensor"),
        P("tensor", "dp"),
        P(("dp", "tensor"), None),
    )
    return jax.shard_map(
        on_device,
        mesh=mesh,
        in_specs=placed,
        out_specs=(
            P(("dp", "tensor"), None),
            P(("dp", "tensor"), None),
            P(("dp", "tensor")),
            P("dp", "tensor"),
            P(("dp", "tensor"), None),
            P(("dp", "tensor"), None),
            P("tensor", "dp"),
            P(("dp", "tensor")),
            P("dp", "tensor"),
            P("dp", "tensor"),
            P("tensor", "dp"),
        ),
        check_vma=False,
    )
```

profile of v0, /device:TPU:25, one launch (start us, length us, event | category | flops | bytes accessed | tf_op | source)
XLA Modules:
  0.0 1691.2 jit_solution(3564625273401012048)
XLA Ops:
  9.7 38.9 %all-reduce.5 = (bf16[2048]{0:T(1024)(128)(2,1)S(1)}, bf16[2048]{0:T(1024)(128)(2,1)S(1)}) all-reduce(bf16[2048]{0:T(1024)(128)(2,1)S(1)} %dynamic-update-slice, bf16[2048]{0:T(1024)(128)(2,1)S(1)} %dynamic-update-slice.1), channel_id=1, replica_groups=mesh['dp'=8,'tensor'=4] {'dp','tensor'}, use_global_device_ids=true, to_apply=%add | all-reduce | flops 4096 | bytes 16384
  56.7 8.5 all-gather.16.cloned.1.call-done
  65.2 80.0 %all-gather.12.cloned.1.call-done = bf16[1024,2048]{1,0:T(8,128)(2,1)} async-done(((bf16[256,2048]{1,0:T(8,128)(2,1)}), bf16[1024,2048]{1,0:T(8,128)(2,1)}) %all-gather.12.cloned.1.call-update) | async-done | bytes 4194320 | tf_op jit(solution)/shard_map/all_gather | solution.py:102
  149.5 26.9 %all-gather.14.cloned.1.call-done = bf16[2048,512]{1,0:T(8,128)(2,1)} async-done(((bf16[256,512]{1,0:T(8,128)(2,1)}), bf16[2048,512]{1,0:T(8,128)(2,1)}) %all-gather.14.cloned.1.call-update) | async-done | bytes 2097168 | tf_op jit(solution)/shard_map/all_gather | solution.py:87
  176.5 5.2 fusion.53
  182.1 14.2 fusion.52
  196.3 13.1 fusion
  209.4 22.7 %all-gather.18.cloned.1.call-done = bf16[2048,256]{1,0:T(8,128)(2,1)} async-done(((bf16[64,256]{1,0:T(8,128)(2,1)}), bf16[2048,256]{1,0:T(8,128)(2,1)}) %all-gather.18.cloned.1.call-update) | async-done | bytes 1048592 | tf_op jit(solution)/shard_map/all_gather | solution.py:82
  236.5 14.0 fusion.31
  250.5 11.5 all-gather.20.cloned.1.call-done
  262.0 7.2 fusion.54
  270.1 143.1 %reduce-scatter.12.cloned.1.call-done = f32[256,2048]{1,0:T(8,128)} async-done(((f32[1024,2048]{1,0:T(8,128)}), f32[256,2048]{1,0:T(8,128)}) %reduce-scatter.12.cloned.1.call-update) | async-done | bytes 2097168 | tf_op jit(solution)/shard_map/reduce_scatter | solution.py:132
  418.7 41.2 %all-gather.26.cloned.1.call-done = bf16[2048,1408]{1,0:T(8,128)(2,1)} async-done(((bf16[256,1408]{1,0:T(8,128)(2,1)}), bf16[2048,1408]{1,0:T(8,128)(2,1)}) %all-gather.26.cloned.1.call-update) | async-done | bytes 5767184 | tf_op jit(solution)/shard_map/all_gather | solution.py:89
  459.9 80.0 %all-gather.22.cloned.1.call-done = bf16[1024,2048]{1,0:T(8,128)(2,1)} async-done(((bf16[256,2048]{1,0:T(8,128)(2,1)}), bf16[1024,2048]{1,0:T(8,128)(2,1)}) %all-gather.22.cloned.1.call-update) | async-done | bytes 4194320 | tf_op jit(solution)/shard_map/all_gather | solution.py:136
  539.9 11.8 fusion.56
  551.7 34.9 %all-gather.24.cloned.1.call-done = bf16[2048,1408]{1,0:T(8,128)(2,1)} async-done(((bf16[256,1408]{1,0:T(8,128)(2,1)}), bf16[2048,1408]{1,0:T(8,128)(2,1)}) %all-gather.24.cloned.1.call-update) | async-done | bytes 5767184 | tf_op jit(solution)/shard_map/all_gather | solution.py:88
  586.6 11.7 fusion.55
  598.3 67.5 %all-gather.30.cloned.1.call-done = bf16[1024,2048]{1,0:T(8,128)(2,1)} async-done(((bf16[256,2048]{1,0:T(8,128)(2,1)}), bf16[1024,2048]{1,0:T(8,128)(2,1)}) %all-gather.30.cloned.1.call-update) | async-done | bytes 4194320 | tf_op jit(solution)/shard_map/all_gather | solution.py:148
  665.8 47.7 %all-gather.28.cloned.1.call-done = bf16[1408,2048]{1,0:T(8,128)(2,1)} async-done(((bf16[1408,256]{1,0:T(8,128)(2,1)}), bf16[1408,2048]{1,0:T(8,128)(2,1)}) %all-gather.28.cloned.1.call-update) | async-done | bytes 5767184 | tf_op jit(solution)/shard_map/all_gather | solution.py:91
  713.6 16.6 multiply_convert_fusion.1
  730.2 8.7 fusion.57
  738.9 11.0 convolution_add_fusion
  750.0 143.8 %reduce-scatter.16.cloned.1.call-done = f32[256,2048]{1,0:T(8,128)} async-done(((f32[1024,2048]{1,0:T(8,128)}), f32[256,2048]{1,0:T(8,128)}) %reduce-scatter.16.cloned.1.call-update) | async-done | bytes 2097168 | tf_op jit(solution)/shard_map/reduce_scatter | solution.py:157
  899.0 10.5 convolution_convert_fusion
  911.5 10.8 convolution_convert_fusion.1
  924.2 11.3 convolution_convert_fusion.2
  939.3 39.1 %all-gather.32.cloned.1.call-done = bf16[1024,2048]{1,0:T(8,128)(2,1)} async-done(((bf16[256,2048]{1,0:T(8,128)(2,1)}), bf16[1024,2048]{1,0:T(8,128)(2,1)}) %all-gather.32.cloned.1.call-update) | async-done | bytes 4194320 | tf_op jit(solution)/shard_map/all_gather | solution.py:167
  978.4 6.1 convolution_convert_fusion.4
  989.2 25.4 %multiply_reduce_fusion = (f32[8,1024]{1,0:T(8,128)S(1)}, f32[8,1024,1024]{1,2,0:T(8,128)}) fusion(f32[8,1024,1024]{1,2,0:T(8,128)} %get-tuple-element.91, f32[8,1024]{1,0:T(8,128)S(1)} %log_add_fusion, bf16[8,1024,64]{1,2,0:T(8,128)(2,1)S(1)} %bitcast.116, bf16[1024,64,1]{0,1,2:T(8,128)(2,1)S(1)} %copy-done.20), kind=kOutput, calls=%fused_computation.1 | convolution fusion | flops 1098899456 | bytes 68354048 | tf_op jit(solution)/shard_map/while/body/eval_jaxpr/hqd,kd->hqk/dot_general | solution.py:176
  1014.6 29.2 %multiply_convert_fusion = bf16[8,1024,1024]{1,2,0:T(8,128)(2,1)} fusion(f32[8,1024,1024]{1,2,0:T(8,128)} %get-tuple-element.93, f32[8,1024,1024]{1,2,0:T(8,128)} %get-tuple-element.91, f32[8,1024]{1,0:T(8,128)S(1)} %get-tuple-element.92, f32[8,1024]{1,0:T(8,128)S(1)} %log_add_fusion), kind=kLoop, calls=%fused_computation | loop fusion | flops 33554432 | bytes 83951616 | tf_op jit(solution)/shard_map/while/body/eval_jaxpr/convert_element_type | solution.py:180
  1043.8 10.3 multiply_bitcast_fusion.1
  1056.2 7.9 multiply_bitcast_fusion
  1073.5 7.0 fusion.59
  1080.6 5.7 fusion.58
  1086.2 14.0 fusion.28
  1100.5 10.5 add_convert_fusion
  1111.1 11.0 convolution_convert_fusion.3
  1127.6 6.1 dynamic_update_slice.20
  1140.3 6.1 dynamic_update_slice.19
  1152.7 14.2 reduce-scatter.28.cloned.1.call-done
  1169.3 42.4 %reduce-scatter.26.cloned.1.call-done = bf16[512,256]{1,0:T(8,128)(2,1)} async-done(((bf16[512,2048]{1,0:T(8,128)(2,1)}), bf16[512,256]{1,0:T(8,128)(2,1)}) %reduce-scatter.26.cloned.1.call-update) | async-done | bytes 262160 | tf_op jit(solution)/shard_map/reduce_scatter | solution.py:237
  1213.5 43.2 %reduce-scatter.20.cloned.1.call-done = bf16[256,512]{1,0:T(8,128)(2,1)} async-done(((bf16[2048,512]{1,0:T(8,128)(2,1)}), bf16[256,512]{1,0:T(8,128)(2,1)}) %reduce-scatter.20.cloned.1.call-update) | async-done | bytes 262160 | tf_op jit(solution)/shard_map/reduce_scatter | solution.py:228
  1258.5 76.8 %reduce-scatter.18.cloned.1.call-done = bf16[256,2048]{1,0:T(8,128)(2,1)} async-done(((bf16[1024,2048]{1,0:T(8,128)(2,1)}), bf16[256,2048]{1,0:T(8,128)(2,1)}) %reduce-scatter.18.cloned.1.call-update) | async-done | bytes 1048592 | tf_op jit(solution)/shard_map/reduce_scatter | solution.py:222
  1337.4 46.7 %all-reduce.4 = (f32[2048]{0:T(1024)S(1)}, f32[2048]{0:T(1024)S(1)}) all-reduce(f32[2048]{0:T(1024)S(1)} %get-tuple-element.54, f32[2048]{0:T(1024)S(1)} %copy-done.29), channel_id=6, replica_groups=mesh['dp'=8,'tensor'=4] {'dp','tensor'}, use_global_device_ids=true, to_apply=%region_12.13.clone | all-reduce | flops 4096 | bytes 32768
  1385.3 30.5 %reduce-scatter.14.cloned.1.call-done = bf16[256,2048]{1,0:T(8,128)(2,1)} async-done(((bf16[1024,2048]{1,0:T(8,128)(2,1)}), bf16[256,2048]{1,0:T(8,128)(2,1)}) %reduce-scatter.14.cloned.1.call-update) | async-done | bytes 1048592 | tf_op jit(solution)/shard_map/reduce_scatter | solution.py:144
  1415.7 5.3 fusion.17
  1421.1 123.7 %reduce-scatter.24.cloned.1.call-done = f32[64,256]{1,0:T(8,128)} async-done(((f32[2048,256]{1,0:T(8,128)}), f32[64,256]{1,0:T(8,128)}) %reduce-scatter.24.cloned.1.call-update) | async-done | bytes 65552 | tf_op jit(solution)/shard_map/reduce_scatter | solution.py:246
  1544.8 139.2 %reduce-scatter.22.cloned.1.call-done = f32[64,256]{1,0:T(8,128)} async-done(((f32[2048,256]{1,0:T(8,128)}), f32[64,256]{1,0:T(8,128)}) %reduce-scatter.22.cloned.1.call-update) | async-done | bytes 65552 | tf_op jit(solution)/shard_map/reduce_scatter | solution.py:245
  (179 shorter events, 82.4 us)
Async XLA Ops:
  7.2 58.0 %all-gather.16.cloned.1.call-start = ((), (), s32[]{:S(2)}) async-start(), calls=%async_computation.13 | async-start | bytes 1081344 | tf_op jit(solution)/shard_map/all_gather | solution.py:81
  7.9 137.3 %all-gather.12.cloned.1.call-start = ((), (), s32[]{:S(2)}) async-start(), calls=%async_computation.11 | async-start | bytes 5242880 | tf_op jit(solution)/shard_map/all_gather | solution.py:102
  53.2 123.3 %all-gather.14.cloned.1.call-start = ((), (), s32[]{:S(2)}) async-start(), calls=%async_computation.12 | async-start | bytes 2359296 | tf_op jit(solution)/shard_map/all_gather | solution.py:87
  53.9 178.1 %all-gather.18.cloned.1.call-start = ((), (), s32[]{:S(2)}) async-start(), calls=%async_computation.14 | async-start | bytes 1081344 | tf_op jit(solution)/shard_map/all_gather | solution.py:82
  54.5 207.5 %all-gather.20.cloned.1.call-start = ((), (), s32[]{:S(2)}) async-start(), calls=%async_computation.15 | async-start | bytes 2359296 | tf_op jit(solution)/shard_map/all_gather | solution.py:90
  55.1 358.1 %reduce-scatter.12.cloned.1.call-start = ((), (), s32[]{:S(2)}) async-start(), calls=%async_computation.16 | async-start | bytes 10485760 | tf_op jit(solution)/shard_map/reduce_scatter | solution.py:132
  56.7 125.0 %copy-start.14 = (f32[1024,32]{0,1:T(8,128)}, f32[1024,32]{0,1:T(8,128)S(1)}, u32[]{:S(2)}) copy-start(f32[1024,32]{0,1:T(8,128)S(1)} %get-tuple-element.89) | copy-start | bytes 393220
  149.5 32.6 %copy-start.23 = (bf16[1024,32]{0,1:T(8,128)(2,1)}, bf16[1024,32]{0,1:T(8,128)(2,1)S(1)}, u32[]{:S(2)}) copy-start(bf16[1024,32]{0,1:T(8,128)(2,1)S(1)} %get-tuple-element.83) | copy-start | bytes 196612
  149.5 32.6 %copy-start.24 = (bf16[1024,32]{0,1:T(8,128)(2,1)}, bf16[1024,32]{0,1:T(8,128)(2,1)S(1)}, u32[]{:S(2)}) copy-start(bf16[1024,32]{0,1:T(8,128)(2,1)S(1)} %get-tuple-element.84) | copy-start | bytes 196612
  182.1 14.2 copy-start.21
  182.1 14.2 copy-start.22
  250.5 18.8 %copy-start.39 = (bf16[8,1024,64]{1,2,0:T(8,128)(2,1)}, bf16[8,1024,64]{1,2,0:T(8,128)(2,1)S(1)}, u32[]{:S(2)}) copy-start(bf16[8,1024,64]{1,2,0:T(8,128)(2,1)S(1)} %fusion.31) | copy-start | bytes 3145732
  269.2 143.9 %copy-start.4 = (bf16[256,2048]{1,0:T(8,128)(2,1)S(1)}, bf16[256,2048]{1,0:T(8,128)(2,1)}, u32[]{:S(2)}) copy-start(bf16[256,2048]{1,0:T(8,128)(2,1)} %param.11) | copy-start | bytes 3145732
  269.3 190.6 %all-gather.26.cloned.1.call-start = ((), (), s32[]{:S(2)}) async-start(), calls=%async_computation.19 | async-start | bytes 6488064 | tf_op jit(solution)/shard_map/all_gather | solution.py:89
  270.0 269.8 %all-gather.22.cloned.1.call-start = ((), (), s32[]{:S(2)}) async-start(), calls=%async_computation.17 | async-start | bytes 5242880 | tf_op jit(solution)/shard_map/all_gather | solution.py:136
  270.1 626.7 %copy-start.25 = (f32[2048]{0:T(1024)}, f32[2048]{0:T(1024)S(1)}, u32[]{:S(2)}) copy-start(f32[2048]{0:T(1024)S(1)} %convert_element_type.135) | copy-start | bytes 24580
  415.1 481.6 %copy-start.1 = (f32[256,2048]{1,0:T(8,128)}, f32[256,2048]{1,0:T(8,128)S(1)}, u32[]{:S(2)}) copy-start(f32[256,2048]{1,0:T(8,128)S(1)} %get-tuple-element.71) | copy-start | bytes 6291460
  415.1 481.6 %copy-start.30 = (f32[256]{0:T(256)}, f32[256]{0:T(256)S(1)}, u32[]{:S(2)}) copy-start(f32[256]{0:T(256)S(1)} %add_rsqrt_fusion) | copy-start | bytes 3076
  416.6 170.0 %all-gather.24.cloned.1.call-start = ((), (), s32[]{:S(2)}) async-start(), calls=%async_computation.18 | async-start | bytes 6488064 | tf_op jit(solution)/shard_map/all_gather | solution.py:88
  417.3 248.5 %all-gather.30.cloned.1.call-start = ((), (), s32[]{:S(2)}) async-start(), calls=%async_computation.22 | async-start | bytes 5242880 | tf_op jit(solution)/shard_map/all_gather | solution.py:148
  417.9 295.7 %all-gather.28.cloned.1.call-start = ((), (), s32[]{:S(2)}) async-start(), calls=%async_computation.20 | async-start | bytes 6488064 | tf_op jit(solution)/shard_map/all_gather | solution.py:91
  418.6 475.2 %reduce-scatter.16.cloned.1.call-start = ((), (), s32[]{:S(2)}) async-start(), calls=%async_computation.23 | async-start | bytes 10485760 | tf_op jit(solution)/shard_map/reduce_scatter | solution.py:157
  713.6 16.6 copy-start.36
  730.2 8.7 copy-start.40
  750.0 147.3 %copy-start.7 = (bf16[256,2048]{1,0:T(8,128)(2,1)S(1)}, bf16[256,2048]{1,0:T(8,128)(2,1)}, u32[]{:S(2)}) copy-start(bf16[256,2048]{1,0:T(8,128)(2,1)} %param.21) | copy-start | bytes 3145732
  750.0 228.4 %all-gather.32.cloned.1.call-start = ((), (), s32[]{:S(2)}) async-start(), calls=%async_computation.24 | async-start | bytes 5242880 | tf_op jit(solution)/shard_map/all_gather | solution.py:167
  898.9 248.9 %reduce-scatter.32.cloned.1.call-start = ((), (), s32[]{:S(2)}) async-start(), calls=%async_computation.32 | async-start | bytes 6488064 | tf_op jit(solution)/shard_map/reduce_scatter | solution.py:240
  909.5 240.8 %reduce-scatter.30.cloned.1.call-start = ((), (), s32[]{:S(2)}) async-start(), calls=%async_computation.31 | async-start | bytes 6488064 | tf_op jit(solution)/shard_map/reduce_scatter | solution.py:234
  922.4 244.6 %reduce-scatter.28.cloned.1.call-start = ((), (), s32[]{:S(2)}) async-start(), calls=%async_computation.30 | async-start | bytes 6488064 | tf_op jit(solution)/shard_map/reduce_scatter | solution.py:231
  935.6 276.1 %reduce-scatter.26.cloned.1.call-start = ((), (), s32[]{:S(2)}) async-start(), calls=%async_computation.29 | async-start | bytes 2359296 | tf_op jit(solution)/shard_map/reduce_scatter | solution.py:237
  939.3 75.3 %copy-start.10 = (f32[8,1024]{1,0:T(8,128)}, f32[8,1024]{1,0:T(8,128)S(1)}, u32[]{:S(2)}) copy-start(f32[8,1024]{1,0:T(8,128)S(1)} %log_add_fusion) | copy-start | bytes 98308
  939.3 45.4 %copy-start.38 = (bf16[512,2048]{1,0:T(8,128)(2,1)S(1)}, bf16[512,2048]{1,0:T(8,128)(2,1)}, u32[]{:S(2)}) copy-start(bf16[512,2048]{1,0:T(8,128)(2,1)} %all-gather.20.cloned.1.call-done) | copy-start | bytes 6291460
  984.6 272.1 %reduce-scatter.20.cloned.1.call-start = ((), (), s32[]{:S(2)}) async-start(), calls=%async_computation.26 | async-start | bytes 2359296 | tf_op jit(solution)/shard_map/reduce_scatter | solution.py:228
  1043.8 12.4 copy-start
  1073.0 262.3 %reduce-scatter.18.cloned.1.call-start = ((), (), s32[]{:S(2)}) async-start(), calls=%async_computation.25 | async-start | bytes 5242880 | tf_op jit(solution)/shard_map/reduce_scatter | solution.py:222
  1073.5 7.1 copy-start.37
  1086.2 14.0 copy-start.17
  1111.0 304.7 %reduce-scatter.14.cloned.1.call-start = ((), (), s32[]{:S(2)}) async-start(), calls=%async_computation.21 | async-start | bytes 5242880 | tf_op jit(solution)/shard_map/reduce_scatter | solution.py:144
  1122.1 422.7 %reduce-scatter.24.cloned.1.call-start = ((), (), s32[]{:S(2)}) async-start(), calls=%async_computation.28 | async-start | bytes 2162688 | tf_op jit(solution)/shard_map/reduce_scatter | solution.py:246
  1135.0 549.0 %reduce-scatter.22.cloned.1.call-start = ((), (), s32[]{:S(2)}) async-start(), calls=%async_computation.27 | async-start | bytes 2162688 | tf_op jit(solution)/shard_map/reduce_scatter | solution.py:245
  1147.8 187.5 %copy-start.5 = (bf16[256,2048]{1,0:T(8,128)(2,1)S(1)}, bf16[256,2048]{1,0:T(8,128)(2,1)}, u32[]{:S(2)}) copy-start(bf16[256,2048]{1,0:T(8,128)(2,1)} %param.11) | copy-start | bytes 3145732
  1147.8 187.5 %copy-start.28 = (f32[2048]{0:T(1024)S(1)}, f32[2048]{0:T(1024)}, u32[]{:S(2)}) copy-start(f32[2048]{0:T(1024)} %copy-done.27) | copy-start | bytes 24580
  1147.8 187.5 %copy-start.33 = (f32[256]{0:T(256)S(1)}, f32[256]{0:T(256)}, u32[]{:S(2)}) copy-start(f32[256]{0:T(256)} %copy-done.32) | copy-start | bytes 3076
  1150.2 187.1 %copy-start.29 = (f32[2048]{0:T(1024)S(1)}, f32[2048]{0:T(1024)}, u32[]{:S(2)}) copy-start(f32[2048]{0:T(1024)} %get-tuple-element.52) | copy-start | bytes 24580
  1150.2 265.5 %copy-start.2 = (f32[256,2048]{1,0:T(8,128)S(1)}, f32[256,2048]{1,0:T(8,128)}, u32[]{:S(2)}) copy-start(f32[256,2048]{1,0:T(8,128)} %copy-done.1) | copy-start | bytes 6291460
  1150.3 265.5 %copy-start.26 = (f32[2048]{0:T(1024)S(1)}, f32[2048]{0:T(1024)}, u32[]{:S(2)}) copy-start(f32[2048]{0:T(1024)} %copy-done.25) | copy-start | bytes 24580
  1150.3 265.5 %copy-start.31 = (f32[256]{0:T(256)S(1)}, f32[256]{0:T(256)}, u32[]{:S(2)}) copy-start(f32[256]{0:T(256)} %copy-done.30) | copy-start | bytes 3076
  1150.3 265.5 %copy-start.35 = (f32[256]{0:T(256)S(1)}, f32[256]{0:T(256)}, u32[]{:S(2)}) copy-start(f32[256]{0:T(256)} %copy-done.34) | copy-start | bytes 3076
  (17 other events, 38.3 us)
Sparse Core Ops, SparseCore 0:
  11.0 54.1 all-gather.15
  67.3 77.8 all-gather.11
  147.1 29.3 all-gather.13
  179.3 52.7 all-gather.17
  233.8 28.1 all-gather.19
  269.4 143.7 reduce-scatter.11
  415.0 44.7 all-gather.25
  462.0 77.8 all-gather.21
  541.7 44.7 all-gather.23
  588.0 77.8 all-gather.29
  667.7 45.8 all-gather.27
  750.1 143.7 reduce-scatter.15
  899.1 79.3 all-gather.31
  981.7 60.0 reduce-scatter.31
  1045.5 59.0 reduce-scatter.29
  1107.9 59.0 reduce-scatter.27
  1170.5 41.1 reduce-scatter.25
  1215.4 41.1 reduce-scatter.19
  1259.0 76.2 reduce-scatter.17
  1337.5 78.2 reduce-scatter.13
  1418.7 126.0 reduce-scatter.23
  1547.6 136.3 reduce-scatter.21
where the time goes:
time: 1710 us; the launch traced here: 1690 us
  waiting for transfers between devices  1220 us (71%)
  matrix products  257 us (15%)
  blocking collectives  85.6 us (5%)
  other arithmetic  79 us (5%)
  local copies, waits for them, and re-layouts  31.1 us (2%)
    reduce_scatter x1, waiting for transfers between devices, on_device(): lax.psum_scatter(product_right(grad_gate_pre, gate_full) + product_right(...  144 us
    reduce_scatter x1, waiting for transfers between devices, on_device(): lax.psum_scatter(attn_part, 'tensor', scatter_dimension=0, tiled=True)  143 us
    reduce_scatter x1, waiting for transfers between devices, on_device(): lax.psum_scatter(grad_key_w, ('dp', 'tensor'), scatter_dimension=0, tiled...  139 us
    reduce_scatter x1, waiting for transfers between devices, on_device(): lax.psum_scatter(grad_value_w, ('dp', 'tensor'), scatter_dimension=0, til...  124 us
    unnamed x2, blocking collectives  85.6 us
    all_gather x1, waiting for transfers between devices, on_device(): lax.all_gather((unit_second * gain_second).astype(jnp.bfloat16), 'tensor'...  80 us
    all_gather x1, waiting for transfers between devices, on_device(): lax.all_gather((unit_first * gain_first).astype(jnp.bfloat16), 'tensor',...  80 us
    reduce_scatter x1, waiting for transfers between devices, on_device(): lax.psum_scatter(back_first.astype(jnp.bfloat16), 'tensor', scatter_dimen...  76.8 us
  transfers between devices with their start and end apart: 22, of which 20 were waited for; matrix products, arithmetic and copies ran while one was open for 18% of the time, Pallas kernels for 0%

commit v1 on v0

v1 whole, which is shorter than its diff:
```python
import functools

import jax
import jax.numpy as jnp
from jax import lax
from jax.experimental import pallas as pl
from jax.experimental.pallas import tpu as pltpu
from jax.sharding import PartitionSpec as P

HEAD_DIM = 64
SEQLEN = 1024
MESH = pl.DeviceIdType.MESH
ANY = pl.BlockSpec(memory_space=pl.ANY)
VMEM = pl.BlockSpec(memory_space=pltpu.VMEM)
VMEM_LIMIT = 56 * 2**20

epsilon = 1e-05
theta_base = 10000.0


def product(left, right):
    return jnp.dot(left, right, preferred_element_type=jnp.float32)


def product_left(left, right):
    return lax.dot_general(
        left, right, (((0,), (0,)), ((), ())), preferred_element_type=jnp.float32
    )


def product_right(left, right):
    return lax.dot_general(
        left, right, (((1,), (1,)), ((), ())), preferred_element_type=jnp.float32
    )


def norm_back(grad_normed, unit_rows, scale_rows, gain):
    scaled_grad = grad_normed * gain
    return scale_rows * (
        scaled_grad - unit_rows * jnp.mean(scaled_grad * unit_rows, axis=-1, keepdims=True)
    )


def flip(index, bit):
    size = 1 << bit
    return index + size * (1 - 2 * lax.rem(lax.div(index, size), 2))


def masked(index, bits, rank):
    for place, bit in enumerate(bits):
        if rank >> place & 1:
            index = flip(index, bit)
    return index


def orders(bit_count, core_last):
    up = list(range(1, bit_count))
    down = up[::-1]
    return [up + [0], down + [0]] if core_last else [[0] + up, [0] + down]


def greet(spots, near, all_tensor, dp_bits):
    dp, tensor, tensor_size = spots
    barrier = pltpu.get_barrier_semaphore()

    def signal(where):
        pl.semaphore_signal(barrier, inc=1, device_id=where, device_id_type=MESH)

    peers = dp_bits
    for bit in range(dp_bits):
        signal((flip(dp, bit), tensor))
    if all_tensor:
        peers += tensor_size - 1
        for other in range(tensor_size):
            pl.when(other != tensor)(functools.partial(signal, (dp, other)))
    elif near:
        below, above = tensor > 0, tensor + 1 < tensor_size
        pl.when(below)(functools.partial(signal, (dp, tensor - 1)))
        pl.when(above)(functools.partial(signal, (dp, tensor + 1)))
        peers = peers + below.astype(jnp.int32) + above.astype(jnp.int32)
    pl.semaphore_wait(barrier, peers)


class Gather:
    def __init__(self, shape, slot, half=None):
        self.shape, self.slot, self.half = shape, slot, half


def gather_kernel(specs, dp_size, tensor_size, *refs):
    count = len(specs)
    sources, outs = refs[:count], refs[count : 2 * count]
    own_sem, z_send, z_recv, h_send, h_recv = refs[2 * count :]
    dp, tensor = lax.axis_index("dp"), lax.axis_index("tensor")
    dp_bits = dp_size.bit_length() - 1
    hyper = [i for i in range(count) if specs[i].half is not None]
    greet((dp, tensor, tensor_size), True, False, dp_bits if hyper else 0)

    def z_copy(i, block, way, source=None):
        slot = specs[i].slot(outs[i], dp, block)
        return pltpu.make_async_remote_copy(
            src_ref=slot if source is None else source,
            dst_ref=slot,
            send_sem=z_send.at[i, way, block],
            recv_sem=z_recv.at[i, block],
            device_id=(dp, tensor + 1 if way == 0 else tensor - 1),
            device_id_type=MESH,
        )

    can = [tensor + 1 < tensor_size, tensor > 0]
    for i in range(count):
        for way in (0, 1):

            @pl.when(can[way])
            def _():
                z_copy(i, tensor, way, sources[i]).start()

    owns = [
        pltpu.make_async_copy(sources[i], specs[i].slot(outs[i], dp, tensor), own_sem.at[i])
        for i in range(count)
    ]
    for own in owns:
        own.start()
    for step in range(1, tensor_size):
        for i in range(count):
            for way, block in ((0, tensor - step), (1, tensor + step)):

                @pl.when((block >= 0) & (block < tensor_size))
                def _():
                    z_copy(i, block, way).wait_recv()

                    @pl.when(can[way])
                    def _():
                        z_copy(i, block, way).start()

    for own in owns:
        own.wait()

    order = orders(dp_bits, True)

    def h_copy(n, half, rank, place):
        spec, out = specs[hyper[n]], outs[hyper[n]]
        bits = order[half]
        part = spec.half(out, masked(dp, bits, rank), half)
        return pltpu.make_async_remote_copy(
            src_ref=part,
            dst_ref=part,
            send_sem=h_send.at[n, half, rank, place],
            recv_sem=h_recv.at[n, half, rank | 1 << place],
            device_id=(flip(dp, bits[place]), tensor),
            device_id_type=MESH,
        )

    if hyper:
        for rank in range(1 << dp_bits):
            top = rank.bit_length()
            for n in range(len(hyper)):
                for half in (0, 1):
                    if rank:
                        wait_part(
                            specs[hyper[n]].half(
                                outs[hyper[n]], masked(dp, order[half], rank), half
                            ),
                            h_recv.at[n, half, rank],
                            h_send.at[n, half, 0, 0],
                            (flip(dp, 0), tensor),
                        )
                    for place in range(top, dp_bits):
                        h_copy(n, half, rank, place).start()
        for rank in range(1 << dp_bits):
            for n in range(len(hyper)):
                for half in (0, 1):
                    for place in range(rank.bit_length(), dp_bits):
                        h_copy(n, half, rank, place).wait_send()
    for i in range(count):
        for block in range(tensor_size):
            for way in (0, 1):
                sent = can[way] & ((block <= tensor) if way == 0 else (block >= tensor))

                @pl.when(sent)
                def _():
                    z_copy(i, block, way).wait_send()


def wait_part(part, recv_sem, send_sem, device):
    pltpu.make_async_remote_copy(
        src_ref=part,
        dst_ref=part,
        send_sem=send_sem,
        recv_sem=recv_sem,
        device_id=device,
        device_id_type=MESH,
    ).wait_recv()


def gather(specs, arrays, dp_size, tensor_size, collective_id):
    count = len(specs)
    hyper = max(1, sum(spec.half is not None for spec in specs))
    dp_bits = dp_size.bit_length() - 1
    return pl.pallas_call(
        functools.partial(gather_kernel, specs, dp_size, tensor_size),
        out_shape=[
            jax.ShapeDtypeStruct(spec.shape, array.dtype) for spec, array in zip(specs, arrays)
        ],
        in_specs=[ANY] * count,
        out_specs=[ANY] * count,
        scratch_shapes=[
            pltpu.SemaphoreType.DMA((count,)),
            pltpu.SemaphoreType.DMA((count, 2, tensor_size)),
            pltpu.SemaphoreType.DMA((count, tensor_size)),
            pltpu.SemaphoreType.DMA((hyper, 2, dp_size, max(dp_bits, 1))),
            pltpu.SemaphoreType.DMA((hyper, 2, dp_size)),
        ],
        compiler_params=pltpu.CompilerParams(
            collective_id=collective_id, has_side_effects=True
        ),
    )(*arrays)


def exchange_kernel(tensor_size, source, out, own_sem, send, recv):
    dp, tensor = lax.axis_index("dp"), lax.axis_index("tensor")
    greet((dp, tensor, tensor_size), False, True, 0)
    own = pltpu.make_async_copy(source.at[tensor], out.at[tensor], own_sem)

    def copy(other, slot):
        return pltpu.make_async_remote_copy(
            src_ref=source.at[other],
            dst_ref=out.at[slot],
            send_sem=send.at[other],
            recv_sem=recv.at[slot],
            device_id=(dp, other),
            device_id_type=MESH,
        )

    for other in range(tensor_size):

        @pl.when(other != tensor)
        def _():
            copy(other, tensor).start()

    own.start()
    own.wait()
    for other in range(tensor_size):

        @pl.when(other != tensor)
        def _():
            copy(other, tensor).wait_send()
            copy(other, other).wait_recv()


def exchange(blocks, tensor_size, collective_id):
    return pl.pallas_call(
        functools.partial(exchange_kernel, tensor_size),
        out_shape=jax.ShapeDtypeStruct(blocks.shape, blocks.dtype),
        in_specs=[ANY],
        out_specs=ANY,
        scratch_shapes=[
            pltpu.SemaphoreType.DMA,
            pltpu.SemaphoreType.DMA((tensor_size,)),
            pltpu.SemaphoreType.DMA((tensor_size,)),
        ],
        compiler_params=pltpu.CompilerParams(
            collective_id=collective_id, has_side_effects=True
        ),
    )(blocks)


class Scatter:
    def __init__(self, shape, part, part_shape, place, cut=None, cut_shape=None):
        self.shape, self.part, self.part_shape, self.place = shape, part, part_shape, place
        self.cut, self.cut_shape = cut, cut_shape


def add_into(total, extra):
    shape = total.shape
    rows = shape[-2]
    slab = min(16, rows)
    if len(shape) == 2:

        def body(step, carry):
            at = pl.ds(pl.multiple_of(step * slab, slab), slab)
            total[at, :] = (
                total[at, :].astype(jnp.float32) + extra[at, :].astype(jnp.float32)
            ).astype(total.dtype)
            return carry

        lax.fori_loop(0, rows // slab, body, 0, unroll=2 if (rows // slab) % 2 == 0 else 1)
    else:
        for lead in range(shape[0]):
            add_into(total.at[lead], extra.at[lead])


def scatter_kernel(specs, dp_size, tensor_size, *refs):
    count = len(specs)
    refs = list(refs)
    sources = [refs.pop(0) for _ in specs]
    outs = [refs.pop(0) for _ in specs]
    dp_bits = dp_size.bit_length() - 1
    total = [refs.pop(0) for _ in specs]
    landing = [[refs.pop(0) for _ in range(dp_bits)] for _ in specs]
    shares = [refs.pop(0) if spec.cut is not None else None for spec in specs]
    own_sem, send, recv, z_send, z_recv = refs
    dp, tensor = lax.axis_index("dp"), lax.axis_index("tensor")
    cuts = any(spec.cut is not None for spec in specs)
    greet((dp, tensor, tensor_size), False, cuts, dp_bits)
    order = orders(dp_bits, False)

    def own_copy(i, half, slot):
        return pltpu.make_async_copy(
            specs[i].part(sources[i], masked(dp, order[half], 2 * slot), half),
            total[i].at[half, slot],
            own_sem.at[i, half, slot],
        )

    def copy(i, half, stage, slot):
        if stage == 0:
            source = specs[i].part(sources[i], masked(dp, order[half], 2 * slot + 1), half)
        else:
            source = total[i].at[half, (2 * slot + 1) << (stage - 1)]
        return pltpu.make_async_remote_copy(
            src_ref=source,
            dst_ref=landing[i][stage].at[half, slot],
            send_sem=send.at[i, half, stage, slot],
            recv_sem=recv.at[i, half, stage, slot],
            device_id=(flip(dp, order[half][stage]), tensor),
            device_id_type=MESH,
        )

    def slots(stage):
        return range(1 << (dp_bits - 1 - stage))

    for i in range(count):
        for slot in slots(0):
            for half in (0, 1):
                copy(i, half, 0, slot).start()
                own_copy(i, half, slot).start()
    for stage in range(dp_bits):
        for i in range(count):
            for slot in sorted(slots(stage), key=lambda s: -(s & 1)):
                for half in (0, 1):
                    if stage == 0:
                        own_copy(i, half, slot).wait()
                    copy(i, half, stage, slot).wait_recv()
                    add_into(total[i].at[half, slot << stage], landing[i][stage].at[half, slot])
                    if slot & 1:
                        copy(i, half, stage + 1, slot >> 1).start()

    def z_copy(i, half, other, slot):
        return pltpu.make_async_remote_copy(
            src_ref=specs[i].cut(total[i].at[half, 0], other),
            dst_ref=shares[i].at[slot, half],
            send_sem=z_send.at[i, half, other],
            recv_sem=z_recv.at[i, half, slot],
            device_id=(dp, other),
            device_id_type=MESH,
        )

    for i in range(count):
        for half in (0, 1):
            if specs[i].cut is None:
                specs[i].place(outs[i], half)[...] = total[i][half, 0].astype(jnp.float32)
            else:
                for other in range(tensor_size):

                    @pl.when(other != tensor)
                    def _():
                        z_copy(i, half, other, tensor).start()

                    @pl.when(other == tensor)
                    def _():
                        shares[i][other, half] = specs[i].cut(total[i].at[half, 0], other)[...]

    for i in range(count):
        if specs[i].cut is None:
            continue
        for half in (0, 1):
            for other in range(tensor_size):

                @pl.when(other != tensor)
                def _():
                    z_copy(i, half, other, other).wait_recv()

            summed = shares[i][0, half].astype(jnp.float32)
            for other in range(1, tensor_size):
                summed = summed + shares[i][other, half].astype(jnp.float32)
            specs[i].place(outs[i], half)[...] = summed
    for i in range(count):
        for half in (0, 1):
            for stage in range(dp_bits):
                for slot in slots(stage):
                    copy(i, half, stage, slot).wait_send()
            if specs[i].cut is not None:
                for other in range(tensor_size):

                    @pl.when(other != tensor)
                    def _():
                        z_copy(i, half, other, tensor).wait_send()


def scatter(specs, arrays, dp_size, tensor_size, collective_id):
    count = len(specs)
    dp_bits = dp_size.bit_length() - 1
    scratch = []
    for spec, array in zip(specs, arrays):
        scratch.append(pltpu.VMEM((2, dp_size // 2) + spec.part_shape, array.dtype))
    for spec, array in zip(specs, arrays):
        for stage in range(dp_bits):
            scratch.append(pltpu.VMEM((2, dp_size >> (stage + 1)) + spec.part_shape, array.dtype))
    for spec, array in zip(specs, arrays):
        if spec.cut is not None:
            scratch.append(pltpu.VMEM((tensor_size, 2) + spec.cut_shape, array.dtype))
    return pl.pallas_call(
        functools.partial(scatter_kernel, specs, dp_size, tensor_size),
        out_shape=[jax.ShapeDtypeStruct(spec.shape, jnp.float32) for spec in specs],
        in_specs=[ANY] * count,
        out_specs=[VMEM] * count,
        scratch_shapes=scratch
        + [
            pltpu.SemaphoreType.DMA((count, 2, dp_size // 2)),
            pltpu.SemaphoreType.DMA((count, 2, dp_bits, dp_size // 2)),
            pltpu.SemaphoreType.DMA((count, 2, dp_bits, dp_size // 2)),
            pltpu.SemaphoreType.DMA((count, 2, tensor_size)),
            pltpu.SemaphoreType.DMA((count, 2, tensor_size)),
        ],
        compiler_params=pltpu.CompilerParams(
            collective_id=collective_id, has_side_effects=True, vmem_limit_bytes=VMEM_LIMIT
        ),
    )(*arrays)


def lanes_of(shape):
    return lax.broadcasted_iota(jnp.int32, shape, len(shape) - 1)


def swap_halves(values):
    width = values.shape[-1]
    first = lanes_of(values.shape) % HEAD_DIM < HEAD_DIM // 2
    return jnp.where(
        first,
        pltpu.roll(values, width - HEAD_DIM // 2, 1),
        pltpu.roll(values, HEAD_DIM // 2, 1),
    )


def left_head(block, odd):
    moved = jnp.where(odd, pltpu.roll(block, HEAD_DIM, 1), block)
    return jnp.where(lanes_of(block.shape) < HEAD_DIM, moved, jnp.zeros_like(moved))


def allowed(keys, rows, start):
    key_at = lax.broadcasted_iota(jnp.int32, (keys, rows), 0)
    query_at = lax.broadcasted_iota(jnp.int32, (keys, rows), 1) + start
    return key_at <= query_at


def attend_kernel(
    group_pairs, q_ref, cos_ref, sin_ref, k_ref, v_ref, o_ref, q_out, lse_ref, k_left, v_turned
):
    pair = pl.program_id(0)
    group = pair // group_pairs
    rows = q_ref.shape[0]
    start = lax.axis_index("tensor") * rows

    @pl.when(pair % group_pairs == 0)
    def _():
        odd = group % 2 == 1
        k_left[...] = left_head(k_ref[...].astype(jnp.float32), odd).astype(jnp.bfloat16)
        v_turned[...] = left_head(v_ref[...].astype(jnp.float32), odd).T[:HEAD_DIM].astype(
            jnp.bfloat16
        )

    raw = q_ref[...]
    turned = (raw * cos_ref[...] + swap_halves(raw) * sin_ref[...]).astype(jnp.bfloat16)
    turned = turned.astype(jnp.float32) * HEAD_DIM ** (-0.5)
    q_out[...] = turned.astype(jnp.bfloat16)
    open_at = allowed(k_left.shape[0], rows, start)
    contexts = []
    for head in (0, 1):
        queries = (turned if head == 0 else pltpu.roll(turned, HEAD_DIM, 1)).astype(jnp.bfloat16)
        scores = product_right(k_left[...], queries)
        scores = jnp.where(open_at, scores, -1e30)
        top = jnp.max(scores, axis=0, keepdims=True)
        exponent = jnp.exp(scores - top)
        summed = jnp.sum(exponent, axis=0, keepdims=True)
        context = product(v_turned[...], exponent.astype(jnp.bfloat16))
        contexts.append(context * (1.0 / summed))
        lse_ref[0, head, :] = (top + jnp.log(summed))[0]
    o_ref[...] = jnp.concatenate(contexts, axis=0).T.astype(jnp.bfloat16)


def attend(q_pre, cosines, sines, keys_values, head_count, group_heads):
    rows, width = q_pre.shape
    length, both = keys_values.shape
    pairs, group_pairs = head_count // 2, group_heads // 2
    kv_blocks = both // 256
    wide = pl.BlockSpec((rows, 128), lambda p: (0, p))
    table = pl.BlockSpec((rows, 128), lambda p: (0, 0))
    return pl.pallas_call(
        functools.partial(attend_kernel, group_pairs),
        grid=(pairs,),
        out_shape=[
            jax.ShapeDtypeStruct((rows, width), jnp.bfloat16),
            jax.ShapeDtypeStruct((rows, width), jnp.bfloat16),
            jax.ShapeDtypeStruct((pairs, 2, rows), jnp.float32),
        ],
        in_specs=[
            wide,
            table,
            table,
            pl.BlockSpec((length, 128), lambda p: (0, p // group_pairs // 2)),
            pl.BlockSpec((length, 128), lambda p: (0, kv_blocks + p // group_pairs // 2)),
        ],
        out_specs=[wide, wide, pl.BlockSpec((1, 2, rows), lambda p: (p, 0, 0))],
        scratch_shapes=[
            pltpu.VMEM((length, 128), jnp.bfloat16),
            pltpu.VMEM((HEAD_DIM, length), jnp.bfloat16),
        ],
        compiler_params=pltpu.CompilerParams(vmem_limit_bytes=VMEM_LIMIT),
        cost_estimate=pl.CostEstimate(
            flops=4 * rows * length * width, bytes_accessed=8 * rows * width, transcendentals=0
        ),
    )(q_pre, cosines, sines, keys_values, keys_values)


def attend_back_kernel(
    group_pairs,
    q_ref,
    do_ref,
    lse_ref,
    cos_ref,
    sin_ref,
    k_ref,
    v_ref,
    dq_ref,
    dk_ref,
    dv_ref,
    k_left,
    v_left,
    k_turned,
    dk_sum,
    dv_sum,
):
    pair = pl.program_id(0)
    group = pair // group_pairs
    odd = group % 2 == 1
    rows = q_ref.shape[0]
    start = lax.axis_index("tensor") * rows

    @pl.when(pair % group_pairs == 0)
    def _():
        left = left_head(k_ref[...].astype(jnp.float32), odd)
        k_left[...] = left.astype(jnp.bfloat16)
        k_turned[...] = left.T[:HEAD_DIM].astype(jnp.bfloat16)
        v_left[...] = left_head(v_ref[...].astype(jnp.float32), odd).astype(jnp.bfloat16)
        dk_sum[...] = jnp.zeros_like(dk_sum)
        dv_sum[...] = jnp.zeros_like(dv_sum)

    open_at = allowed(k_left.shape[0], rows, start)
    grads = []
    for head in (0, 1):
        queries, grad_out = q_ref[...], do_ref[...]
        if head == 1:
            queries = pltpu.roll(queries.astype(jnp.float32), HEAD_DIM, 1).astype(jnp.bfloat16)
            grad_out = pltpu.roll(grad_out.astype(jnp.float32), HEAD_DIM, 1).astype(jnp.bfloat16)
        scores = product_right(k_left[...], queries)
        scores = jnp.where(open_at, scores, -1e30)
        softmaxed = jnp.exp(scores - lse_ref[0, head, :][None, :])
        grad_soft = product_right(v_left[...], grad_out)
        mixed = softmaxed * grad_soft
        mixed_sum = jnp.sum(mixed, axis=0, keepdims=True)
        grad_scores = (mixed - softmaxed * mixed_sum).astype(jnp.bfloat16)
        dv_sum[...] += product(softmaxed.astype(jnp.bfloat16), grad_out)
        dk_sum[...] += product(grad_scores, queries)
        grads.append(product(k_turned[...], grad_scores))
    grad_q = jnp.concatenate(grads, axis=0).T * HEAD_DIM ** (-0.5)
    dq_ref[...] = (grad_q * cos_ref[...] - swap_halves(grad_q) * sin_ref[...]).astype(jnp.bfloat16)

    @pl.when(pair % group_pairs == group_pairs - 1)
    def _():
        for total, out in ((dk_sum, dk_ref), (dv_sum, dv_ref)):
            value = total[...]
            left = lanes_of(value.shape) < HEAD_DIM

            @pl.when(jnp.logical_not(odd))
            def _():
                out[...] = jnp.where(left, value, 0.0).astype(out.dtype)

            @pl.when(odd)
            def _():
                out[...] = jnp.where(
                    left, out[...].astype(jnp.float32), pltpu.roll(value, HEAD_DIM, 1)
                ).astype(out.dtype)


def attend_back(queries, grad_context, lse, cosines, sines, keys_values, head_count, group_heads):
    rows, width = queries.shape
    length, both = keys_values.shape
    pairs, group_pairs = head_count // 2, group_heads // 2
    kv_blocks = both // 256
    wide = pl.BlockSpec((rows, 128), lambda p: (0, p))
    table = pl.BlockSpec((rows, 128), lambda p: (0, 0))
    kv_out = pl.BlockSpec((length, 128), lambda p: (0, p // group_pairs // 2))
    return pl.pallas_call(
        functools.partial(attend_back_kernel, group_pairs),
        grid=(pairs,),
        out_shape=[
            jax.ShapeDtypeStruct((rows, width), jnp.bfloat16),
            jax.ShapeDtypeStruct((length, both // 2), jnp.bfloat16),
            jax.ShapeDtypeStruct((length, both // 2), jnp.bfloat16),
        ],
        in_specs=[
            wide,
            wide,
            pl.BlockSpec((1, 2, rows), lambda p: (p, 0, 0)),
            table,
            table,
            pl.BlockSpec((length, 128), lambda p: (0, p // group_pairs // 2)),
            pl.BlockSpec((length, 128), lambda p: (0, kv_blocks + p // group_pairs // 2)),
        ],
        out_specs=[wide, kv_out, kv_out],
        scratch_shapes=[
            pltpu.VMEM((length, 128), jnp.bfloat16),
            pltpu.VMEM((length, 128), jnp.bfloat16),
            pltpu.VMEM((HEAD_DIM, length), jnp.bfloat16),
            pltpu.VMEM((length, 128), jnp.float32),
            pltpu.VMEM((length, 128), jnp.float32),
        ],
        compiler_params=pltpu.CompilerParams(vmem_limit_bytes=VMEM_LIMIT),
        cost_estimate=pl.CostEstimate(
            flops=10 * rows * length * width, bytes_accessed=8 * rows * width, transcendentals=0
        ),
    )(queries, grad_context, lse, cosines, sines, keys_values, keys_values)


def rope_tables(rows, tensor):
    halved = HEAD_DIM // 2
    freqs = theta_base ** (-2.0 * jnp.arange(halved, dtype=jnp.float32) / HEAD_DIM)
    places = (tensor * rows + jnp.arange(rows)).astype(jnp.float32)
    angles = places[:, None] * freqs[None, :]
    cosines, sines = jnp.cos(angles), jnp.sin(angles)
    return (
        jnp.concatenate([cosines, cosines] * 2, axis=1),
        jnp.concatenate([-sines, sines] * 2, axis=1),
    )


def turn_heads(values, cosines, sines):
    rows, width = values.shape
    parts = values.reshape(rows, width // HEAD_DIM, 2, HEAD_DIM // 2)
    swapped = parts[:, :, ::-1, :].reshape(rows, width)
    repeat = width // 128
    return values * jnp.tile(cosines, (1, repeat)) + swapped * jnp.tile(sines, (1, repeat))


def start_row(dp, size):
    return pl.multiple_of(dp * size, size)


def on_device(
    dp_size,
    tensor_size,
    tokens,
    attn_gain,
    w_query,
    w_key,
    w_value,
    w_out,
    mlp_gain,
    w_gate,
    w_up,
    w_down,
    cotangent,
):
    tensor_index = lax.axis_index("tensor")
    rows, width = tokens.shape
    heads = w_query.shape[1] * tensor_size // HEAD_DIM
    kv_width = w_key.shape[1]
    kv_heads = kv_width // HEAD_DIM
    group_heads = heads // kv_heads
    q_rows, q_cols = w_query.shape
    kv_rows = w_key.shape[0]
    o_rows, o_cols = w_out.shape
    gain_part = attn_gain.shape[0]
    call = functools.partial(gather, dp_size=dp_size, tensor_size=tensor_size)

    key_value = jnp.concatenate([w_key, w_value], axis=1)
    gains = jnp.zeros((16, 128), jnp.bfloat16)
    gains = gains.at[0, :gain_part].set(attn_gain).at[1, :gain_part].set(mlp_gain)
    gate_full, up_full, down_full = (
        lax.all_gather(w_gate, "dp", axis=0, tiled=True),
        lax.all_gather(w_up, "dp", axis=0, tiled=True),
        lax.all_gather(w_down, "dp", axis=1, tiled=True),
    )
    cot_all = lax.all_gather(cotangent, "tensor", axis=0, tiled=True)
    query_spec = Gather(
        (width, heads * HEAD_DIM),
        lambda ref, dp, t: ref.at[
            pl.ds(start_row(dp, q_rows), q_rows), pl.ds(start_row(t, q_cols), q_cols)
        ],
        lambda ref, dp, half: ref.at[
            pl.ds(pl.multiple_of(dp * q_rows + half * (q_rows // 2), q_rows // 2), q_rows // 2), :
        ],
    )
    kv_all_rows = kv_rows * tensor_size
    kv_spec = Gather(
        (width, 2 * kv_width),
        lambda ref, dp, t: ref.at[pl.ds(start_row(dp * tensor_size + t, kv_rows), kv_rows), :],
        lambda ref, dp, half: ref.at[
            pl.ds(
                pl.multiple_of(dp * kv_all_rows + half * (kv_all_rows // 2), kv_all_rows // 2),
                kv_all_rows // 2,
            ),
            :,
        ],
    )
    gain_spec = Gather(
        (dp_size * tensor_size * 16, 128),
        lambda ref, dp, t: ref.at[pl.ds(start_row(dp * tensor_size + t, 16), 16), :],
        lambda ref, dp, half: ref.at[
            pl.ds(
                pl.multiple_of((2 * dp + half) * tensor_size * 8, tensor_size * 8),
                tensor_size * 8,
            ),
            :,
        ],
    )
    out_spec = Gather(
        (heads * HEAD_DIM, width),
        lambda ref, dp, t: ref.at[
            pl.ds(start_row(t, o_rows), o_rows), pl.ds(start_row(dp, o_cols), o_cols)
        ],
        lambda ref, dp, half: ref.at[
            pl.ds(half * (heads * HEAD_DIM // 2), heads * HEAD_DIM // 2),
            pl.ds(start_row(dp, o_cols), o_cols),
        ],
    )
    row_spec = lambda shape: Gather(
        (tensor_size * shape[0], shape[1]),
        lambda ref, dp, t: ref.at[pl.ds(start_row(t, shape[0]), shape[0]), :],
    )
    query_full, key_value_full, gains_full = call(
        [query_spec, kv_spec, gain_spec], [w_query, key_value, gains], collective_id=1
    )
    gains_full = gains_full.reshape(-1, 16, 128)[:, :2, :gain_part].astype(jnp.float32)
    gain_first = gains_full[:, 0].reshape(width)
    gain_second = gains_full[:, 1].reshape(width)
    cosines, sines = rope_tables(rows, tensor_index)

    residual = tokens.astype(jnp.float32)
    scale_first = lax.rsqrt(jnp.mean(residual * residual, axis=-1, keepdims=True) + epsilon)
    unit_first = residual * scale_first
    normed_first = (unit_first * gain_first).astype(jnp.bfloat16)
    kv_pre = product(normed_first, key_value_full)
    kv_own = jnp.concatenate(
        [turn_heads(kv_pre[:, :kv_width], cosines, sines), kv_pre[:, kv_width:]], axis=1
    ).astype(jnp.bfloat16)
    query_pre = product(normed_first, query_full)
    kv_all, out_full = call([row_spec(kv_own.shape), out_spec], [kv_own, w_out], collective_id=2)
    context, queries, log_sums = attend(
        query_pre, cosines, sines, kv_all, heads, group_heads
    )
    middle = residual + product(context, out_full)
    scale_second = lax.rsqrt(jnp.mean(middle * middle, axis=-1, keepdims=True) + epsilon)
    unit_second = middle * scale_second
    normed_own = (unit_second * gain_second).astype(jnp.bfloat16)
    (normed_second,) = call([row_spec(normed_own.shape)], [normed_own], collective_id=3)

    gate_pre = product(normed_second, gate_full)
    upward = product(normed_second, up_full)
    sigmoid_gate = jax.nn.sigmoid(gate_pre)
    silu_gate = gate_pre * sigmoid_gate
    hidden = (silu_gate * upward).astype(jnp.bfloat16)
    mlp_rows = lax.psum_scatter(
        product(hidden, down_full).astype(jnp.bfloat16), "tensor", scatter_dimension=0, tiled=True
    ).astype(jnp.float32)
    output = (middle + mlp_rows).astype(jnp.bfloat16)
    grad_hidden = product_right(cot_all, down_full)
    grad_gate_pre = (
        grad_hidden * upward * sigmoid_gate * (1.0 + gate_pre * (1.0 - sigmoid_gate))
    ).astype(jnp.bfloat16)
    grad_upward = (grad_hidden * silu_gate).astype(jnp.bfloat16)
    back_part = (
        product_right(grad_gate_pre, gate_full) + product_right(grad_upward, up_full)
    ).astype(jnp.bfloat16)
    back_blocks = exchange(back_part.reshape(tensor_size, rows, width), tensor_size, 4)
    back_second = jnp.sum(back_blocks.astype(jnp.float32), axis=0)
    grad_down_w = product_left(hidden, cot_all).astype(jnp.bfloat16)
    grad_gate_w = product_left(normed_second, grad_gate_pre).astype(jnp.bfloat16)
    grad_up_w = product_left(normed_second, grad_upward).astype(jnp.bfloat16)
    sum_gate, sum_up, sum_down = (
        lax.psum_scatter(grad_gate_w, "dp", scatter_dimension=0, tiled=True).astype(jnp.float32),
        lax.psum_scatter(grad_up_w, "dp", scatter_dimension=0, tiled=True).astype(jnp.float32),
        lax.psum_scatter(grad_down_w, "dp", scatter_dimension=1, tiled=True).astype(jnp.float32),
    )

    grad_gain_second = jnp.sum(back_second * unit_second, axis=0)
    grad_middle = cotangent.astype(jnp.float32) + norm_back(
        back_second, unit_second, scale_second, gain_second
    )
    middle_low = grad_middle.astype(jnp.bfloat16)
    grad_context = product_right(middle_low, out_full).astype(jnp.bfloat16)
    grad_out_w = product_left(context, middle_low).astype(jnp.bfloat16)
    grad_queries, grad_keys, grad_values = attend_back(
        queries, grad_context, log_sums, cosines, sines, kv_all, heads, group_heads
    )
    grad_kv = jnp.concatenate([grad_keys, grad_values], axis=1)
    kv_blocks = exchange(grad_kv.reshape(tensor_size, rows, 2 * kv_width), tensor_size, 5)
    grad_kv_own = jnp.sum(kv_blocks.astype(jnp.float32), axis=0)
    grad_kv_own = jnp.concatenate(
        [turn_heads(grad_kv_own[:, :kv_width], cosines, -sines), grad_kv_own[:, kv_width:]], axis=1
    ).astype(jnp.bfloat16)
    grad_query_w = product_left(normed_first, grad_queries).astype(jnp.bfloat16)
    grad_kv_w = product_left(normed_first, grad_kv_own).astype(jnp.bfloat16)
    back_first = product_right(grad_queries, query_full) + product_right(
        grad_kv_own, key_value_full
    )
    grad_gain_first = jnp.sum(back_first * unit_first, axis=0)
    grad_tokens = grad_middle + norm_back(back_first, unit_first, scale_first, gain_first)

    grad_gains = jnp.zeros((dp_size * tensor_size, 16, 128), jnp.float32)
    grad_gains = grad_gains.at[:, 0, :gain_part].set(grad_gain_first.reshape(-1, gain_part))
    grad_gains = grad_gains.at[:, 8, :gain_part].set(grad_gain_second.reshape(-1, gain_part))
    query_scatter = Scatter(
        (q_rows, q_cols),
        query_spec.half,
        (q_rows // 2, tensor_size * q_cols),
        lambda ref, half: ref.at[pl.ds(half * (q_rows // 2), q_rows // 2), :],
        lambda ref, j: ref.at[:, pl.ds(j * q_cols, q_cols)],
        (q_rows // 2, q_cols),
    )
    kv_scatter = Scatter(
        (kv_rows, 2 * kv_width),
        lambda ref, dp, half: ref.at[
            pl.ds(dp * tensor_size, tensor_size), :, pl.ds(half * kv_width, kv_width)
        ],
        (tensor_size, kv_rows, kv_width),
        lambda ref, half: ref.at[:, pl.ds(half * kv_width, kv_width)],
        lambda ref, j: ref.at[j],
        (kv_rows, kv_width),
    )
    out_scatter = Scatter(
        (o_rows, o_cols),
        lambda ref, dp, half: ref.at[
            :, pl.ds(half * (o_rows // 2), o_rows // 2), pl.ds(start_row(dp, o_cols), o_cols)
        ],
        (tensor_size, o_rows // 2, o_cols),
        lambda ref, half: ref.at[pl.ds(half * (o_rows // 2), o_rows // 2), :],
        lambda ref, j: ref.at[j],
        (o_rows // 2, o_cols),
    )
    gain_scatter = Scatter(
        (16, 128),
        lambda ref, dp, half: ref.at[
            pl.ds(dp * tensor_size, tensor_size), pl.ds(half * 8, 8), :
        ],
        (tensor_size, 8, 128),
        lambda ref, half: ref.at[pl.ds(half * 8, 8), :],
        lambda ref, j: ref.at[j],
        (8, 128),
    )
    sum_out, sum_query, sum_kv, sum_gains = scatter(
        [out_scatter, query_scatter, kv_scatter, gain_scatter],
        [
            grad_out_w.reshape(tensor_size, o_rows, width),
            grad_query_w,
            grad_kv_w.reshape(dp_size * tensor_size, kv_rows, 2 * kv_width),
            grad_gains,
        ],
        dp_size,
        tensor_size,
        6,
    )
    return (
        output,
        grad_tokens,
        sum_gains[0, :gain_part],
        sum_query,
        sum_kv[:, :kv_width],
        sum_kv[:, kv_width:],
        sum_out,
        sum_gains[8, :gain_part],
        sum_gate,
        sum_up,
        sum_down,
    )


def solution(mesh):
    placed = (
        P(("dp", "tensor"), None),
        P(("dp", "tensor")),
        P("dp", "tensor"),
        P(("dp", "tensor"), None),
        P(("dp", "tensor"), None),
        P("tensor", "dp"),
        P(("dp", "tensor")),
        P("dp", "tensor"),
        P("dp", "tensor"),
        P("tensor", "dp"),
        P(("dp", "tensor"), None),
    )
    return jax.shard_map(
        functools.partial(on_device, mesh.shape["dp"], mesh.shape["tensor"]),
        mesh=mesh,
        in_specs=placed,
        out_specs=(
            P(("dp", "tensor"), None),
            P(("dp", "tensor"), None),
            P(("dp", "tensor")),
            P("dp", "tensor"),
            P(("dp", "tensor"), None),
            P(("dp", "tensor"), None),
            P("tensor", "dp"),
            P(("dp", "tensor")),
            P("dp", "tensor"),
            P("dp", "tensor"),
            P("tensor", "dp"),
        ),
        check_vma=False,
    )
```

time: 1710 us -> 884 us (0.52)
  waiting for transfers between devices: 1220 us -> 2.68 us
  Pallas kernels: 0 us -> 660 us
  matrix products: 257 us -> 149 us
  blocking collectives: 85.6 us -> 0 us
  other arithmetic: 79 us -> 27.8 us
    reduce_scatter x10 -> x3, waiting for transfers between devices: 727 us -> 0.01 us  [the longest x1 0.01 us: on_device(): lax.psum_scatter(grad_gate_w, 'dp', scatter_dimension=0, tiled=True)]
    pallas_call x0 -> x8, Pallas kernels: none -> 660 us  [the longest x3 292 us: gather(): pl.pallas_call(functools.partial(gather_kernel, specs, dp_size, tensor_si...]
    all_gather x7 -> x0, waiting for transfers between devices: 269 us -> none  [the longest x1 80 us: on_device(): lax.all_gather((unit_second * gain_second).astype(jnp.bfloat16), 'tensor'...]
    dot_general x6 -> x0, matrix products: 85.8 us -> none  [the longest x1 25.4 us: attend_back(): jnp.einsum('hqd,kd->hqk', grad_seq, value_seq, preferred_element_type=jnp...]
    unnamed x2 -> x0, blocking collectives: 85.6 us -> none
    all_gather x1, waiting for transfers between devices: 67.5 us -> 0.01 us  [on_device(): cot_all = lax.all_gather(cotangent, 'tensor', axis=0, tiled=True)]
    all_gather x1, waiting for transfers between devices: 47.7 us -> 0.01 us  [on_device(): lax.all_gather(w_down, 'dp', axis=1, tiled=True)]
    all_gather x1, waiting for transfers between devices: 41.2 us -> 0.01 us  [on_device(): lax.all_gather(w_up, 'dp', axis=0, tiled=True)]
  transfers between devices with their start and end apart: 22 -> 8, of which waited for: 20 -> 0; matrix products, arithmetic and copies ran while one was open for 18% -> 19% of each run, Pallas kernels for 0% -> 76%
where the time goes in v1:
time: 884 us; the launch traced here: 872 us
  Pallas kernels  660 us (75%)
  matrix products  149 us (17%)
  other arithmetic  27.8 us (3%)
  local copies, waits for them, and re-layouts  16.8 us (2%)
  between operations  15.2 us (2%)
    pallas_call x3, Pallas kernels, gather(): pl.pallas_call(functools.partial(gather_kernel, specs, dp_size, tensor_si...  292 us
    pallas_call x1, Pallas kernels, scatter(): pl.pallas_call(functools.partial(scatter_kernel, specs, dp_size, tensor_s...  158 us
    pallas_call x2, Pallas kernels, exchange(): pl.pallas_call(functools.partial(exchange_kernel, tensor_size), out_shape...  138 us
    dot_general x6, matrix products, product_right(): lax.dot_general(left, right, (((1,), (1,)), ((), ())), preferred_element_...  52.7 us
    dot_general x6, matrix products, product(): return jnp.dot(left, right, preferred_element_type=jnp.float32)  49.1 us
    dot_general x6, matrix products, product_left(): lax.dot_general(left, right, (((0,), (0,)), ((), ())), preferred_element_...  47.1 us
    pallas_call x1, Pallas kernels, attend_back(): pl.pallas_call(functools.partial(attend_back_kernel, group_pairs), grid=(...  39.5 us
    pallas_call x1, Pallas kernels, attend(): pl.pallas_call(functools.partial(attend_kernel, group_pairs), grid=(pairs...  32.5 us
  transfers between devices with their start and end apart: 8, of which 0 were waited for; matrix products, arithmetic and copies ran while one was open for 19% of the time, Pallas kernels for 76%

profile of v1, /device:TPU:25, one launch (start us, length us, event | category | flops | bytes accessed | tf_op | source)
XLA Modules:
  0.0 871.9 jit_solution(13075925072339559624)
XLA Ops:
  10.9 95.3 %shard_map.194 = (bf16[2048,2048]{1,0:T(8,128)(2,1)}, bf16[2048,512]{1,0:T(8,128)(2,1)}, bf16[512,128]{1,0:T(8,128)(2,1)}) custom-call(bf16[256,512]{1,0:T(8,128)(2,1)} %refs_0_.1, bf16[64,512]{1,0:T(8,128)(2,1)} %pad_maximum_fusion.7.refs_1_, bf16[16,128]{1,0:T(8,128)(2,1)} %copy-done.23), custom_call_target="tpu_custom_call" | custom-call | tf_op jit(solution)/shard_map/pallas_call | solution.py:199
  106.2 0.9 slice_convert_fusion.2
  107.5 2.4 fusion.23
  110.9 0.9 fusion.27
  113.4 126.4 %shard_map.195 = (bf16[1024,512]{1,0:T(8,128)(2,1)}, bf16[2048,2048]{1,0:T(8,128)(2,1)}) custom-call(bf16[256,512]{1,0:T(8,128)(2,1)} %pad_maximum_fusion.1.refs_0_, bf16[512,256]{1,0:T(8,128)(2,1)} %refs_1_.1), custom_call_target="tpu_custom_call" | custom-call | tf_op jit(solution)/shard_map/pallas_call | solution.py:199
  239.9 7.1 fusion.25.q_ref
  246.9 32.5 %shard_map.196 = (bf16[256,2048]{1,0:T(8,128)(2,1)}, bf16[256,2048]{1,0:T(8,128)(2,1)}, f32[16,2,256]{2,1,0:T(2,128)}) custom-call(f32[256,2048]{1,0:T(8,128)} %fusion.25.q_ref, f32[256,128]{1,0:T(8,128)} %copy-done.16, f32[256,128]{1,0:T(8,128)} %copy-done.15, bf16[1024,512]{1,0:T(8,128)(2,1)} %get-tuple-element.77.k_ref.v_ref, ...), custom_call_target="tpu_custom_call" | custom-call | flops 2147483648 | bytes 4194304 | tf_op jit(solution)/shard_map/pallas_call | solution.py:497
  279.5 6.2 multiply_reduce_fusion.2
  285.7 1.4 multiply_convert_fusion.3.refs_0_
  287.1 70.0 %shard_map.197 = bf16[1024,2048]{1,0:T(8,128)(2,1)} custom-call(bf16[256,2048]{1,0:T(8,128)(2,1)} %multiply_convert_fusion.3.refs_0_), custom_call_target="tpu_custom_call" | custom-call | tf_op jit(solution)/shard_map/pallas_call | solution.py:199
  357.1 11.7 %fusion.29 = f32[1024,1408]{1,0:T(8,128)} fusion(bf16[1024,2048]{1,0:T(8,128)(2,1)} %shard_map.197, bf16[2048,1408]{1,0:T(8,128)(2,1)} %all-gather.5.cloned.1.call-done), kind=kOutput, calls=%fused_computation.75 | convolution fusion | flops 5905580032 | bytes 15728640 | tf_op jit(solution)/shard_map/dot_general | solution.py:22
  368.8 11.6 %fusion.30 = f32[1024,1408]{1,0:T(8,128)} fusion(bf16[1024,2048]{1,0:T(8,128)(2,1)} %shard_map.197, bf16[2048,1408]{1,0:T(8,128)(2,1)} %all-gather.7.cloned.1.call-done), kind=kOutput, calls=%fused_computation.76 | convolution fusion | flops 5905580032 | bytes 15728640 | tf_op jit(solution)/shard_map/dot_general | solution.py:22
  380.5 16.6 %multiply_convert_fusion = (bf16[1024,1408]{1,0:T(8,128)(2,1)}, bf16[1024,1408]{1,0:T(8,128)(2,1)}, bf16[1024,1408]{1,0:T(8,128)(2,1)}) fusion(f32[1024,1408]{1,0:T(8,128)} %fusion.29, f32[1024,1408]{1,0:T(8,128)} %fusion.30, bf16[1024,2048]{1,0:T(8,128)(2,1)} %all-gather.11.cloned.1.call-done, bf16[1408,2048]{1,0:T(8,128)(2,1)} %all-gather.9.cloned.1.call-done), kind=kOutput, calls=%fused_computation.7 | convolution fusion | flops 5927206912 | bytes 30146560 | tf_op jit(solution)/shard_map/dot_general | solution.py:32
  397.1 10.1 %convolution_convert_fusion.5 = bf16[1024,2048]{1,0:T(8,128)(2,1)} fusion(bf16[1024,1408]{1,0:T(8,128)(2,1)} %get-tuple-element.99, bf16[1408,2048]{1,0:T(8,128)(2,1)S(1)} %copy-done.26), kind=kOutput, calls=%fused_computation.12 | convolution fusion | flops 5907677184 | bytes 12845056 | tf_op jit(solution)/shard_map/dot_general | solution.py:22
  407.5 11.0 %convolution_convert_fusion.2 = bf16[2048,1408]{1,0:T(8,128)(2,1)} fusion(bf16[1024,2048]{1,0:T(8,128)(2,1)} %shard_map.197, bf16[1024,1408]{1,0:T(8,128)(2,1)} %get-tuple-element.98), kind=kOutput, calls=%fused_computation.4 | convolution fusion | flops 5908463616 | bytes 12845056 | tf_op jit(solution)/shard_map/dot_general | solution.py:26
  418.6 11.0 %convolution_convert_fusion.1 = bf16[2048,1408]{1,0:T(8,128)(2,1)} fusion(bf16[1024,2048]{1,0:T(8,128)(2,1)} %shard_map.197, bf16[1024,1408]{1,0:T(8,128)(2,1)} %get-tuple-element.97), kind=kOutput, calls=%fused_computation.3 | convolution fusion | flops 5908463616 | bytes 12845056 | tf_op jit(solution)/shard_map/dot_general | solution.py:26
  429.8 10.5 %convolution_convert_fusion = bf16[1408,2048]{1,0:T(8,128)(2,1)} fusion(bf16[1024,1408]{1,0:T(8,128)(2,1)} %get-tuple-element.99, bf16[1024,2048]{1,0:T(8,128)(2,1)} %all-gather.11.cloned.1.call-done), kind=kOutput, calls=%fused_computation.2 | convolution fusion | flops 5908463616 | bytes 12845056 | tf_op jit(solution)/shard_map/dot_general | solution.py:26
  440.4 9.8 %fusion.31 = f32[1024,2048]{1,0:T(8,128)S(1)} fusion(bf16[1024,1408]{1,0:T(8,128)(2,1)} %get-tuple-element.98, bf16[2048,1408]{1,0:T(8,128)(2,1)} %all-gather.5.cloned.1.call-done), kind=kOutput, calls=%fused_computation.77 | convolution fusion | flops 5905580032 | bytes 17039360 | tf_op jit(solution)/shard_map/dot_general | solution.py:32
  450.2 11.1 %add_convert_fusion = bf16[1024,2048]{1,0:T(8,128)(2,1)} fusion(f32[1024,2048]{1,0:T(8,128)S(1)} %fusion.31, bf16[1024,1408]{1,0:T(8,128)(2,1)S(1)} %copy-done.27, bf16[2048,1408]{1,0:T(8,128)(2,1)} %all-gather.7.cloned.1.call-done), kind=kOutput, calls=%fused_computation.1 | convolution fusion | flops 5909774336 | bytes 21233664 | tf_op jit(solution)/shard_map/dot_general | solution.py:32
  461.3 113.1 %shard_map.198 = bf16[4,256,2048]{2,1,0:T(8,128)(2,1)} custom-call(bf16[4,256,2048]{2,1,0:T(8,128)(2,1)} %bitcast.66), custom_call_target="tpu_custom_call" | custom-call | tf_op jit(solution)/shard_map/pallas_call | solution.py:251
  574.4 3.3 convert_reduce_fusion
  579.7 4.5 multiply_add_fusion
  584.2 6.9 convolution_convert_fusion.7.do_ref
  591.0 39.5 %shard_map.199 = (bf16[256,2048]{1,0:T(8,128)(2,1)}, bf16[1024,256]{1,0:T(8,128)(2,1)}, bf16[1024,256]{1,0:T(8,128)(2,1)}) custom-call(bf16[256,2048]{1,0:T(8,128)(2,1)} %get-tuple-element.80.q_ref, bf16[256,2048]{1,0:T(8,128)(2,1)} %convolution_convert_fusion.7.do_ref, f32[16,2,256]{2,1,0:T(2,128)} %get-tuple-element.81.lse_ref, f32[256,128]{1,0:T(8,128)} %copy-done.16, ...), custom_call_target="tpu_custom_call" | custom-call | flops 5368709120 | bytes 4194304 | tf_op jit(solution)/shard_map/pallas_call | solution.py:602
  630.5 2.5 pad_maximum_fusion
  633.0 24.8 %shard_map.200 = bf16[4,256,512]{2,1,0:T(8,128)(2,1)} custom-call(bf16[4,256,512]{2,1,0:T(8,128)(2,1)} %bitcast.67), custom_call_target="tpu_custom_call" | custom-call | tf_op jit(solution)/shard_map/pallas_call | solution.py:251
  657.8 1.4 convert_reduce_fusion.1
  659.2 0.8 slice.135
  660.8 1.8 copy.29
  662.6 1.7 rev.7
  664.2 1.8 copy.30
  666.1 1.1 fusion.15
  667.3 6.2 fusion.32
  673.5 2.2 fusion.10
  676.4 0.7 scatter.16
  677.1 1.2 scatter.19.refs_3_
  678.4 3.3 convolution_convert_fusion.6
  681.6 5.7 convolution_convert_fusion.3.refs_1_
  687.3 5.6 convolution_convert_fusion.4
  693.0 158.2 %shard_map.201 = (f32[512,256]{1,0:T(8,128)}, f32[256,512]{1,0:T(8,128)}, f32[64,512]{1,0:T(8,128)}, f32[16,128]{1,0:T(8,128)}) custom-call(bf16[4,512,2048]{2,1,0:T(8,128)(2,1)} %bitcast.65, bf16[2048,2048]{1,0:T(8,128)(2,1)} %convolution_convert_fusion.3.refs_1_, bf16[32,64,512]{2,1,0:T(8,128)(2,1)} %bitcast.70, f32[32,16,128]{2,1,0:T(8,128)} %copy-done.9), custom_call_target="tpu_custom_call" | custom-call | tf_op jit(solution)/shard_map/pallas_call | solution.py:411
  851.2 1.2 slice_bitcast_fusion
  852.5 1.5 fusion.28
  854.0 1.9 fusion.9
  855.9 2.4 convert_element_type.105
  858.2 2.4 convert_element_type.107
  860.6 2.3 convert_element_type.109
  862.9 0.8 copy.42
  863.7 0.8 copy.43
  (108 shorter events, 10.8 us)
Async XLA Ops:
  7.2 2.9 copy-start.24
  7.2 2.9 copy-start.25
  7.2 3.1 copy-start.20
  7.2 3.1 copy-start.19
  7.2 100.0 %copy-start = (bf16[256,2048]{1,0:T(8,128)(2,1)S(1)}, bf16[256,2048]{1,0:T(8,128)(2,1)}, u32[]{:S(2)}) copy-start(bf16[256,2048]{1,0:T(8,128)(2,1)} %param.19) | copy-start | bytes 3145732
  7.2 349.9 %all-gather.5.cloned.1.call-start = ((), (), s32[]{:S(2)}) async-start(), calls=%async_computation.4 | async-start | bytes 6488064 | tf_op jit(solution)/shard_map/all_gather | solution.py:689
  8.0 360.9 %all-gather.7.cloned.1.call-start = ((), (), s32[]{:S(2)}) async-start(), calls=%async_computation.5 | async-start | bytes 6488064 | tf_op jit(solution)/shard_map/all_gather | solution.py:690
  8.7 371.8 %all-gather.11.cloned.1.call-start = ((), (), s32[]{:S(2)}) async-start(), calls=%async_computation.8 | async-start | bytes 5242880 | tf_op jit(solution)/shard_map/all_gather | solution.py:693
  9.4 371.0 %all-gather.9.cloned.1.call-start = ((), (), s32[]{:S(2)}) async-start(), calls=%async_computation.6 | async-start | bytes 6488064 | tf_op jit(solution)/shard_map/all_gather | solution.py:691
  10.0 569.7 %reduce-scatter.5.cloned.1.call-start = ((), (), s32[]{:S(2)}) async-start(), calls=%async_computation.7 | async-start | bytes 5242880 | tf_op jit(solution)/shard_map/reduce_scatter | solution.py:772
  10.3 0.7 copy-start.23
  107.2 132.6 %copy-start.17 = (f32[2048]{0:T(1024)}, f32[2048]{0:T(1024)S(1)}, u32[]{:S(2)}) copy-start(f32[2048]{0:T(1024)S(1)} %mul.155) | copy-start | bytes 24580
  107.5 132.3 %copy-start.21 = (f32[256]{0:T(256)}, f32[256]{0:T(256)S(1)}, u32[]{:S(2)}) copy-start(f32[256]{0:T(256)S(1)} %add_rsqrt_fusion.1) | copy-start | bytes 3076
  111.8 135.1 %copy-start.15 = (f32[256,128]{1,0:T(8,128)}, f32[256,128]{1,0:T(8,128)S(1)}, u32[]{:S(2)}) copy-start(f32[256,128]{1,0:T(8,128)S(1)} %get-tuple-element.96.sin_ref) | copy-start | bytes 393220
  111.8 135.1 %copy-start.16 = (f32[256,128]{1,0:T(8,128)}, f32[256,128]{1,0:T(8,128)S(1)}, u32[]{:S(2)}) copy-start(f32[256,128]{1,0:T(8,128)S(1)} %get-tuple-element.112.cos_ref) | copy-start | bytes 393220
  111.9 0.7 copy-start.5
  285.7 292.0 %copy-start.1 = (f32[256,2048]{1,0:T(8,128)}, f32[256,2048]{1,0:T(8,128)S(1)}, u32[]{:S(2)}) copy-start(f32[256,2048]{1,0:T(8,128)S(1)} %get-tuple-element.110) | copy-start | bytes 6291460
  380.5 16.6 %copy-start.26 = (bf16[1408,2048]{1,0:T(8,128)(2,1)S(1)}, bf16[1408,2048]{1,0:T(8,128)(2,1)}, u32[]{:S(2)}) copy-start(bf16[1408,2048]{1,0:T(8,128)(2,1)} %all-gather.9.cloned.1.call-done) | copy-start | bytes 17301508
  407.3 448.6 %reduce-scatter.7.cloned.1.call-start = ((), (), s32[]{:S(2)}) async-start(), calls=%async_computation.9 | async-start | bytes 6488064 | tf_op jit(solution)/shard_map/reduce_scatter | solution.py:790
  418.5 439.7 %reduce-scatter.9.cloned.1.call-start = ((), (), s32[]{:S(2)}) async-start(), calls=%async_computation.10 | async-start | bytes 6488064 | tf_op jit(solution)/shard_map/reduce_scatter | solution.py:791
  429.6 431.0 %reduce-scatter.11.cloned.1.call-start = ((), (), s32[]{:S(2)}) async-start(), calls=%async_computation.11 | async-start | bytes 6488064 | tf_op jit(solution)/shard_map/reduce_scatter | solution.py:792
  440.4 9.8 %copy-start.27 = (bf16[1024,1408]{1,0:T(8,128)(2,1)S(1)}, bf16[1024,1408]{1,0:T(8,128)(2,1)}, u32[]{:S(2)}) copy-start(bf16[1024,1408]{1,0:T(8,128)(2,1)} %get-tuple-element.97) | copy-start | bytes 8650756
  577.7 1.3 copy-start.2
  632.9 33.1 %copy-start.14 = (f32[256,128]{1,0:T(8,128)S(1)}, f32[256,128]{1,0:T(8,128)}, u32[]{:S(2)}) copy-start(f32[256,128]{1,0:T(8,128)} %get-tuple-element.95) | copy-start | bytes 393220
  632.9 33.2 %copy-start.6 = (f32[256,2,128]{2,1,0:T(2,128)S(1)}, f32[256,2,128]{2,1,0:T(2,128)}, u32[]{:S(2)}) copy-start(f32[256,2,128]{2,1,0:T(2,128)} %copy-done.5) | copy-start | bytes 786436
  659.2 0.9 copy-start.4
  667.2 6.3 copy-start.7
  667.2 6.3 copy-start.11
  667.2 6.3 copy-start.18
  667.3 6.3 copy-start.22
  678.4 9.0 %copy-start.9 = (f32[32,16,128]{2,1,0:T(8,128)}, f32[32,16,128]{2,1,0:T(8,128)S(1)}, u32[]{:S(2)}) copy-start(f32[32,16,128]{2,1,0:T(8,128)S(1)} %scatter.19.refs_3_) | copy-start | bytes 786436
  678.4 3.3 copy-start.10
  681.6 5.7 copy-start.8
  693.0 161.0 %copy-start.3 = (f32[256,2048]{1,0:T(8,128)S(1)}, f32[256,2048]{1,0:T(8,128)}, u32[]{:S(2)}) copy-start(f32[256,2048]{1,0:T(8,128)} %get-tuple-element.111) | copy-start | bytes 6291460
  855.9 7.1 copy-start.13
  858.2 5.5 copy-start.12
Sparse Core Ops, SparseCore 0:
  9.9 59.8 all-gather.4
  71.7 51.1 all-gather.6
  124.5 94.7 all-gather.10
  221.0 47.7 all-gather.8
  407.4 95.4 reduce-scatter.4
  506.6 96.2 reduce-scatter.6
  606.4 59.0 reduce-scatter.8
  669.3 75.0 reduce-scatter.10

commit v2 on v1

--- a/solution.py
+++ b/solution.py
@@ -629,6 +629,268 @@
             flops=10 * rows * length * width, bytes_accessed=8 * rows * width, transcendentals=0
         ),
     )(queries, grad_context, lse, cosines, sines, keys_values, keys_values)
+
+
+def block_at(place, tensor, tensor_size):
+    last = tensor_size - 1
+    pairs = jnp.minimum(tensor, last - tensor)
+    near = lax.div(place + 1, 2)
+    paired = jnp.where(lax.rem(place, 2) == 1, tensor - near, tensor + near)
+    far = place - pairs
+    lone = jnp.where(tensor > last - tensor, tensor - far, tensor + far)
+    return jnp.where(place <= 2 * pairs, paired, lone)
+
+
+def mlp_kernel(
+    tensor_size,
+    normed_ref,
+    cot_ref,
+    gate_ref,
+    up_ref,
+    down_ref,
+    back_ref,
+    y_ref,
+    d_gate_ref,
+    d_up_ref,
+    d_down_ref,
+    normed,
+    cot,
+    gate,
+    up,
+    down,
+    hidden,
+    d_gate,
+    d_up,
+    y_stage,
+    stage,
+    landing,
+    load_sem,
+    n_send,
+    n_recv,
+    y_sem,
+    b_send,
+    b_recv,
+    out_sem,
+):
+    dp, tensor = lax.axis_index("dp"), lax.axis_index("tensor")
+    rows, width = normed_ref.shape
+    units = gate.shape[1]
+    loads = [
+        pltpu.make_async_copy(source, target, load_sem.at[i])
+        for i, (source, target) in enumerate(
+            (
+                (normed_ref, normed.at[tensor]),
+                (gate_ref, gate),
+                (up_ref, up),
+                (down_ref, down),
+                (cot_ref, cot),
+            )
+        )
+    ]
+    for load in loads:
+        load.start()
+    greet((dp, tensor, tensor_size), False, True, 0)
+    has = [tensor + 1 < tensor_size, tensor > 0]
+
+    def n_copy(block, way, source=None):
+        return pltpu.make_async_remote_copy(
+            src_ref=normed.at[block] if source is None else source,
+            dst_ref=normed.at[block],
+            send_sem=n_send.at[way, block],
+            recv_sem=n_recv.at[block],
+            device_id=(dp, tensor + 1 if way == 0 else tensor - 1),
+            device_id_type=MESH,
+        )
+
+    for way in (0, 1):
+        pl.when(has[way])(n_copy(tensor, way, normed_ref).start)
+    landing[tensor] = jnp.zeros((rows, width), landing.dtype)
+
+    def pump(distance):
+        for way, block in ((0, tensor - distance), (1, tensor + distance)):
+
+            @pl.when((block >= 0) & (block < tensor_size))
+            def _():
+                n_copy(block, way).wait_recv()
+                pl.when(has[way])(n_copy(block, way).start)
+
+    def distance_at(place):
+        return jnp.abs(block_at(place, tensor, tensor_size) - tensor)
+
+    inner = (tensor > 0) & (tensor + 1 < tensor_size)
+
+    def b_copy(block, slot):
+        return pltpu.make_async_remote_copy(
+            src_ref=stage.at[block],
+            dst_ref=landing.at[slot],
+            send_sem=b_send.at[block],
+            recv_sem=b_recv.at[slot],
+            device_id=(dp, block),
+            device_id_type=MESH,
+        )
+
+    def y_copy(block, slot):
+        return pltpu.make_async_copy(y_stage.at[slot], y_ref.at[block], y_sem.at[slot])
+
+    for load in loads[:3]:
+        load.wait()
+
+    def chunk(place, carry):
+        block = block_at(place, tensor, tensor_size)
+        fresh = (place >= 1) & (distance_at(place) != distance_at(place - 1))
+
+        @pl.when(fresh & jnp.logical_not((place >= 2) & inner))
+        def _():
+            pump(distance_at(place))
+
+        rows_in = normed[block]
+        gate_pre = product(rows_in, gate[...])
+        upward = product(rows_in, up[...])
+
+        @pl.when((place >= 1) & (place + 1 < tensor_size) & inner)
+        def _():
+            @pl.when(distance_at(place + 1) != distance_at(place))
+            def _():
+                pump(distance_at(place + 1))
+
+        @pl.when(place == 0)
+        def _():
+            for load in loads[3:]:
+                load.wait()
+
+        sigmoid = 1.0 / (1.0 + jnp.exp(-gate_pre))
+        silu = gate_pre * sigmoid
+        active = (silu * upward).astype(jnp.bfloat16)
+        hidden[block] = active
+        slot = lax.rem(place, 2)
+
+        @pl.when(place >= 2)
+        def _():
+            y_copy(block, slot).wait()
+
+        y_stage[slot] = product(active, down[...]).astype(jnp.bfloat16)
+        y_copy(block, slot).start()
+        grad_hidden = product_right(cot[block], down[...])
+        low_gate = (
+            grad_hidden * upward * sigmoid * (1.0 + gate_pre * (1.0 - sigmoid))
+        ).astype(jnp.bfloat16)
+        low_up = (grad_hidden * silu).astype(jnp.bfloat16)
+        d_gate[block] = low_gate
+        d_up[block] = low_up
+        back = product_right(low_gate, gate[...]) + product_right(low_up, up[...])
+
+        @pl.when(block == tensor)
+        def _():
+            back_ref[...] = back
+
+        @pl.when(block != tensor)
+        def _():
+            stage[block] = back.astype(stage.dtype)
+            b_copy(block, tensor).start()
+
+        return carry
+
+    lax.fori_loop(0, tensor_size, chunk, 0)
+    for slot in range(2):
+        y_copy(0, slot).wait()
+
+    all_rows = tensor_size * rows
+
+    def weight_grad(left, right, out, out_hbm, sem):
+        extent = left.shape[2]
+        tile = 256 if extent % 256 == 0 else 128 if extent % 128 == 0 else extent
+
+        def body(step, carry):
+            at = pl.ds(pl.multiple_of(step * tile, tile), tile)
+            columns = left[:, :, at].reshape(all_rows, tile)
+            out[at, :] = product_left(columns, right[...].reshape(all_rows, -1)).astype(out.dtype)
+            return carry
+
+        lax.fori_loop(0, extent // tile, body, 0)
+        pltpu.make_async_copy(out, out_hbm, sem).start()
+
+    weight_grad(hidden, cot, down, d_down_ref, out_sem.at[0])
+    weight_grad(normed, d_gate, gate, d_gate_ref, out_sem.at[1])
+    weight_grad(normed, d_up, up, d_up_ref, out_sem.at[2])
+
+    for other in range(tensor_size):
+
+        @pl.when(other != tensor)
+        def _():
+            b_copy(other, other).wait_recv()
+
+    slab = 16
+
+    def add_slab(step, carry):
+        at = pl.ds(pl.multiple_of(step * slab, slab), slab)
+        total = back_ref[at, :]
+        for other in range(tensor_size):
+            total = total + landing[other, at, :].astype(jnp.float32)
+        back_ref[at, :] = total
+        return carry
+
+    lax.fori_loop(0, rows // slab, add_slab, 0)
+    pltpu.make_async_copy(down, d_down_ref, out_sem.at[0]).wait()
+    pltpu.make_async_copy(gate, d_gate_ref, out_sem.at[1]).wait()
+    pltpu.make_async_copy(up, d_up_ref, out_sem.at[2]).wait()
+    for other in range(tensor_size):
+
+        @pl.when(other != tensor)
+        def _():
+            b_copy(other, tensor).wait_send()
+
+        for way in (0, 1):
+            sent = has[way] & ((other <= tensor) if way == 0 else (other >= tensor))
+            pl.when(sent)(n_copy(other, way).wait_send)
+
+
+def feed_forward(normed, cot_all, gate, up, down, tensor_size, collective_id):
+    rows, width = normed.shape
+    units = gate.shape[1]
+    low = jnp.bfloat16
+    tokens = (tensor_size, rows, width)
+    inner = (tensor_size, rows, units)
+    dma = pltpu.SemaphoreType.DMA
+    return pl.pallas_call(
+        functools.partial(mlp_kernel, tensor_size),
+        out_shape=[
+            jax.ShapeDtypeStruct((rows, width), jnp.float32),
+            jax.ShapeDtypeStruct(tokens, low),
+            jax.ShapeDtypeStruct(gate.shape, low),
+            jax.ShapeDtypeStruct(up.shape, low),
+            jax.ShapeDtypeStruct(down.shape, low),
+        ],
+        in_specs=[ANY] * 5,
+        out_specs=[VMEM] + [ANY] * 4,
+        scratch_shapes=[
+            pltpu.VMEM(tokens, low),
+            pltpu.VMEM(tokens, low),
+            pltpu.VMEM(gate.shape, low),
+            pltpu.VMEM(up.shape, low),
+            pltpu.VMEM(down.shape, low),
+            pltpu.VMEM(inner, low),
+            pltpu.VMEM(inner, low),
+            pltpu.VMEM(inner, low),
+            pltpu.VMEM((2, rows, width), low),
+            pltpu.VMEM(tokens, low),
+            pltpu.VMEM(tokens, low),
+            dma((5,)),
+            dma((2, tensor_size)),
+            dma((tensor_size,)),
+            dma((2,)),
+            dma((tensor_size,)),
+            dma((tensor_size,)),
+            dma((3,)),
+        ],
+        compiler_params=pltpu.CompilerParams(
+            collective_id=collective_id, has_side_effects=True, vmem_limit_bytes=60 * 2**20
+        ),
+        cost_estimate=pl.CostEstimate(
+            flops=18 * tensor_size * rows * width * units,
+            bytes_accessed=8 * width * units,
+            transcendentals=0,
+        ),
+    )(normed, cot_all.reshape(tokens), gate, up, down)
 
 
 def rope_tables(rows, tensor):
@@ -762,30 +1024,13 @@
     scale_second = lax.rsqrt(jnp.mean(middle * middle, axis=-1, keepdims=True) + epsilon)
     unit_second = middle * scale_second
     normed_own = (unit_second * gain_second).astype(jnp.bfloat16)
-    (normed_second,) = call([row_spec(normed_own.shape)], [normed_own], collective_id=3)
-
-    gate_pre = product(normed_second, gate_full)
-    upward = product(normed_second, up_full)
-    sigmoid_gate = jax.nn.sigmoid(gate_pre)
-    silu_gate = gate_pre * sigmoid_gate
-    hidden = (silu_gate * upward).astype(jnp.bfloat16)
+    back_second, mlp_part, grad_gate_w, grad_up_w, grad_down_w = feed_forward(
+        normed_own, cot_all, gate_full, up_full, down_full, tensor_size, 3
+    )
     mlp_rows = lax.psum_scatter(
-        product(hidden, down_full).astype(jnp.bfloat16), "tensor", scatter_dimension=0, tiled=True
+        mlp_part.reshape(tensor_size * rows, width), "tensor", scatter_dimension=0, tiled=True
     ).astype(jnp.float32)
     output = (middle + mlp_rows).astype(jnp.bfloat16)
-    grad_hidden = product_right(cot_all, down_full)
-    grad_gate_pre = (
-        grad_hidden * upward * sigmoid_gate * (1.0 + gate_pre * (1.0 - sigmoid_gate))
-    ).astype(jnp.bfloat16)
-    grad_upward = (grad_hidden * silu_gate).astype(jnp.bfloat16)
-    back_part = (
-        product_right(grad_gate_pre, gate_full) + product_right(grad_upward, up_full)
-    ).astype(jnp.bfloat16)
-    back_blocks = exchange(back_part.reshape(tensor_size, rows, width), tensor_size, 4)
-    back_second = jnp.sum(back_blocks.astype(jnp.float32), axis=0)
-    grad_down_w = product_left(hidden, cot_all).astype(jnp.bfloat16)
-    grad_gate_w = product_left(normed_second, grad_gate_pre).astype(jnp.bfloat16)
-    grad_up_w = product_left(normed_second, grad_upward).astype(jnp.bfloat16)
     sum_gate, sum_up, sum_down = (
         lax.psum_scatter(grad_gate_w, "dp", scatter_dimension=0, tiled=True).astype(jnp.float32),
         lax.psum_scatter(grad_up_w, "dp", scatter_dimension=0, tiled=True).astype(jnp.float32),

time: 884 us -> 816 us (0.923)
  matrix products: 149 us -> 46.1 us
  waiting for transfers between devices: 2.68 us -> 75.6 us
  Pallas kernels: 660 us -> 622 us
    pallas_call x0 -> x1, Pallas kernels: none -> 155 us  [feed_forward(): pl.pallas_call(functools.partial(mlp_kernel, tensor_size), out_shape=[jax...]
    pallas_call x2 -> x1, Pallas kernels: 138 us -> 25.6 us  [exchange(): pl.pallas_call(functools.partial(exchange_kernel, tensor_size), out_shape...]
    pallas_call x3 -> x2, Pallas kernels: 292 us -> 203 us  [gather(): pl.pallas_call(functools.partial(gather_kernel, specs, dp_size, tensor_si...]
    reduce_scatter x1, waiting for transfers between devices: 0.01 us -> 71.5 us  [on_device(): lax.psum_scatter(mlp_part.reshape(tensor_size * rows, width), 'tensor', s...]
    dot_general x6 -> x3, matrix products: 52.7 us -> 15.8 us  [product_right(): lax.dot_general(left, right, (((1,), (1,)), ((), ())), preferred_element_...]
    dot_general x6 -> x3, matrix products: 49.1 us -> 15.8 us  [product(): return jnp.dot(left, right, preferred_element_type=jnp.float32)]
    dot_general x6 -> x3, matrix products: 47.1 us -> 14.5 us  [product_left(): lax.dot_general(left, right, (((0,), (0,)), ((), ())), preferred_element_...]
  transfers between devices with their start and end apart: 8 -> 8, of which waited for: 0 -> 1; matrix products, arithmetic and copies ran while one was open for 19% -> 11% of each run, Pallas kernels for 76% -> 58%
where the time goes in v2:
time: 816 us; the launch traced here: 803 us
  Pallas kernels  622 us (76%)
  waiting for transfers between devices  75.6 us (9%)
  matrix products  46.1 us (6%)
  other arithmetic  27 us (3%)
  local copies, waits for them, and re-layouts  16.8 us (2%)
  between operations  14.8 us (2%)
    pallas_call x2, Pallas kernels, gather(): pl.pallas_call(functools.partial(gather_kernel, specs, dp_size, tensor_si...  203 us
    pallas_call x1, Pallas kernels, scatter(): pl.pallas_call(functools.partial(scatter_kernel, specs, dp_size, tensor_s...  167 us
    pallas_call x1, Pallas kernels, feed_forward(): pl.pallas_call(functools.partial(mlp_kernel, tensor_size), out_shape=[jax...  155 us
    reduce_scatter x1, waiting for transfers between devices, on_device(): lax.psum_scatter(mlp_part.reshape(tensor_size * rows, width), 'tensor', s...  71.5 us
    pallas_call x1, Pallas kernels, attend_back(): pl.pallas_call(functools.partial(attend_back_kernel, group_pairs), grid=(...  39.5 us
    pallas_call x1, Pallas kernels, attend(): pl.pallas_call(functools.partial(attend_kernel, group_pairs), grid=(pairs...  32.6 us
    pallas_call x1, Pallas kernels, exchange(): pl.pallas_call(functools.partial(exchange_kernel, tensor_size), out_shape...  25.6 us
  transfers between devices with their start and end apart: 8, of which 1 were waited for; matrix products, arithmetic and copies ran while one was open for 11% of the time, Pallas kernels for 58%

profile of v2, /device:TPU:25, one launch (start us, length us, event | category | flops | bytes accessed | tf_op | source)
XLA Modules:
  0.0 803.3 jit_solution(5011499327334111431)
XLA Ops:
  7.3 0.7 all-gather.5.cloned.1.call-update
  8.0 0.7 all-gather.11.cloned.1.call-update
  8.8 0.7 all-gather.7.cloned.1.call-update
  10.3 0.6 pad_maximum_fusion.7.refs_1_
  10.9 102.0 %shard_map.194 = (bf16[2048,2048]{1,0:T(8,128)(2,1)}, bf16[2048,512]{1,0:T(8,128)(2,1)}, bf16[512,128]{1,0:T(8,128)(2,1)}) custom-call(bf16[256,512]{1,0:T(8,128)(2,1)} %refs_0_.1, bf16[64,512]{1,0:T(8,128)(2,1)} %pad_maximum_fusion.7.refs_1_, bf16[16,128]{1,0:T(8,128)(2,1)} %copy-done.17), custom_call_target="tpu_custom_call" | custom-call | tf_op jit(solution)/shard_map/pallas_call | solution.py:199
  113.0 0.9 slice_convert_fusion.2
  114.3 2.4 fusion.22
  118.3 0.7 pad_maximum_fusion.1.refs_0_
  119.0 100.7 %shard_map.195 = (bf16[1024,512]{1,0:T(8,128)(2,1)}, bf16[2048,2048]{1,0:T(8,128)(2,1)}) custom-call(bf16[256,512]{1,0:T(8,128)(2,1)} %pad_maximum_fusion.1.refs_0_, bf16[512,256]{1,0:T(8,128)(2,1)} %refs_1_.1), custom_call_target="tpu_custom_call" | custom-call | tf_op jit(solution)/shard_map/pallas_call | solution.py:199
  219.7 7.1 fusion.24.q_ref
  226.8 32.6 %shard_map.196 = (bf16[256,2048]{1,0:T(8,128)(2,1)}, bf16[256,2048]{1,0:T(8,128)(2,1)}, f32[16,2,256]{2,1,0:T(2,128)}) custom-call(f32[256,2048]{1,0:T(8,128)} %fusion.24.q_ref, f32[256,128]{1,0:T(8,128)} %copy-done.12, f32[256,128]{1,0:T(8,128)} %copy-done.11, bf16[1024,512]{1,0:T(8,128)(2,1)} %get-tuple-element.82.k_ref.v_ref, ...), custom_call_target="tpu_custom_call" | custom-call | flops 2147483648 | bytes 4194304 | tf_op jit(solution)/shard_map/pallas_call | solution.py:497
  259.4 6.3 multiply_reduce_fusion.2
  266.4 1.2 multiply_convert_fusion.normed_ref
  267.6 155.1 %shard_map.197 = (f32[256,2048]{1,0:T(8,128)}, bf16[4,256,2048]{2,1,0:T(8,128)(2,1)}, bf16[2048,1408]{1,0:T(8,128)(2,1)}, bf16[2048,1408]{1,0:T(8,128)(2,1)}, bf16[1408,2048]{1,0:T(8,128)(2,1)}) custom-call(bf16[256,2048]{1,0:T(8,128)(2,1)} %multiply_convert_fusion.normed_ref, bf16[4,256,2048]{2,1,0:T(8,128)(2,1)} %bitcast.63, ...), custom_call_target="tpu_custom_call" | custom-call | flops 53150220288 | bytes 23068672 | tf_op jit(solution)/shard_map/pallas_call | solution.py:854
  423.4 0.7 reduce-scatter.9.cloned.1.call-update
  424.8 2.8 multiply_reduce_fusion
  427.6 1.4 reshape.305
  429.0 1.2 broadcast_multiply_fusion.1
  430.2 71.5 %reduce-scatter.5.cloned.1.call-done = bf16[256,2048]{1,0:T(8,128)(2,1)} async-done(((bf16[1024,2048]{1,0:T(8,128)(2,1)}), bf16[256,2048]{1,0:T(8,128)(2,1)}) %reduce-scatter.5.cloned.1.call-update) | async-done | bytes 1048592 | tf_op jit(solution)/shard_map/reduce_scatter | solution.py:1030
  501.7 4.5 multiply_add_fusion
  506.2 6.7 convolution_convert_fusion.3.do_ref
  513.0 39.5 %shard_map.198 = (bf16[256,2048]{1,0:T(8,128)(2,1)}, bf16[1024,256]{1,0:T(8,128)(2,1)}, bf16[1024,256]{1,0:T(8,128)(2,1)}) custom-call(bf16[256,2048]{1,0:T(8,128)(2,1)} %get-tuple-element.87.q_ref, bf16[256,2048]{1,0:T(8,128)(2,1)} %convolution_convert_fusion.3.do_ref, f32[16,2,256]{2,1,0:T(2,128)} %get-tuple-element.88.lse_ref, f32[256,128]{1,0:T(8,128)} %copy-done.12, ...), custom_call_target="tpu_custom_call" | custom-call | flops 5368709120 | bytes 4194304 | tf_op jit(solution)/shard_map/pallas_call | solution.py:602
  552.4 2.2 pad_maximum_fusion
  554.7 25.6 %shard_map.199 = bf16[4,256,512]{2,1,0:T(8,128)(2,1)} custom-call(bf16[4,256,512]{2,1,0:T(8,128)(2,1)} %bitcast.50), custom_call_target="tpu_custom_call" | custom-call | tf_op jit(solution)/shard_map/pallas_call | solution.py:251
  580.3 1.6 convert_reduce_fusion
  581.9 0.8 slice.135
  582.7 0.7 slice.146
  583.4 1.8 copy.29
  585.2 1.7 rev.7
  586.9 1.8 copy.30
  588.8 1.1 fusion.14
  589.9 6.9 fusion.28
  596.8 2.2 fusion.9
  599.0 0.7 reshape.304
  599.7 0.7 scatter.16
  600.4 1.2 scatter.19.refs_3_
  601.6 3.2 convolution_convert_fusion.2
  604.9 5.7 convolution_convert_fusion.refs_1_
  610.6 5.6 convolution_convert_fusion.1
  616.2 166.8 %shard_map.200 = (f32[512,256]{1,0:T(8,128)}, f32[256,512]{1,0:T(8,128)}, f32[64,512]{1,0:T(8,128)}, f32[16,128]{1,0:T(8,128)}) custom-call(bf16[4,512,2048]{2,1,0:T(8,128)(2,1)} %bitcast.48, bf16[2048,2048]{1,0:T(8,128)(2,1)} %convolution_convert_fusion.refs_1_, bf16[32,64,512]{2,1,0:T(8,128)(2,1)} %bitcast.53, f32[32,16,128]{2,1,0:T(8,128)} %copy-done.6), custom_call_target="tpu_custom_call" | custom-call | tf_op jit(solution)/shard_map/pallas_call | solution.py:411
  783.0 1.2 slice_bitcast_fusion
  784.2 1.5 fusion.27
  785.7 1.9 fusion.8
  787.6 2.3 convert_element_type.71
  789.9 2.4 convert_element_type.72
  792.3 2.4 convert_element_type.73
  794.7 0.8 copy.42
  795.5 0.8 copy.43
  (83 shorter events, 5.1 us)
Async XLA Ops:
  7.2 2.9 copy-start.19
  7.2 2.9 copy-start.20
  7.2 3.1 copy-start.14
  7.2 3.1 copy-start.13
  7.2 106.8 %copy-start = (bf16[256,2048]{1,0:T(8,128)(2,1)S(1)}, bf16[256,2048]{1,0:T(8,128)(2,1)}, u32[]{:S(2)}) copy-start(bf16[256,2048]{1,0:T(8,128)(2,1)} %param.19) | copy-start | bytes 3145732
  7.2 260.4 %all-gather.5.cloned.1.call-start = ((), (), s32[]{:S(2)}) async-start(), calls=%async_computation.4 | async-start | bytes 5242880 | tf_op jit(solution)/shard_map/all_gather | solution.py:955
  8.0 259.6 %all-gather.11.cloned.1.call-start = ((), (), s32[]{:S(2)}) async-start(), calls=%async_computation.7 | async-start | bytes 6488064 | tf_op jit(solution)/shard_map/all_gather | solution.py:953
  8.7 258.9 %all-gather.7.cloned.1.call-start = ((), (), s32[]{:S(2)}) async-start(), calls=%async_computation.5 | async-start | bytes 6488064 | tf_op jit(solution)/shard_map/all_gather | solution.py:951
  9.4 258.1 %all-gather.9.cloned.1.call-start = ((), (), s32[]{:S(2)}) async-start(), calls=%async_computation.6 | async-start | bytes 6488064 | tf_op jit(solution)/shard_map/all_gather | solution.py:952
  10.0 491.7 %reduce-scatter.5.cloned.1.call-start = ((), (), s32[]{:S(2)}) async-start(), calls=%async_computation.8 | async-start | bytes 5242880 | tf_op jit(solution)/shard_map/reduce_scatter | solution.py:1030
  10.3 0.7 copy-start.17
  114.3 105.4 %copy-start.15 = (f32[256]{0:T(256)}, f32[256]{0:T(256)S(1)}, u32[]{:S(2)}) copy-start(f32[256]{0:T(256)S(1)} %add_rsqrt_fusion.1) | copy-start | bytes 3076
  118.0 108.8 %copy-start.11 = (f32[256,128]{1,0:T(8,128)}, f32[256,128]{1,0:T(8,128)S(1)}, u32[]{:S(2)}) copy-start(f32[256,128]{1,0:T(8,128)S(1)} %get-tuple-element.106.sin_ref) | copy-start | bytes 393220
  118.0 108.8 %copy-start.12 = (f32[256,128]{1,0:T(8,128)}, f32[256,128]{1,0:T(8,128)S(1)}, u32[]{:S(2)}) copy-start(f32[256,128]{1,0:T(8,128)S(1)} %get-tuple-element.119.cos_ref) | copy-start | bytes 393220
  265.7 159.1 %copy-start.1 = (f32[256,2048]{1,0:T(8,128)}, f32[256,2048]{1,0:T(8,128)S(1)}, u32[]{:S(2)}) copy-start(f32[256,2048]{1,0:T(8,128)S(1)} %get-tuple-element.117) | copy-start | bytes 6291460
  265.7 0.6 copy-start.18
  422.7 364.9 %reduce-scatter.7.cloned.1.call-start = ((), (), s32[]{:S(2)}) async-start(), calls=%async_computation.9 | async-start | bytes 6488064 | tf_op jit(solution)/shard_map/reduce_scatter | solution.py:1035
  423.3 366.6 %reduce-scatter.9.cloned.1.call-start = ((), (), s32[]{:S(2)}) async-start(), calls=%async_computation.10 | async-start | bytes 6488064 | tf_op jit(solution)/shard_map/reduce_scatter | solution.py:1036
  424.1 368.2 %reduce-scatter.11.cloned.1.call-start = ((), (), s32[]{:S(2)}) async-start(), calls=%async_computation.11 | async-start | bytes 6488064 | tf_op jit(solution)/shard_map/reduce_scatter | solution.py:1037
  581.9 0.9 copy-start.3
  589.9 6.9 copy-start.4
  589.9 6.9 copy-start.8
  589.9 6.9 copy-start.16
  601.6 8.9 %copy-start.6 = (f32[32,16,128]{2,1,0:T(8,128)}, f32[32,16,128]{2,1,0:T(8,128)S(1)}, u32[]{:S(2)}) copy-start(f32[32,16,128]{2,1,0:T(8,128)S(1)} %scatter.19.refs_3_) | copy-start | bytes 786436
  601.6 3.2 copy-start.7
  604.9 5.7 copy-start.5
  616.2 169.5 %copy-start.2 = (f32[256,2048]{1,0:T(8,128)S(1)}, f32[256,2048]{1,0:T(8,128)}, u32[]{:S(2)}) copy-start(f32[256,2048]{1,0:T(8,128)} %get-tuple-element.118) | copy-start | bytes 6291460
  789.9 4.7 copy-start.10
  792.3 3.2 copy-start.9
Sparse Core Ops, SparseCore 0:
  9.6 93.2 all-gather.4
  104.8 45.5 all-gather.10
  152.3 65.9 all-gather.6
  220.0 43.6 all-gather.8
  422.9 78.7 reduce-scatter.4
  505.4 60.0 reduce-scatter.6
  568.9 60.7 reduce-scatter.8
  633.6 83.4 reduce-scatter.10

commit v3 on v2

--- a/solution.py
+++ b/solution.py
@@ -82,103 +82,166 @@
 
 
 class Gather:
-    def __init__(self, shape, slot, half=None):
-        self.shape, self.slot, self.half = shape, slot, half
-
-
-def gather_kernel(specs, dp_size, tensor_size, *refs):
-    count = len(specs)
-    sources, outs = refs[:count], refs[count : 2 * count]
-    own_sem, z_send, z_recv, h_send, h_recv = refs[2 * count :]
-    dp, tensor = lax.axis_index("dp"), lax.axis_index("tensor")
-    dp_bits = dp_size.bit_length() - 1
-    hyper = [i for i in range(count) if specs[i].half is not None]
-    greet((dp, tensor, tensor_size), True, False, dp_bits if hyper else 0)
-
-    def z_copy(i, block, way, source=None):
-        slot = specs[i].slot(outs[i], dp, block)
+    def __init__(self, shape, slot, half=None, line=True):
+        self.shape, self.slot, self.half, self.line = shape, slot, half, line
+
+
+class GatherRun:
+    def __init__(self, specs, dp_size, tensor_size, sources, outs, held, sems):
+        self.specs, self.sources, self.outs, self.held = specs, sources, outs, held
+        self.own_sem, self.z_send, self.z_recv, self.h_send, self.h_recv = sems
+        self.dp, self.tensor = lax.axis_index("dp"), lax.axis_index("tensor")
+        self.tensor_size, self.dp_bits = tensor_size, dp_size.bit_length() - 1
+        self.order = orders(self.dp_bits, True)
+        self.hyper = [i for i, spec in enumerate(specs) if spec.half is not None]
+        self.lines = [i for i, spec in enumerate(specs) if spec.line]
+        self.early = [n for n, i in enumerate(self.hyper) if not specs[i].line]
+        self.late = [n for n, i in enumerate(self.hyper) if specs[i].line]
+        self.can = [self.tensor + 1 < tensor_size, self.tensor > 0]
+
+    def greet(self):
+        greet(
+            (self.dp, self.tensor, self.tensor_size),
+            bool(self.lines),
+            False,
+            self.dp_bits if self.hyper else 0,
+        )
+
+    def z_copy(self, i, block, way, source=None):
+        slot = self.specs[i].slot(self.outs[i], self.dp, block)
         return pltpu.make_async_remote_copy(
             src_ref=slot if source is None else source,
             dst_ref=slot,
-            send_sem=z_send.at[i, way, block],
-            recv_sem=z_recv.at[i, block],
-            device_id=(dp, tensor + 1 if way == 0 else tensor - 1),
+            send_sem=self.z_send.at[i, way, block],
+            recv_sem=self.z_recv.at[i, block],
+            device_id=(self.dp, self.tensor + 1 if way == 0 else self.tensor - 1),
             device_id_type=MESH,
         )
 
-    can = [tensor + 1 < tensor_size, tensor > 0]
-    for i in range(count):
+    def own(self, i):
+        slot = self.specs[i].slot(self.outs[i], self.dp, self.tensor)
+        return pltpu.make_async_copy(self.held[i], slot, self.own_sem.at[i])
+
+    def begin_line(self, i):
         for way in (0, 1):
-
-            @pl.when(can[way])
+            pl.when(self.can[way])(self.z_copy(i, self.tensor, way, self.sources[i]).start)
+
+    def begin(self, slow=()):
+        loads = [
+            pltpu.make_async_copy(source, held, self.own_sem.at[i])
+            for i, (source, held) in enumerate(zip(self.sources, self.held))
+        ]
+        for load in loads:
+            load.start()
+        for i in self.lines:
+            if i not in slow:
+                self.begin_line(i)
+        for i, load in enumerate(loads):
+            load.wait()
+            self.own(i).start()
+        for n in self.early:
+            self.own(self.hyper[n]).wait()
+            self.hop(n, 0)
+
+    def line(self, i, step):
+        for way, block in ((0, self.tensor - step), (1, self.tensor + step)):
+
+            @pl.when((block >= 0) & (block < self.tensor_size))
             def _():
-                z_copy(i, tensor, way, sources[i]).start()
-
-    owns = [
-        pltpu.make_async_copy(sources[i], specs[i].slot(outs[i], dp, tensor), own_sem.at[i])
-        for i in range(count)
-    ]
-    for own in owns:
-        own.start()
-    for step in range(1, tensor_size):
-        for i in range(count):
-            for way, block in ((0, tensor - step), (1, tensor + step)):
-
-                @pl.when((block >= 0) & (block < tensor_size))
-                def _():
-                    z_copy(i, block, way).wait_recv()
-
-                    @pl.when(can[way])
-                    def _():
-                        z_copy(i, block, way).start()
-
-    for own in owns:
-        own.wait()
-
-    order = orders(dp_bits, True)
-
-    def h_copy(n, half, rank, place):
-        spec, out = specs[hyper[n]], outs[hyper[n]]
-        bits = order[half]
-        part = spec.half(out, masked(dp, bits, rank), half)
+                self.z_copy(i, block, way).wait_recv()
+                pl.when(self.can[way])(self.z_copy(i, block, way).start)
+
+    def part(self, n, half, rank):
+        i = self.hyper[n]
+        return self.specs[i].half(self.outs[i], masked(self.dp, self.order[half], rank), half)
+
+    def h_copy(self, n, half, rank, place):
         return pltpu.make_async_remote_copy(
-            src_ref=part,
-            dst_ref=part,
-            send_sem=h_send.at[n, half, rank, place],
-            recv_sem=h_recv.at[n, half, rank | 1 << place],
-            device_id=(flip(dp, bits[place]), tensor),
+            src_ref=self.part(n, half, rank),
+            dst_ref=self.part(n, half, rank),
+            send_sem=self.h_send.at[n, half, rank, place],
+            recv_sem=self.h_recv.at[n, half, rank | 1 << place],
+            device_id=(flip(self.dp, self.order[half][place]), self.tensor),
             device_id_type=MESH,
         )
 
-    if hyper:
-        for rank in range(1 << dp_bits):
-            top = rank.bit_length()
-            for n in range(len(hyper)):
+    def hop(self, n, rank):
+        for half in (0, 1):
+            if rank:
+                wait_part(
+                    self.part(n, half, rank),
+                    self.h_recv.at[n, half, rank],
+                    self.h_send.at[n, half, 0, 0],
+                    (flip(self.dp, 0), self.tensor),
+                )
+            for place in range(rank.bit_length(), self.dp_bits):
+                self.h_copy(n, half, rank, place).start()
+
+    def end_line(self, i):
+        self.own(i).wait()
+
+    def close(self):
+        for rank in range(1 << self.dp_bits):
+            for n in range(len(self.hyper)):
                 for half in (0, 1):
-                    if rank:
-                        wait_part(
-                            specs[hyper[n]].half(
-                                outs[hyper[n]], masked(dp, order[half], rank), half
-                            ),
-                            h_recv.at[n, half, rank],
-                            h_send.at[n, half, 0, 0],
-                            (flip(dp, 0), tensor),
-                        )
-                    for place in range(top, dp_bits):
-                        h_copy(n, half, rank, place).start()
-        for rank in range(1 << dp_bits):
-            for n in range(len(hyper)):
-                for half in (0, 1):
-                    for place in range(rank.bit_length(), dp_bits):
-                        h_copy(n, half, rank, place).wait_send()
-    for i in range(count):
-        for block in range(tensor_size):
-            for way in (0, 1):
-                sent = can[way] & ((block <= tensor) if way == 0 else (block >= tensor))
-
-                @pl.when(sent)
-                def _():
-                    z_copy(i, block, way).wait_send()
+                    for place in range(rank.bit_length(), self.dp_bits):
+                        self.h_copy(n, half, rank, place).wait_send()
+        for i in self.lines:
+            for block in range(self.tensor_size):
+                for way in (0, 1):
+                    sent = self.can[way] & (
+                        (block <= self.tensor) if way == 0 else (block >= self.tensor)
+                    )
+                    pl.when(sent)(self.z_copy(i, block, way).wait_send)
+
+
+def gather_kernel(specs, slow, dp_size, tensor_size, *refs):
+    count = len(specs)
+    run = GatherRun(
+        specs,
+        dp_size,
+        tensor_size,
+        refs[:count],
+        refs[count : 2 * count],
+        refs[2 * count : 3 * count],
+        refs[3 * count :],
+    )
+    run.greet()
+    run.begin(slow)
+    first = [i for i in run.lines if i not in slow]
+    for step in range(1, tensor_size):
+        for i in first:
+            run.line(i, step)
+    for i in first:
+        run.end_line(i)
+    for n in run.late:
+        run.hop(n, 0)
+    for i in slow:
+        run.begin_line(i)
+    ranks = 1 << run.dp_bits
+    for rank in range(1, max(ranks, tensor_size)):
+        if rank < ranks:
+            for n in range(len(run.hyper)):
+                run.hop(n, rank)
+        if rank < tensor_size:
+            for i in slow:
+                run.line(i, rank)
+    for i in slow:
+        run.end_line(i)
+    run.close()
+
+
+def gather_scratch(specs, arrays, dp_size, tensor_size):
+    count = len(specs)
+    hyper = max(1, sum(spec.half is not None for spec in specs))
+    dp_bits = dp_size.bit_length() - 1
+    return [pltpu.VMEM(array.shape, array.dtype) for array in arrays], [
+        pltpu.SemaphoreType.DMA((count,)),
+        pltpu.SemaphoreType.DMA((count, 2, tensor_size)),
+        pltpu.SemaphoreType.DMA((count, tensor_size)),
+        pltpu.SemaphoreType.DMA((hyper, 2, dp_size, max(dp_bits, 1))),
+        pltpu.SemaphoreType.DMA((hyper, 2, dp_size)),
+    ]
 
 
 def wait_part(part, recv_sem, send_sem, device):
@@ -192,82 +255,30 @@
     ).wait_recv()
 
 
-def gather(specs, arrays, dp_size, tensor_size, collective_id):
+def gather_shapes(specs, arrays):
+    return [jax.ShapeDtypeStruct(spec.shape, array.dtype) for spec, array in zip(specs, arrays)]
+
+
+def gather(specs, arrays, dp_size, tensor_size, collective_id, slow=()):
     count = len(specs)
-    hyper = max(1, sum(spec.half is not None for spec in specs))
-    dp_bits = dp_size.bit_length() - 1
+    held, sems = gather_scratch(specs, arrays, dp_size, tensor_size)
     return pl.pallas_call(
-        functools.partial(gather_kernel, specs, dp_size, tensor_size),
-        out_shape=[
-            jax.ShapeDtypeStruct(spec.shape, array.dtype) for spec, array in zip(specs, arrays)
-        ],
+        functools.partial(gather_kernel, specs, slow, dp_size, tensor_size),
+        out_shape=gather_shapes(specs, arrays),
         in_specs=[ANY] * count,
         out_specs=[ANY] * count,
-        scratch_shapes=[
-            pltpu.SemaphoreType.DMA((count,)),
-            pltpu.SemaphoreType.DMA((count, 2, tensor_size)),
-            pltpu.SemaphoreType.DMA((count, tensor_size)),
-            pltpu.SemaphoreType.DMA((hyper, 2, dp_size, max(dp_bits, 1))),
-            pltpu.SemaphoreType.DMA((hyper, 2, dp_size)),
-        ],
+        scratch_shapes=held + sems,
         compiler_params=pltpu.CompilerParams(
-            collective_id=collective_id, has_side_effects=True
+            collective_id=collective_id, has_side_effects=True, vmem_limit_bytes=VMEM_LIMIT
         ),
     )(*arrays)
 
 
-def exchange_kernel(tensor_size, source, out, own_sem, send, recv):
-    dp, tensor = lax.axis_index("dp"), lax.axis_index("tensor")
-    greet((dp, tensor, tensor_size), False, True, 0)
-    own = pltpu.make_async_copy(source.at[tensor], out.at[tensor], own_sem)
-
-    def copy(other, slot):
-        return pltpu.make_async_remote_copy(
-            src_ref=source.at[other],
-            dst_ref=out.at[slot],
-            send_sem=send.at[other],
-            recv_sem=recv.at[slot],
-            device_id=(dp, other),
-            device_id_type=MESH,
-        )
-
-    for other in range(tensor_size):
-
-        @pl.when(other != tensor)
-        def _():
-            copy(other, tensor).start()
-
-    own.start()
-    own.wait()
-    for other in range(tensor_size):
-
-        @pl.when(other != tensor)
-        def _():
-            copy(other, tensor).wait_send()
-            copy(other, other).wait_recv()
-
-
-def exchange(blocks, tensor_size, collective_id):
-    return pl.pallas_call(
-        functools.partial(exchange_kernel, tensor_size),
-        out_shape=jax.ShapeDtypeStruct(blocks.shape, blocks.dtype),
-        in_specs=[ANY],
-        out_specs=ANY,
-        scratch_shapes=[
-            pltpu.SemaphoreType.DMA,
-            pltpu.SemaphoreType.DMA((tensor_size,)),
-            pltpu.SemaphoreType.DMA((tensor_size,)),
-        ],
-        compiler_params=pltpu.CompilerParams(
-            collective_id=collective_id, has_side_effects=True
-        ),
-    )(blocks)
-
-
 class Scatter:
-    def __init__(self, shape, part, part_shape, place, cut=None, cut_shape=None):
-        self.shape, self.part, self.part_shape, self.place = shape, part, part_shape, place
-        self.cut, self.cut_shape = cut, cut_shape
+    def __init__(self, kind, shape, part, part_shape, place, cut=None, cut_shape=None):
+        self.kind, self.shape, self.part, self.part_shape = kind, shape, part, part_shape
+        self.place, self.cut = place, cut
+        self.cut_shape = part_shape if kind == "own" else cut_shape
 
 
 def add_into(total, extra):
@@ -289,142 +300,297 @@
             add_into(total.at[lead], extra.at[lead])
 
 
+class ScatterRun:
+    def __init__(self, specs, dp_size, tensor_size, sources, outs, scratch):
+        scratch = list(scratch)
+        self.specs, self.sources, self.outs = specs, sources, outs
+        self.tensor_size, self.dp_bits = tensor_size, dp_size.bit_length() - 1
+        self.total = [scratch.pop(0) for _ in specs]
+        self.landing = [[scratch.pop(0) for _ in range(self.dp_bits)] for _ in specs]
+        self.shares = [scratch.pop(0) if spec.kind != "dp" else None for spec in specs]
+        self.own_sem, self.send, self.recv, self.z_send, self.z_recv = scratch
+        self.dp, self.tensor = lax.axis_index("dp"), lax.axis_index("tensor")
+        self.order = orders(self.dp_bits, False)
+        self.units = scatter_units(specs, tensor_size)
+
+    def greet(self):
+        cuts = any(spec.kind != "dp" for spec in self.specs)
+        greet((self.dp, self.tensor, self.tensor_size), False, cuts, self.dp_bits)
+
+    def slots(self, stage):
+        return range(1 << (self.dp_bits - 1 - stage))
+
+    def part(self, unit, half, rank):
+        i, owner = self.units[unit]
+        place = masked(self.dp, self.order[half], rank)
+        return self.specs[i].part(self.sources[i], place, half, owner or 0)
+
+    def sum_at(self, unit, half, slot):
+        i, owner = self.units[unit]
+        return self.total[i].at[owner or 0, half, slot]
+
+    def own_copy(self, unit, half, slot):
+        return pltpu.make_async_copy(
+            self.part(unit, half, 2 * slot),
+            self.sum_at(unit, half, slot),
+            self.own_sem.at[unit, half, slot],
+        )
+
+    def landed(self, unit, half, stage, slot):
+        i, owner = self.units[unit]
+        return self.landing[i][stage].at[owner or 0, half, slot]
+
+    def copy(self, unit, half, stage, slot):
+        if stage == 0:
+            source = self.part(unit, half, 2 * slot + 1)
+        else:
+            source = self.sum_at(unit, half, (2 * slot + 1) << (stage - 1))
+        return pltpu.make_async_remote_copy(
+            src_ref=source,
+            dst_ref=self.landed(unit, half, stage, slot),
+            send_sem=self.send.at[unit, half, stage, slot],
+            recv_sem=self.recv.at[unit, half, stage, slot],
+            device_id=(flip(self.dp, self.order[half][stage]), self.tensor),
+            device_id_type=MESH,
+        )
+
+    def begin(self):
+        for unit in range(len(self.units)):
+            for slot in self.slots(0):
+                for half in (0, 1):
+                    self.copy(unit, half, 0, slot).start()
+                    self.own_copy(unit, half, slot).start()
+
+    def z_copy(self, unit, half, other, slot):
+        i, owner = self.units[unit]
+        spec, total = self.specs[i], self.sum_at(unit, half, 0)
+        return pltpu.make_async_remote_copy(
+            src_ref=total if spec.kind == "own" else spec.cut(total, other),
+            dst_ref=self.shares[i].at[slot, half],
+            send_sem=self.z_send.at[i, half, other],
+            recv_sem=self.z_recv.at[i, half, slot],
+            device_id=(self.dp, other),
+            device_id_type=MESH,
+        )
+
+    def others(self, unit):
+        owner = self.units[unit][1]
+        return range(self.tensor_size) if owner is None else [owner]
+
+    def step(self, unit, stage):
+        i, owner = self.units[unit]
+        spec = self.specs[i]
+        if stage < self.dp_bits:
+            for slot in sorted(self.slots(stage), key=lambda s: -(s & 1)):
+                for half in (0, 1):
+                    if stage == 0:
+                        self.own_copy(unit, half, slot).wait()
+                    self.copy(unit, half, stage, slot).wait_recv()
+                    add_into(
+                        self.sum_at(unit, half, slot << stage),
+                        self.landed(unit, half, stage, slot),
+                    )
+                    if slot & 1:
+                        self.copy(unit, half, stage + 1, slot >> 1).start()
+            return
+        for half in (0, 1):
+            total = self.sum_at(unit, half, 0)
+            if spec.kind == "dp":
+                spec.place(self.outs[i], half)[...] = total[...].astype(jnp.float32)
+                continue
+            for other in self.others(unit):
+
+                @pl.when(other != self.tensor)
+                def _():
+                    self.z_copy(unit, half, other, self.tensor).start()
+
+                @pl.when(other == self.tensor)
+                def _():
+                    mine = total if spec.kind == "own" else spec.cut(total, other)
+                    self.shares[i][other, half] = mine[...]
+
+    def steps(self):
+        count = len(self.units)
+        return [
+            (unit, turn - unit)
+            for turn in range(count + self.dp_bits)
+            for unit in range(count)
+            if 0 <= turn - unit <= self.dp_bits
+        ]
+
+    def close(self):
+        for i, spec in enumerate(self.specs):
+            if spec.kind == "dp":
+                continue
+            unit = [u for u, (at, owner) in enumerate(self.units) if at == i][0]
+            for half in (0, 1):
+                for other in range(self.tensor_size):
+
+                    @pl.when(other != self.tensor)
+                    def _():
+                        self.z_copy(unit, half, other, other).wait_recv()
+
+                summed = self.shares[i][0, half].astype(jnp.float32)
+                for other in range(1, self.tensor_size):
+                    summed = summed + self.shares[i][other, half].astype(jnp.float32)
+                spec.place(self.outs[i], half)[...] = summed
+        for unit, (i, owner) in enumerate(self.units):
+            for half in (0, 1):
+                for stage in range(self.dp_bits):
+                    for slot in self.slots(stage):
+                        self.copy(unit, half, stage, slot).wait_send()
+                if self.specs[i].kind != "dp":
+                    for other in self.others(unit):
+
+                        @pl.when(other != self.tensor)
+                        def _():
+                            self.z_copy(unit, half, other, self.tensor).wait_send()
+
+
+def scatter_units(specs, tensor_size):
+    units = []
+    for i, spec in enumerate(specs):
+        units += [(i, j) for j in range(tensor_size)] if spec.kind == "own" else [(i, None)]
+    return units
+
+
 def scatter_kernel(specs, dp_size, tensor_size, *refs):
     count = len(specs)
-    refs = list(refs)
-    sources = [refs.pop(0) for _ in specs]
-    outs = [refs.pop(0) for _ in specs]
+    run = ScatterRun(
+        specs, dp_size, tensor_size, refs[:count], refs[count : 2 * count], refs[2 * count :]
+    )
+    run.greet()
+    run.begin()
+    for unit, stage in run.steps():
+        run.step(unit, stage)
+    run.close()
+
+
+def scatter_scratch(specs, arrays, dp_size, tensor_size):
     dp_bits = dp_size.bit_length() - 1
-    total = [refs.pop(0) for _ in specs]
-    landing = [[refs.pop(0) for _ in range(dp_bits)] for _ in specs]
-    shares = [refs.pop(0) if spec.cut is not None else None for spec in specs]
-    own_sem, send, recv, z_send, z_recv = refs
-    dp, tensor = lax.axis_index("dp"), lax.axis_index("tensor")
-    cuts = any(spec.cut is not None for spec in specs)
-    greet((dp, tensor, tensor_size), False, cuts, dp_bits)
-    order = orders(dp_bits, False)
-
-    def own_copy(i, half, slot):
-        return pltpu.make_async_copy(
-            specs[i].part(sources[i], masked(dp, order[half], 2 * slot), half),
-            total[i].at[half, slot],
-            own_sem.at[i, half, slot],
-        )
-
-    def copy(i, half, stage, slot):
-        if stage == 0:
-            source = specs[i].part(sources[i], masked(dp, order[half], 2 * slot + 1), half)
-        else:
-            source = total[i].at[half, (2 * slot + 1) << (stage - 1)]
-        return pltpu.make_async_remote_copy(
-            src_ref=source,
-            dst_ref=landing[i][stage].at[half, slot],
-            send_sem=send.at[i, half, stage, slot],
-            recv_sem=recv.at[i, half, stage, slot],
-            device_id=(flip(dp, order[half][stage]), tensor),
-            device_id_type=MESH,
-        )
-
-    def slots(stage):
-        return range(1 << (dp_bits - 1 - stage))
-
-    for i in range(count):
-        for slot in slots(0):
-            for half in (0, 1):
-                copy(i, half, 0, slot).start()
-                own_copy(i, half, slot).start()
-    for stage in range(dp_bits):
-        for i in range(count):
-            for slot in sorted(slots(stage), key=lambda s: -(s & 1)):
-                for half in (0, 1):
-                    if stage == 0:
-                        own_copy(i, half, slot).wait()
-                    copy(i, half, stage, slot).wait_recv()
-                    add_into(total[i].at[half, slot << stage], landing[i][stage].at[half, slot])
-                    if slot & 1:
-                        copy(i, half, stage + 1, slot >> 1).start()
-
-    def z_copy(i, half, other, slot):
-        return pltpu.make_async_remote_copy(
-            src_ref=specs[i].cut(total[i].at[half, 0], other),
-            dst_ref=shares[i].at[slot, half],
-            send_sem=z_send.at[i, half, other],
-            recv_sem=z_recv.at[i, half, slot],
-            device_id=(dp, other),
-            device_id_type=MESH,
-        )
-
-    for i in range(count):
-        for half in (0, 1):
-            if specs[i].cut is None:
-                specs[i].place(outs[i], half)[...] = total[i][half, 0].astype(jnp.float32)
-            else:
-                for other in range(tensor_size):
-
-                    @pl.when(other != tensor)
-                    def _():
-                        z_copy(i, half, other, tensor).start()
-
-                    @pl.when(other == tensor)
-                    def _():
-                        shares[i][other, half] = specs[i].cut(total[i].at[half, 0], other)[...]
-
-    for i in range(count):
-        if specs[i].cut is None:
-            continue
-        for half in (0, 1):
-            for other in range(tensor_size):
-
-                @pl.when(other != tensor)
-                def _():
-                    z_copy(i, half, other, other).wait_recv()
-
-            summed = shares[i][0, half].astype(jnp.float32)
-            for other in range(1, tensor_size):
-                summed = summed + shares[i][other, half].astype(jnp.float32)
-            specs[i].place(outs[i], half)[...] = summed
-    for i in range(count):
-        for half in (0, 1):
-            for stage in range(dp_bits):
-                for slot in slots(stage):
-                    copy(i, half, stage, slot).wait_send()
-            if specs[i].cut is not None:
-                for other in range(tensor_size):
-
-                    @pl.when(other != tensor)
-                    def _():
-                        z_copy(i, half, other, tensor).wait_send()
+    scratch = []
+    units = len(scatter_units(specs, tensor_size))
+    pieces = [tensor_size if spec.kind == "own" else 1 for spec in specs]
+    for spec, array, count in zip(specs, arrays, pieces):
+        scratch.append(pltpu.VMEM((count, 2, dp_size // 2) + spec.part_shape, array.dtype))
+    for spec, array, count in zip(specs, arrays, pieces):
+        for stage in range(dp_bits):
+            scratch.append(
+                pltpu.VMEM((count, 2, dp_size >> (stage + 1)) + spec.part_shape, array.dtype)
+            )
+    for spec, array in zip(specs, arrays):
+        if spec.kind != "dp":
+            scratch.append(pltpu.VMEM((tensor_size, 2) + spec.cut_shape, array.dtype))
+    dma = pltpu.SemaphoreType.DMA
+    return scratch + [
+        dma((units, 2, dp_size // 2)),
+        dma((units, 2, dp_bits, dp_size // 2)),
+        dma((units, 2, dp_bits, dp_size // 2)),
+        dma((len(specs), 2, tensor_size)),
+        dma((len(specs), 2, tensor_size)),
+    ]
+
+
+def scatter_shapes(specs):
+    return [jax.ShapeDtypeStruct(spec.shape, jnp.float32) for spec in specs]
 
 
 def scatter(specs, arrays, dp_size, tensor_size, collective_id):
     count = len(specs)
-    dp_bits = dp_size.bit_length() - 1
-    scratch = []
-    for spec, array in zip(specs, arrays):
-        scratch.append(pltpu.VMEM((2, dp_size // 2) + spec.part_shape, array.dtype))
-    for spec, array in zip(specs, arrays):
-        for stage in range(dp_bits):
-            scratch.append(pltpu.VMEM((2, dp_size >> (stage + 1)) + spec.part_shape, array.dtype))
-    for spec, array in zip(specs, arrays):
-        if spec.cut is not None:
-            scratch.append(pltpu.VMEM((tensor_size, 2) + spec.cut_shape, array.dtype))
     return pl.pallas_call(
         functools.partial(scatter_kernel, specs, dp_size, tensor_size),
-        out_shape=[jax.ShapeDtypeStruct(spec.shape, jnp.float32) for spec in specs],
+        out_shape=scatter_shapes(specs),
         in_specs=[ANY] * count,
         out_specs=[VMEM] * count,
-        scratch_shapes=scratch
-        + [
-            pltpu.SemaphoreType.DMA((count, 2, dp_size // 2)),
-            pltpu.SemaphoreType.DMA((count, 2, dp_bits, dp_size // 2)),
-            pltpu.SemaphoreType.DMA((count, 2, dp_bits, dp_size // 2)),
-            pltpu.SemaphoreType.DMA((count, 2, tensor_size)),
-            pltpu.SemaphoreType.DMA((count, 2, tensor_size)),
-        ],
+        scratch_shapes=scatter_scratch(specs, arrays, dp_size, tensor_size),
         compiler_params=pltpu.CompilerParams(
             collective_id=collective_id, has_side_effects=True, vmem_limit_bytes=VMEM_LIMIT
         ),
     )(*arrays)
+
+
+class ExchangeRun:
+    def __init__(self, tensor_size, source, out, own_sem, send, recv):
+        self.tensor_size, self.source, self.out = tensor_size, source, out
+        self.own_sem, self.send, self.recv = own_sem, send, recv
+        self.dp, self.tensor = lax.axis_index("dp"), lax.axis_index("tensor")
+
+    def copy(self, other, slot):
+        return pltpu.make_async_remote_copy(
+            src_ref=self.source.at[other],
+            dst_ref=self.out.at[slot],
+            send_sem=self.send.at[other],
+            recv_sem=self.recv.at[slot],
+            device_id=(self.dp, other),
+            device_id_type=MESH,
+        )
+
+    def own(self):
+        return pltpu.make_async_copy(
+            self.source.at[self.tensor], self.out.at[self.tensor], self.own_sem
+        )
+
+    def begin(self):
+        for other in range(self.tensor_size):
+            pl.when(other != self.tensor)(self.copy(other, self.tensor).start)
+        self.own().start()
+
+    def close(self):
+        self.own().wait()
+        for other in range(self.tensor_size):
+
+            @pl.when(other != self.tensor)
+            def _():
+                self.copy(other, self.tensor).wait_send()
+                self.copy(other, other).wait_recv()
+
+
+def exchange_kernel(specs, dp_size, tensor_size, *refs):
+    count = len(specs)
+    run = ScatterRun(
+        specs,
+        dp_size,
+        tensor_size,
+        refs[1 : count + 1],
+        refs[count + 2 : 2 * count + 2],
+        refs[2 * count + 6 :],
+    )
+    blocks, summed = refs[0], refs[count + 1]
+    landing = refs[2 * count + 2]
+    exchange_run = ExchangeRun(tensor_size, blocks, landing, *refs[2 * count + 3 : 2 * count + 6])
+    greet((run.dp, run.tensor, tensor_size), False, True, run.dp_bits)
+    exchange_run.begin()
+    run.begin()
+    for unit, stage in run.steps():
+        run.step(unit, stage)
+    exchange_run.close()
+    total = landing[0].astype(jnp.float32)
+    for other in range(1, tensor_size):
+        total = total + landing[other].astype(jnp.float32)
+    summed[...] = total
+    run.close()
+
+
+def exchange(blocks, specs, arrays, sizes, collective_id):
+    dp_size, tensor_size = sizes
+    count = len(specs)
+    dma = pltpu.SemaphoreType.DMA
+    return pl.pallas_call(
+        functools.partial(exchange_kernel, specs, dp_size, tensor_size),
+        out_shape=[jax.ShapeDtypeStruct(blocks.shape[1:], jnp.float32)] + scatter_shapes(specs),
+        in_specs=[ANY] * (count + 1),
+        out_specs=[VMEM] * (count + 1),
+        scratch_shapes=[
+            pltpu.VMEM(blocks.shape, blocks.dtype),
+            dma,
+            dma((tensor_size,)),
+            dma((tensor_size,)),
+        ]
+        + scatter_scratch(specs, arrays, dp_size, tensor_size),
+        compiler_params=pltpu.CompilerParams(
+            collective_id=collective_id, has_side_effects=True, vmem_limit_bytes=VMEM_LIMIT
+        ),
+    )(blocks, *arrays)
 
 
 def lanes_of(shape):
@@ -452,13 +618,47 @@
     return key_at <= query_at
 
 
-def attend_kernel(
-    group_pairs, q_ref, cos_ref, sin_ref, k_ref, v_ref, o_ref, q_out, lse_ref, k_left, v_turned
-):
+def at_steps(actions, step, steps):
+    places = [(min(steps - 1, int(time * steps)), action) for time, action in actions]
+    for place in sorted({place for place, _ in places}):
+
+        @pl.when(step == place)
+        def _():
+            for at, action in places:
+                if at == place:
+                    action()
+
+
+def gather_plan(run):
+    plan = [(0.0, run.greet), (0.0, run.begin)]
+    for rank in range(1, 1 << run.dp_bits):
+        if rank >> (run.dp_bits - 1):
+            time = 1.0
+        else:
+            time = 0.45 + 0.35 * (rank.bit_count() - 1) / max(1, run.dp_bits - 2)
+        plan += [(time, functools.partial(run.hop, n, rank)) for n in range(len(run.hyper))]
+    for step in range(1, run.tensor_size):
+        time = 0.95 * step / (run.tensor_size - 1)
+        plan += [(time, functools.partial(run.line, i, step)) for i in run.lines]
+    plan += [(1.0, functools.partial(run.end_line, i)) for i in run.lines]
+    return sorted(plan, key=lambda entry: entry[0]) + [(1.0, run.close)]
+
+
+def attend_kernel(group_pairs, pairs, specs, dp_size, tensor_size, *refs):
+    count = len(specs)
+    refs = list(refs)
+    q_ref, cos_ref, sin_ref, k_ref, v_ref = (refs.pop(0) for _ in range(5))
+    sources = [refs.pop(0) for _ in specs]
+    o_ref, q_out, lse_ref = (refs.pop(0) for _ in range(3))
+    outs = [refs.pop(0) for _ in specs]
+    k_left, v_turned = (refs.pop(0) for _ in range(2))
+    run = GatherRun(specs, dp_size, tensor_size, sources, outs, refs[:count], refs[count:])
     pair = pl.program_id(0)
     group = pair // group_pairs
     rows = q_ref.shape[0]
     start = lax.axis_index("tensor") * rows
+    plan = gather_plan(run)
+    at_steps([entry for entry in plan if entry[0] < 1.0], pair, pairs)
 
     @pl.when(pair % group_pairs == 0)
     def _():
@@ -485,60 +685,71 @@
         contexts.append(context * (1.0 / summed))
         lse_ref[0, head, :] = (top + jnp.log(summed))[0]
     o_ref[...] = jnp.concatenate(contexts, axis=0).T.astype(jnp.bfloat16)
-
-
-def attend(q_pre, cosines, sines, keys_values, head_count, group_heads):
+    at_steps([entry for entry in plan if entry[0] >= 1.0], pair, pairs)
+
+
+def attend(
+    q_pre, cosines, sines, keys_values, head_count, group_heads, specs, arrays, sizes, collective_id
+):
     rows, width = q_pre.shape
     length, both = keys_values.shape
     pairs, group_pairs = head_count // 2, group_heads // 2
     kv_blocks = both // 256
     wide = pl.BlockSpec((rows, 128), lambda p: (0, p))
     table = pl.BlockSpec((rows, 128), lambda p: (0, 0))
+    held, sems = gather_scratch(specs, arrays, *sizes)
     return pl.pallas_call(
-        functools.partial(attend_kernel, group_pairs),
+        functools.partial(attend_kernel, group_pairs, pairs, specs, *sizes),
         grid=(pairs,),
         out_shape=[
             jax.ShapeDtypeStruct((rows, width), jnp.bfloat16),
             jax.ShapeDtypeStruct((rows, width), jnp.bfloat16),
             jax.ShapeDtypeStruct((pairs, 2, rows), jnp.float32),
-        ],
+        ]
+        + gather_shapes(specs, arrays),
         in_specs=[
             wide,
             table,
             table,
             pl.BlockSpec((length, 128), lambda p: (0, p // group_pairs // 2)),
             pl.BlockSpec((length, 128), lambda p: (0, kv_blocks + p // group_pairs // 2)),
-        ],
-        out_specs=[wide, wide, pl.BlockSpec((1, 2, rows), lambda p: (p, 0, 0))],
+        ]
+        + [ANY] * len(specs),
+        out_specs=[wide, wide, pl.BlockSpec((1, 2, rows), lambda p: (p, 0, 0))]
+        + [ANY] * len(specs),
         scratch_shapes=[
             pltpu.VMEM((length, 128), jnp.bfloat16),
             pltpu.VMEM((HEAD_DIM, length), jnp.bfloat16),
-        ],
-        compiler_params=pltpu.CompilerParams(vmem_limit_bytes=VMEM_LIMIT),
+        ]
+        + held
+        + sems,
+        compiler_params=pltpu.CompilerParams(
+            collective_id=collective_id, has_side_effects=True, vmem_limit_bytes=VMEM_LIMIT
+        ),
         cost_estimate=pl.CostEstimate(
             flops=4 * rows * length * width, bytes_accessed=8 * rows * width, transcendentals=0
         ),
-    )(q_pre, cosines, sines, keys_values, keys_values)
-
-
-def attend_back_kernel(
-    group_pairs,
-    q_ref,
-    do_ref,
-    lse_ref,
-    cos_ref,
-    sin_ref,
-    k_ref,
-    v_ref,
-    dq_ref,
-    dk_ref,
-    dv_ref,
-    k_left,
-    v_left,
-    k_turned,
-    dk_sum,
-    dv_sum,
-):
+    )(q_pre, cosines, sines, keys_values, keys_values, *arrays)
+
+
+def scatter_plan(run):
+    plan = [(0.0, run.greet), (0.0, run.begin)]
+    for unit, stage in run.steps():
+        time = 0.15 + 0.1 * unit if stage == 0 else 0.55 + 0.35 * unit if stage == 1 else 1.0
+        plan.append((min(time, 1.0), functools.partial(run.step, unit, stage)))
+    return plan + [(1.0, run.close)]
+
+
+def attend_back_kernel(group_pairs, pairs, specs, dp_size, tensor_size, *refs):
+    refs = list(refs)
+    q_ref, do_ref, lse_ref, cos_ref, sin_ref, k_ref, v_ref = (refs.pop(0) for _ in range(7))
+    sources = [refs.pop(0) for _ in specs]
+    dq_ref, dk_ref, dv_ref = (refs.pop(0) for _ in range(3))
+    outs = [refs.pop(0) for _ in specs]
+    k_left, v_left, k_turned, dk_sum, dv_sum = (refs.pop(0) for _ in range(5))
+    run = ScatterRun(specs, dp_size, tensor_size, sources, outs, refs)
+    plan = scatter_plan(run)
+    at_steps([entry for entry in plan if entry[0] < 1.0], pl.program_id(0), pairs)
     pair = pl.program_id(0)
     group = pair // group_pairs
     odd = group % 2 == 1
@@ -589,9 +800,23 @@
                 out[...] = jnp.where(
                     left, out[...].astype(jnp.float32), pltpu.roll(value, HEAD_DIM, 1)
                 ).astype(out.dtype)
-
-
-def attend_back(queries, grad_context, lse, cosines, sines, keys_values, head_count, group_heads):
+    at_steps([entry for entry in plan if entry[0] >= 1.0], pair, pairs)
+
+
+def attend_back(
+    queries,
+    grad_context,
+    lse,
+    cosines,
+    sines,
+    keys_values,
+    head_count,
+    group_heads,
+    specs,
+    arrays,
+    sizes,
+    collective_id,
+):
     rows, width = queries.shape
     length, both = keys_values.shape
     pairs, group_pairs = head_count // 2, group_heads // 2
@@ -600,13 +825,14 @@
     table = pl.BlockSpec((rows, 128), lambda p: (0, 0))
     kv_out = pl.BlockSpec((length, 128), lambda p: (0, p // group_pairs // 2))
     return pl.pallas_call(
-        functools.partial(attend_back_kernel, group_pairs),
+        functools.partial(attend_back_kernel, group_pairs, pairs, specs, *sizes),
         grid=(pairs,),
         out_shape=[
             jax.ShapeDtypeStruct((rows, width), jnp.bfloat16),
             jax.ShapeDtypeStruct((length, both // 2), jnp.bfloat16),
             jax.ShapeDtypeStruct((length, both // 2), jnp.bfloat16),
-        ],
+        ]
+        + scatter_shapes(specs),
         in_specs=[
             wide,
             wide,
@@ -615,20 +841,24 @@
             table,
             pl.BlockSpec((length, 128), lambda p: (0, p // group_pairs // 2)),
             pl.BlockSpec((length, 128), lambda p: (0, kv_blocks + p // group_pairs // 2)),
-        ],
-        out_specs=[wide, kv_out, kv_out],
+        ]
+        + [ANY] * len(specs),
+        out_specs=[wide, kv_out, kv_out] + [VMEM] * len(specs),
         scratch_shapes=[
             pltpu.VMEM((length, 128), jnp.bfloat16),
             pltpu.VMEM((length, 128), jnp.bfloat16),
             pltpu.VMEM((HEAD_DIM, length), jnp.bfloat16),
             pltpu.VMEM((length, 128), jnp.float32),
             pltpu.VMEM((length, 128), jnp.float32),
-        ],
-        compiler_params=pltpu.CompilerParams(vmem_limit_bytes=VMEM_LIMIT),
+        ]
+        + scatter_scratch(specs, arrays, *sizes),
+        compiler_params=pltpu.CompilerParams(
+            collective_id=collective_id, has_side_effects=True, vmem_limit_bytes=VMEM_LIMIT
+        ),
         cost_estimate=pl.CostEstimate(
             flops=10 * rows * length * width, bytes_accessed=8 * rows * width, transcendentals=0
         ),
-    )(queries, grad_context, lse, cosines, sines, keys_values, keys_values)
+    )(queries, grad_context, lse, cosines, sines, keys_values, keys_values, *arrays)
 
 
 def block_at(place, tensor, tensor_size):
@@ -644,7 +874,8 @@
 def mlp_kernel(
     tensor_size,
     normed_ref,
-    cot_ref,
+    cot_low_ref,
+    cot_high_ref,
     gate_ref,
     up_ref,
     down_ref,
@@ -683,7 +914,8 @@
                 (gate_ref, gate),
                 (up_ref, up),
                 (down_ref, down),
-                (cot_ref, cot),
+                (cot_low_ref, cot.at[:, : cot_low_ref.shape[1]]),
+                (cot_high_ref, cot.at[:, cot_low_ref.shape[1] :]),
             )
         )
     ]
@@ -844,7 +1076,7 @@
             pl.when(sent)(n_copy(other, way).wait_send)
 
 
-def feed_forward(normed, cot_all, gate, up, down, tensor_size, collective_id):
+def feed_forward(normed, cot_low, cot_high, gate, up, down, tensor_size, collective_id):
     rows, width = normed.shape
     units = gate.shape[1]
     low = jnp.bfloat16
@@ -860,7 +1092,7 @@
             jax.ShapeDtypeStruct(up.shape, low),
             jax.ShapeDtypeStruct(down.shape, low),
         ],
-        in_specs=[ANY] * 5,
+        in_specs=[ANY] * 6,
         out_specs=[VMEM] + [ANY] * 4,
         scratch_shapes=[
             pltpu.VMEM(tokens, low),
@@ -874,7 +1106,7 @@
             pltpu.VMEM((2, rows, width), low),
             pltpu.VMEM(tokens, low),
             pltpu.VMEM(tokens, low),
-            dma((5,)),
+            dma((6,)),
             dma((2, tensor_size)),
             dma((tensor_size,)),
             dma((2,)),
@@ -890,7 +1122,14 @@
             bytes_accessed=8 * width * units,
             transcendentals=0,
         ),
-    )(normed, cot_all.reshape(tokens), gate, up, down)
+    )(
+        normed,
+        cot_low.reshape(tensor_size, -1, width),
+        cot_high.reshape(tensor_size, -1, width),
+        gate,
+        up,
+        down,
+    )
 
 
 def rope_tables(rows, tensor):
@@ -947,12 +1186,6 @@
     key_value = jnp.concatenate([w_key, w_value], axis=1)
     gains = jnp.zeros((16, 128), jnp.bfloat16)
     gains = gains.at[0, :gain_part].set(attn_gain).at[1, :gain_part].set(mlp_gain)
-    gate_full, up_full, down_full = (
-        lax.all_gather(w_gate, "dp", axis=0, tiled=True),
-        lax.all_gather(w_up, "dp", axis=0, tiled=True),
-        lax.all_gather(w_down, "dp", axis=1, tiled=True),
-    )
-    cot_all = lax.all_gather(cotangent, "tensor", axis=0, tiled=True)
     query_spec = Gather(
         (width, heads * HEAD_DIM),
         lambda ref, dp, t: ref.at[
@@ -999,9 +1232,38 @@
         (tensor_size * shape[0], shape[1]),
         lambda ref, dp, t: ref.at[pl.ds(start_row(t, shape[0]), shape[0]), :],
     )
-    query_full, key_value_full, gains_full = call(
-        [query_spec, kv_spec, gain_spec], [w_query, key_value, gains], collective_id=1
-    )
+    up_rows, units = w_gate.shape
+    column_spec = Gather(
+        (width, units),
+        lambda ref, dp, t: ref.at[pl.ds(start_row(dp, up_rows), up_rows), :],
+        lambda ref, dp, half: ref.at[
+            pl.ds(
+                pl.multiple_of(dp * up_rows + half * (up_rows // 2), up_rows // 2), up_rows // 2
+            ),
+            :,
+        ],
+        False,
+    )
+    down_cols = w_down.shape[1]
+    down_spec = Gather(
+        (units, width),
+        lambda ref, dp, t: ref.at[:, pl.ds(start_row(dp, down_cols), down_cols)],
+        lambda ref, dp, half: ref.at[
+            pl.ds(half * (units // 2), units // 2), pl.ds(start_row(dp, down_cols), down_cols)
+        ],
+        False,
+    )
+    low_rows = rows // 4 * 3
+    cot_low_spec, cot_high_spec = row_spec((low_rows, width)), row_spec((rows - low_rows, width))
+    sizes = (dp_size, tensor_size)
+    query_full, key_value_full, gains_full, gate_full, cot_low = call(
+        [query_spec, kv_spec, gain_spec, column_spec, cot_low_spec],
+        [w_query, key_value, gains, w_gate, cotangent[:low_rows]],
+        collective_id=1,
+        slow=(4,),
+    )
+    down_late, query_full = lax.optimization_barrier((w_down, query_full))
+    down_full = lax.all_gather(down_late, "dp", axis=1, tiled=True)
     gains_full = gains_full.reshape(-1, 16, 128)[:, :2, :gain_part].astype(jnp.float32)
     gain_first = gains_full[:, 0].reshape(width)
     gain_second = gains_full[:, 1].reshape(width)
@@ -1017,26 +1279,28 @@
     ).astype(jnp.bfloat16)
     query_pre = product(normed_first, query_full)
     kv_all, out_full = call([row_spec(kv_own.shape), out_spec], [kv_own, w_out], collective_id=2)
-    context, queries, log_sums = attend(
-        query_pre, cosines, sines, kv_all, heads, group_heads
+    context, queries, log_sums, up_full, cot_high = attend(
+        query_pre,
+        cosines,
+        sines,
+        kv_all,
+        heads,
+        group_heads,
+        [column_spec, cot_high_spec],
+        [w_up, cotangent[low_rows:]],
+        sizes,
+        8,
     )
     middle = residual + product(context, out_full)
     scale_second = lax.rsqrt(jnp.mean(middle * middle, axis=-1, keepdims=True) + epsilon)
     unit_second = middle * scale_second
     normed_own = (unit_second * gain_second).astype(jnp.bfloat16)
     back_second, mlp_part, grad_gate_w, grad_up_w, grad_down_w = feed_forward(
-        normed_own, cot_all, gate_full, up_full, down_full, tensor_size, 3
+        normed_own, cot_low, cot_high, gate_full, up_full, down_full, tensor_size, 3
     )
     mlp_rows = lax.psum_scatter(
         mlp_part.reshape(tensor_size * rows, width), "tensor", scatter_dimension=0, tiled=True
-    ).astype(jnp.float32)
-    output = (middle + mlp_rows).astype(jnp.bfloat16)
-    sum_gate, sum_up, sum_down = (
-        lax.psum_scatter(grad_gate_w, "dp", scatter_dimension=0, tiled=True).astype(jnp.float32),
-        lax.psum_scatter(grad_up_w, "dp", scatter_dimension=0, tiled=True).astype(jnp.float32),
-        lax.psum_scatter(grad_down_w, "dp", scatter_dimension=1, tiled=True).astype(jnp.float32),
-    )
-
+    )
     grad_gain_second = jnp.sum(back_second * unit_second, axis=0)
     grad_middle = cotangent.astype(jnp.float32) + norm_back(
         back_second, unit_second, scale_second, gain_second
@@ -1044,12 +1308,84 @@
     middle_low = grad_middle.astype(jnp.bfloat16)
     grad_context = product_right(middle_low, out_full).astype(jnp.bfloat16)
     grad_out_w = product_left(context, middle_low).astype(jnp.bfloat16)
-    grad_queries, grad_keys, grad_values = attend_back(
-        queries, grad_context, log_sums, cosines, sines, kv_all, heads, group_heads
+    query_scatter = Scatter(
+        "own",
+        (q_rows, q_cols),
+        lambda ref, dp, half, j: ref.at[
+            pl.ds(pl.multiple_of(dp * q_rows + half * (q_rows // 2), q_rows // 2), q_rows // 2),
+            pl.ds(j * q_cols, q_cols),
+        ],
+        (q_rows // 2, q_cols),
+        lambda ref, half: ref.at[pl.ds(half * (q_rows // 2), q_rows // 2), :],
+    )
+    kv_scatter = Scatter(
+        "cut",
+        (kv_rows, 2 * kv_width),
+        lambda ref, dp, half, j: ref.at[
+            pl.ds(dp * tensor_size, tensor_size), :, pl.ds(half * kv_width, kv_width)
+        ],
+        (tensor_size, kv_rows, kv_width),
+        lambda ref, half: ref.at[:, pl.ds(half * kv_width, kv_width)],
+        lambda ref, j: ref.at[j],
+        (kv_rows, kv_width),
+    )
+    out_scatter = Scatter(
+        "own",
+        (o_rows, o_cols),
+        lambda ref, dp, half, j: ref.at[
+            pl.ds(j * o_rows + half * (o_rows // 2), o_rows // 2),
+            pl.ds(start_row(dp, o_cols), o_cols),
+        ],
+        (o_rows // 2, o_cols),
+        lambda ref, half: ref.at[pl.ds(half * (o_rows // 2), o_rows // 2), :],
+    )
+    gain_scatter = Scatter(
+        "cut",
+        (16, 128),
+        lambda ref, dp, half, j: ref.at[
+            pl.ds(dp * tensor_size, tensor_size), pl.ds(half * 8, 8), :
+        ],
+        (tensor_size, 8, 128),
+        lambda ref, half: ref.at[pl.ds(half * 8, 8), :],
+        lambda ref, j: ref.at[j],
+        (8, 128),
+    )
+    column_scatter = Scatter(
+        "dp",
+        (up_rows, units),
+        lambda ref, dp, half, j: column_spec.half(ref, dp, half),
+        (up_rows // 2, units),
+        lambda ref, half: ref.at[pl.ds(half * (up_rows // 2), up_rows // 2), :],
+    )
+    down_scatter = Scatter(
+        "dp",
+        (units, down_cols),
+        lambda ref, dp, half, j: down_spec.half(ref, dp, half),
+        (units // 2, down_cols),
+        lambda ref, half: ref.at[pl.ds(half * (units // 2), units // 2), :],
+    )
+    grad_queries, grad_keys, grad_values, sum_gate, sum_up = attend_back(
+        queries,
+        grad_context,
+        log_sums,
+        cosines,
+        sines,
+        kv_all,
+        heads,
+        group_heads,
+        [column_scatter, column_scatter],
+        [grad_gate_w, grad_up_w],
+        sizes,
+        7,
     )
     grad_kv = jnp.concatenate([grad_keys, grad_values], axis=1)
-    kv_blocks = exchange(grad_kv.reshape(tensor_size, rows, 2 * kv_width), tensor_size, 5)
-    grad_kv_own = jnp.sum(kv_blocks.astype(jnp.float32), axis=0)
+    grad_kv_own, sum_out, sum_down = exchange(
+        grad_kv.reshape(tensor_size, rows, 2 * kv_width),
+        [out_scatter, down_scatter],
+        [grad_out_w, grad_down_w],
+        sizes,
+        5,
+    )
     grad_kv_own = jnp.concatenate(
         [turn_heads(grad_kv_own[:, :kv_width], cosines, -sines), grad_kv_own[:, kv_width:]], axis=1
     ).astype(jnp.bfloat16)
@@ -1064,48 +1400,9 @@
     grad_gains = jnp.zeros((dp_size * tensor_size, 16, 128), jnp.float32)
     grad_gains = grad_gains.at[:, 0, :gain_part].set(grad_gain_first.reshape(-1, gain_part))
     grad_gains = grad_gains.at[:, 8, :gain_part].set(grad_gain_second.reshape(-1, gain_part))
-    query_scatter = Scatter(
-        (q_rows, q_cols),
-        query_spec.half,
-        (q_rows // 2, tensor_size * q_cols),
-        lambda ref, half: ref.at[pl.ds(half * (q_rows // 2), q_rows // 2), :],
-        lambda ref, j: ref.at[:, pl.ds(j * q_cols, q_cols)],
-        (q_rows // 2, q_cols),
-    )
-    kv_scatter = Scatter(
-        (kv_rows, 2 * kv_width),
-        lambda ref, dp, half: ref.at[
-            pl.ds(dp * tensor_size, tensor_size), :, pl.ds(half * kv_width, kv_width)
-        ],
-        (tensor_size, kv_rows, kv_width),
-        lambda ref, half: ref.at[:, pl.ds(half * kv_width, kv_width)],
-        lambda ref, j: ref.at[j],
-        (kv_rows, kv_width),
-    )
-    out_scatter = Scatter(
-        (o_rows, o_cols),
-        lambda ref, dp, half: ref.at[
-            :, pl.ds(half * (o_rows // 2), o_rows // 2), pl.ds(start_row(dp, o_cols), o_cols)
-        ],
-        (tensor_size, o_rows // 2, o_cols),
-        lambda ref, half: ref.at[pl.ds(half * (o_rows // 2), o_rows // 2), :],
-        lambda ref, j: ref.at[j],
-        (o_rows // 2, o_cols),
-    )
-    gain_scatter = Scatter(
-        (16, 128),
-        lambda ref, dp, half: ref.at[
-            pl.ds(dp * tensor_size, tensor_size), pl.ds(half * 8, 8), :
-        ],
-        (tensor_size, 8, 128),
-        lambda ref, half: ref.at[pl.ds(half * 8, 8), :],
-        lambda ref, j: ref.at[j],
-        (8, 128),
-    )
-    sum_out, sum_query, sum_kv, sum_gains = scatter(
-        [out_scatter, query_scatter, kv_scatter, gain_scatter],
+    sum_query, sum_kv, sum_gains = scatter(
+        [query_scatter, kv_scatter, gain_scatter],
         [
-            grad_out_w.reshape(tensor_size, o_rows, width),
             grad_query_w,
             grad_kv_w.reshape(dp_size * tensor_size, kv_rows, 2 * kv_width),
             grad_gains,
@@ -1114,6 +1411,8 @@
         tensor_size,
         6,
     )
+    middle, mlp_rows, sum_query = lax.optimization_barrier((middle, mlp_rows, sum_query))
+    output = (middle + mlp_rows.astype(jnp.float32)).astype(jnp.bfloat16)
     return (
         output,
         grad_tokens,

time: 816 us -> 690 us (0.85)
  waiting for transfers between devices: 75.6 us -> 0.04 us
  Pallas kernels: 622 us -> 575 us
  local copies, waits for them, and re-layouts: 16.8 us -> 27.6 us
  other arithmetic: 27 us -> 16.8 us
    pallas_call x1, Pallas kernels: 167 us -> 75.2 us  [scatter(): pl.pallas_call(functools.partial(scatter_kernel, specs, dp_size, tensor_s...]
    reduce_scatter x1, waiting for transfers between devices: 71.5 us -> 0.01 us  [on_device(): lax.psum_scatter(mlp_part.reshape(tensor_size * rows, width), 'tensor', s...]
    pallas_call x5, Pallas kernels: 300 us -> 352 us  [the longest x2 159 us: gather(): pl.pallas_call(functools.partial(gather_kernel, specs, slow, dp_size, ten...]
  transfers between devices with their start and end apart: 8 -> 2, of which waited for: 1 -> 0; matrix products, arithmetic and copies ran while one was open for 11% -> 11% of each run, Pallas kernels for 58% -> 50%
where the time goes in v3:
time: 690 us; the launch traced here: 680 us
  Pallas kernels  575 us (83%)
  matrix products  46.1 us (7%)
  local copies, waits for them, and re-layouts  27.6 us (4%)
  other arithmetic  16.8 us (2%)
  between operations  14.6 us (2%)
    pallas_call x2, Pallas kernels, gather(): pl.pallas_call(functools.partial(gather_kernel, specs, slow, dp_size, ten...  159 us
    pallas_call x1, Pallas kernels, feed_forward(): pl.pallas_call(functools.partial(mlp_kernel, tensor_size), out_shape=[jax...  148 us
    pallas_call x1, Pallas kernels, exchange(): pl.pallas_call(functools.partial(exchange_kernel, specs, dp_size, tensor_...  88.3 us
    pallas_call x1, Pallas kernels, scatter(): pl.pallas_call(functools.partial(scatter_kernel, specs, dp_size, tensor_s...  75.2 us
    pallas_call x1, Pallas kernels, attend_back(): pl.pallas_call(functools.partial(attend_back_kernel, group_pairs, pairs,...  62.2 us
    pallas_call x1, Pallas kernels, attend(): pl.pallas_call(functools.partial(attend_kernel, group_pairs, pairs, specs...  42 us
    dot_general x3, matrix products, product_right(): lax.dot_general(left, right, (((1,), (1,)), ((), ())), preferred_element_...  15.9 us
    dot_general x3, matrix products, product(): return jnp.dot(left, right, preferred_element_type=jnp.float32)  15.6 us
  transfers between devices with their start and end apart: 2, of which 0 were waited for; matrix products, arithmetic and copies ran while one was open for 11% of the time, Pallas kernels for 50%

profile of v3, /device:TPU:25, one launch (start us, length us, event | category | flops | bytes accessed | tf_op | source)
XLA Modules:
  0.0 680.2 jit_solution(9401471946470872676)
XLA Ops:
  7.2 2.2 slice.125.refs_4_
  9.4 1.4 pad_maximum_fusion.7.refs_1_
  10.8 0.7 scatter.14
  11.5 0.8 scatter.15.refs_2_
  12.3 0.6 copy-done.21
  12.8 85.0 %shard_map.194 = (bf16[2048,2048]{1,0:T(8,128)(2,1)}, bf16[2048,512]{1,0:T(8,128)(2,1)}, bf16[512,128]{1,0:T(8,128)(2,1)}, bf16[2048,1408]{1,0:T(8,128)(2,1)}, bf16[768,2048]{1,0:T(8,128)(2,1)}) custom-call(bf16[256,512]{1,0:T(8,128)(2,1)} %refs_0_.1, bf16[64,512]{1,0:T(8,128)(2,1)} %pad_maximum_fusion.7.refs_1_, bf16[16,128]{1,0:T(8,128)(2,1)} %copy-done.21, ...), custom_call_target="tpu_custom_call" | custom-call | tf_op jit(solution)/shard_map/pallas_call | solution.py:265
  98.0 0.9 slice_convert_fusion.2
  99.3 2.3 fusion.22
  101.7 1.7 slice.130.refs_6_
  104.9 0.7 pad_maximum_fusion.1.refs_0_
  105.6 74.4 %shard_map.195 = (bf16[1024,512]{1,0:T(8,128)(2,1)}, bf16[2048,2048]{1,0:T(8,128)(2,1)}) custom-call(bf16[256,512]{1,0:T(8,128)(2,1)} %pad_maximum_fusion.1.refs_0_, bf16[512,256]{1,0:T(8,128)(2,1)} %refs_1_.1), custom_call_target="tpu_custom_call" | custom-call | tf_op jit(solution)/shard_map/pallas_call | solution.py:265
  180.0 7.1 %fusion.24.refs_0_ = f32[256,2048]{1,0:T(8,128)} fusion(bf16[2048,2048]{1,0:T(8,128)(2,1)} %get-tuple-element.94, bf16[256,2048]{1,0:T(8,128)(2,1)S(1)} %copy-done, f32[2048]{0:T(1024)S(1)} %mul.134, f32[256]{0:T(256)S(1)} %add_rsqrt_fusion.1), kind=kOutput, calls=%fused_computation.60 | convolution fusion | flops 2149580800 | bytes 11543552 | tf_op jit(solution)/shard_map/dot_general | solution.py:22
  187.1 42.0 %shard_map.196 = (bf16[256,2048]{1,0:T(8,128)(2,1)}, bf16[256,2048]{1,0:T(8,128)(2,1)}, f32[16,2,256]{2,1,0:T(2,128)}, bf16[2048,1408]{1,0:T(8,128)(2,1)}, bf16[256,2048]{1,0:T(8,128)(2,1)}) custom-call(f32[256,2048]{1,0:T(8,128)} %fusion.24.refs_0_, f32[256,128]{1,0:T(8,128)} %copy-done.17, f32[256,128]{1,0:T(8,128)} %copy-done.16, ...), custom_call_target="tpu_custom_call" | custom-call | flops 2147483648 | bytes 4194304 | tf_op jit(solution)/shard_map/pallas_call | solution.py:701
  229.1 6.2 multiply_reduce_fusion.2
  235.9 1.2 multiply_convert_fusion.normed_ref
  237.1 147.8 %shard_map.197 = (f32[256,2048]{1,0:T(8,128)}, bf16[4,256,2048]{2,1,0:T(8,128)(2,1)}, bf16[2048,1408]{1,0:T(8,128)(2,1)}, bf16[2048,1408]{1,0:T(8,128)(2,1)}, bf16[1408,2048]{1,0:T(8,128)(2,1)}) custom-call(bf16[256,2048]{1,0:T(8,128)(2,1)} %multiply_convert_fusion.normed_ref, bf16[4,192,2048]{2,1,0:T(8,128)(2,1)} %bitcast.62, ...), custom_call_target="tpu_custom_call" | custom-call | flops 53150220288 | bytes 23068672 | tf_op jit(solution)/shard_map/pallas_call | solution.py:1086
  385.0 2.9 multiply_reduce_fusion
  387.9 0.6 multiply_add_fusion
  388.5 7.5 %convolution_convert_fusion.3.refs_1_ = bf16[256,2048]{1,0:T(8,128)(2,1)} fusion(bf16[2048,2048]{1,0:T(8,128)(2,1)} %get-tuple-element.98, f32[256,2048]{1,0:T(8,128)S(1)} %multiply_add_fusion), kind=kOutput, calls=%fused_computation.11 | convolution fusion | flops 2148532224 | bytes 11534336 | tf_op jit(solution)/shard_map/dot_general | solution.py:32
  396.0 62.2 %shard_map.198 = (bf16[256,2048]{1,0:T(8,128)(2,1)}, bf16[1024,256]{1,0:T(8,128)(2,1)}, bf16[1024,256]{1,0:T(8,128)(2,1)}, f32[256,1408]{1,0:T(8,128)}, f32[256,1408]{1,0:T(8,128)}) custom-call(bf16[256,2048]{1,0:T(8,128)(2,1)} %get-tuple-element.105.refs_0_, bf16[256,2048]{1,0:T(8,128)(2,1)} %convolution_convert_fusion.3.refs_1_, ...), custom_call_target="tpu_custom_call" | custom-call | flops 5368709120 | bytes 4194304 | tf_op jit(solution)/shard_map/pallas_call | solution.py:827
  458.2 2.3 pad_maximum_fusion
  460.5 5.6 convolution_convert_fusion.refs_1_
  466.2 88.3 %shard_map.199 = (f32[256,512]{1,0:T(8,128)}, f32[512,256]{1,0:T(8,128)}, f32[1408,256]{1,0:T(8,128)}) custom-call(bf16[4,256,512]{2,1,0:T(8,128)(2,1)} %bitcast.49, bf16[2048,2048]{1,0:T(8,128)(2,1)} %convolution_convert_fusion.refs_1_, bf16[1408,2048]{1,0:T(8,128)(2,1)} %get-tuple-element.113.refs_2_), custom_call_target="tpu_custom_call" | custom-call | tf_op jit(solution)/shard_map/pallas_call | solution.py:578
  554.5 1.7 slice.132
  556.2 1.6 slice.153
  557.8 1.8 copy.29
  559.6 1.7 rev.7
  561.2 1.8 copy.30
  563.1 1.1 fusion.14
  564.3 6.2 fusion.28
  570.5 2.2 fusion.6
  572.8 0.7 reshape.304
  573.5 0.7 reshape.305
  574.1 0.7 scatter.16
  574.9 1.2 scatter.19.refs_2_
  576.1 3.2 convolution_convert_fusion.2
  579.3 5.7 convolution_convert_fusion.1.refs_0_
  585.1 75.2 %shard_map.200 = (f32[256,512]{1,0:T(8,128)}, f32[64,512]{1,0:T(8,128)}, f32[16,128]{1,0:T(8,128)}) custom-call(bf16[2048,2048]{1,0:T(8,128)(2,1)} %convolution_convert_fusion.1.refs_0_, bf16[32,64,512]{2,1,0:T(8,128)(2,1)} %bitcast.52, f32[32,16,128]{2,1,0:T(8,128)} %copy-done.12), custom_call_target="tpu_custom_call" | custom-call | tf_op jit(solution)/shard_map/pallas_call | solution.py:500
  660.3 1.2 slice_bitcast_fusion
  661.5 1.5 fusion.27
  663.0 1.9 fusion.9
  664.9 2.6 add_convert_fusion
  667.5 0.8 copy.45
  668.3 0.8 copy.46
  669.1 1.1 copy.47
  670.2 1.1 copy.48
  671.3 0.8 copy-done.10
  672.1 1.1 copy.49
  (73 shorter events, 2.8 us)
Async XLA Ops:
  7.2 91.8 %copy-start = (bf16[256,2048]{1,0:T(8,128)(2,1)S(1)}, bf16[256,2048]{1,0:T(8,128)(2,1)}, u32[]{:S(2)}) copy-start(bf16[256,2048]{1,0:T(8,128)(2,1)} %param.19) | copy-start | bytes 3145732
  7.2 229.9 %all-gather.2.cloned.1.call-start = ((), (), s32[]{:S(2)}) async-start(), calls=%async_computation.1 | async-start | bytes 6488064 | tf_op jit(solution)/shard_map/all_gather | solution.py:1266
  12.2 0.6 copy-start.21
  97.9 567.0 %reduce-scatter.2.cloned.1.call-start = ((), (), s32[]{:S(2)}) async-start(), calls=%async_computation.2 | async-start | bytes 5242880 | tf_op jit(solution)/shard_map/reduce_scatter | solution.py:1301
  99.3 80.7 %copy-start.19 = (f32[256]{0:T(256)}, f32[256]{0:T(256)S(1)}, u32[]{:S(2)}) copy-start(f32[256]{0:T(256)S(1)} %add_rsqrt_fusion.1) | copy-start | bytes 3076
  104.6 82.5 %copy-start.16 = (f32[256,128]{1,0:T(8,128)}, f32[256,128]{1,0:T(8,128)S(1)}, u32[]{:S(2)}) copy-start(f32[256,128]{1,0:T(8,128)S(1)} %get-tuple-element.132.refs_2_.refs_4_) | copy-start | bytes 393220
  104.6 82.5 %copy-start.17 = (f32[256,128]{1,0:T(8,128)}, f32[256,128]{1,0:T(8,128)S(1)}, u32[]{:S(2)}) copy-start(f32[256,128]{1,0:T(8,128)S(1)} %get-tuple-element.143.refs_1_.refs_3_) | copy-start | bytes 393220
  235.3 0.6 copy-start.22
  384.9 3.0 copy-start.3
  384.9 2.9 copy-start.5
  385.0 2.9 copy-start.23
  388.5 72.0 %copy-start.1 = (f32[256,2048]{1,0:T(8,128)}, f32[256,2048]{1,0:T(8,128)S(1)}, u32[]{:S(2)}) copy-start(f32[256,2048]{1,0:T(8,128)S(1)} %multiply_add_fusion) | copy-start | bytes 6291460
  458.2 2.3 copy-start.7
  564.2 6.3 copy-start.6
  564.2 6.3 copy-start.13
  564.2 6.2 copy-start.20
  570.5 2.9 copy-start.18
  576.1 9.0 %copy-start.12 = (f32[32,16,128]{2,1,0:T(8,128)}, f32[32,16,128]{2,1,0:T(8,128)S(1)}, u32[]{:S(2)}) copy-start(f32[32,16,128]{2,1,0:T(8,128)S(1)} %scatter.19.refs_2_) | copy-start | bytes 786436
  576.1 3.2 copy-start.11
  585.1 78.0 %copy-start.2 = (f32[256,2048]{1,0:T(8,128)S(1)}, f32[256,2048]{1,0:T(8,128)}, u32[]{:S(2)}) copy-start(f32[256,2048]{1,0:T(8,128)} %copy-done.1) | copy-start | bytes 6291460
  585.1 78.0 %copy-start.4 = (f32[256,2048]{1,0:T(8,128)S(1)}, f32[256,2048]{1,0:T(8,128)}, u32[]{:S(2)}) copy-start(f32[256,2048]{1,0:T(8,128)} %get-tuple-element.142) | copy-start | bytes 6291460
  664.9 2.6 copy-start.15
  664.9 3.4 copy-start.14
  667.5 1.6 copy-start.9
  668.3 1.9 copy-start.8
  670.2 1.9 copy-start.10
Sparse Core Ops, SparseCore 0:
  98.0 47.9 all-gather.1
  385.1 84.4 reduce-scatter.1

commit v4 on v3

--- a/solution.py
+++ b/solution.py
@@ -195,42 +195,6 @@
                     pl.when(sent)(self.z_copy(i, block, way).wait_send)
 
 
-def gather_kernel(specs, slow, dp_size, tensor_size, *refs):
-    count = len(specs)
-    run = GatherRun(
-        specs,
-        dp_size,
-        tensor_size,
-        refs[:count],
-        refs[count : 2 * count],
-        refs[2 * count : 3 * count],
-        refs[3 * count :],
-    )
-    run.greet()
-    run.begin(slow)
-    first = [i for i in run.lines if i not in slow]
-    for step in range(1, tensor_size):
-        for i in first:
-            run.line(i, step)
-    for i in first:
-        run.end_line(i)
-    for n in run.late:
-        run.hop(n, 0)
-    for i in slow:
-        run.begin_line(i)
-    ranks = 1 << run.dp_bits
-    for rank in range(1, max(ranks, tensor_size)):
-        if rank < ranks:
-            for n in range(len(run.hyper)):
-                run.hop(n, rank)
-        if rank < tensor_size:
-            for i in slow:
-                run.line(i, rank)
-    for i in slow:
-        run.end_line(i)
-    run.close()
-
-
 def gather_scratch(specs, arrays, dp_size, tensor_size):
     count = len(specs)
     hyper = max(1, sum(spec.half is not None for spec in specs))
@@ -259,21 +223,6 @@
     return [jax.ShapeDtypeStruct(spec.shape, array.dtype) for spec, array in zip(specs, arrays)]
 
 
-def gather(specs, arrays, dp_size, tensor_size, collective_id, slow=()):
-    count = len(specs)
-    held, sems = gather_scratch(specs, arrays, dp_size, tensor_size)
-    return pl.pallas_call(
-        functools.partial(gather_kernel, specs, slow, dp_size, tensor_size),
-        out_shape=gather_shapes(specs, arrays),
-        in_specs=[ANY] * count,
-        out_specs=[ANY] * count,
-        scratch_shapes=held + sems,
-        compiler_params=pltpu.CompilerParams(
-            collective_id=collective_id, has_side_effects=True, vmem_limit_bytes=VMEM_LIMIT
-        ),
-    )(*arrays)
-
-
 class Scatter:
     def __init__(self, kind, shape, part, part_shape, place, cut=None, cut_shape=None):
         self.kind, self.shape, self.part, self.part_shape = kind, shape, part, part_shape
@@ -301,11 +250,12 @@
 
 
 class ScatterRun:
-    def __init__(self, specs, dp_size, tensor_size, sources, outs, scratch):
+    def __init__(self, specs, dp_size, tensor_size, sources, outs, scratch, in_place=False):
         scratch = list(scratch)
         self.specs, self.sources, self.outs = specs, sources, outs
         self.tensor_size, self.dp_bits = tensor_size, dp_size.bit_length() - 1
-        self.total = [scratch.pop(0) for _ in specs]
+        self.in_place = in_place
+        self.total = None if in_place else [scratch.pop(0) for _ in specs]
         self.landing = [[scratch.pop(0) for _ in range(self.dp_bits)] for _ in specs]
         self.shares = [scratch.pop(0) if spec.kind != "dp" else None for spec in specs]
         self.own_sem, self.send, self.recv, self.z_send, self.z_recv = scratch
@@ -327,6 +277,8 @@
 
     def sum_at(self, unit, half, slot):
         i, owner = self.units[unit]
+        if self.in_place:
+            return self.part(unit, half, 2 * slot)
         return self.total[i].at[owner or 0, half, slot]
 
     def own_copy(self, unit, half, slot):
@@ -354,12 +306,16 @@
             device_id_type=MESH,
         )
 
+    def begin_unit(self, unit):
+        for slot in self.slots(0):
+            for half in (0, 1):
+                self.copy(unit, half, 0, slot).start()
+                if not self.in_place:
+                    self.own_copy(unit, half, slot).start()
+
     def begin(self):
         for unit in range(len(self.units)):
-            for slot in self.slots(0):
-                for half in (0, 1):
-                    self.copy(unit, half, 0, slot).start()
-                    self.own_copy(unit, half, slot).start()
+            self.begin_unit(unit)
 
     def z_copy(self, unit, half, other, slot):
         i, owner = self.units[unit]
@@ -383,7 +339,7 @@
         if stage < self.dp_bits:
             for slot in sorted(self.slots(stage), key=lambda s: -(s & 1)):
                 for half in (0, 1):
-                    if stage == 0:
+                    if stage == 0 and not self.in_place:
                         self.own_copy(unit, half, slot).wait()
                     self.copy(unit, half, stage, slot).wait_recv()
                     add_into(
@@ -466,13 +422,14 @@
     run.close()
 
 
-def scatter_scratch(specs, arrays, dp_size, tensor_size):
+def scatter_scratch(specs, arrays, dp_size, tensor_size, in_place=False):
     dp_bits = dp_size.bit_length() - 1
     scratch = []
     units = len(scatter_units(specs, tensor_size))
     pieces = [tensor_size if spec.kind == "own" else 1 for spec in specs]
     for spec, array, count in zip(specs, arrays, pieces):
-        scratch.append(pltpu.VMEM((count, 2, dp_size // 2) + spec.part_shape, array.dtype))
+        if not in_place:
+            scratch.append(pltpu.VMEM((count, 2, dp_size // 2) + spec.part_shape, array.dtype))
     for spec, array, count in zip(specs, arrays, pieces):
         for stage in range(dp_bits):
             scratch.append(
@@ -545,54 +502,6 @@
                 self.copy(other, other).wait_recv()
 
 
-def exchange_kernel(specs, dp_size, tensor_size, *refs):
-    count = len(specs)
-    run = ScatterRun(
-        specs,
-        dp_size,
-        tensor_size,
-        refs[1 : count + 1],
-        refs[count + 2 : 2 * count + 2],
-        refs[2 * count + 6 :],
-    )
-    blocks, summed = refs[0], refs[count + 1]
-    landing = refs[2 * count + 2]
-    exchange_run = ExchangeRun(tensor_size, blocks, landing, *refs[2 * count + 3 : 2 * count + 6])
-    greet((run.dp, run.tensor, tensor_size), False, True, run.dp_bits)
-    exchange_run.begin()
-    run.begin()
-    for unit, stage in run.steps():
-        run.step(unit, stage)
-    exchange_run.close()
-    total = landing[0].astype(jnp.float32)
-    for other in range(1, tensor_size):
-        total = total + landing[other].astype(jnp.float32)
-    summed[...] = total
-    run.close()
-
-
-def exchange(blocks, specs, arrays, sizes, collective_id):
-    dp_size, tensor_size = sizes
-    count = len(specs)
-    dma = pltpu.SemaphoreType.DMA
-    return pl.pallas_call(
-        functools.partial(exchange_kernel, specs, dp_size, tensor_size),
-        out_shape=[jax.ShapeDtypeStruct(blocks.shape[1:], jnp.float32)] + scatter_shapes(specs),
-        in_specs=[ANY] * (count + 1),
-        out_specs=[VMEM] * (count + 1),
-        scratch_shapes=[
-            pltpu.VMEM(blocks.shape, blocks.dtype),
-            dma,
-            dma((tensor_size,)),
-            dma((tensor_size,)),
-        ]
-        + scatter_scratch(specs, arrays, dp_size, tensor_size),
-        compiler_params=pltpu.CompilerParams(
-            collective_id=collective_id, has_side_effects=True, vmem_limit_bytes=VMEM_LIMIT
-        ),
-    )(blocks, *arrays)
-
-
 def lanes_of(shape):
     return lax.broadcasted_iota(jnp.int32, shape, len(shape) - 1)
 
@@ -629,49 +538,27 @@
                     action()
 
 
-def gather_plan(run):
-    plan = [(0.0, run.greet), (0.0, run.begin)]
-    for rank in range(1, 1 << run.dp_bits):
-        if rank >> (run.dp_bits - 1):
-            time = 1.0
-        else:
-            time = 0.45 + 0.35 * (rank.bit_count() - 1) / max(1, run.dp_bits - 2)
-        plan += [(time, functools.partial(run.hop, n, rank)) for n in range(len(run.hyper))]
-    for step in range(1, run.tensor_size):
-        time = 0.95 * step / (run.tensor_size - 1)
-        plan += [(time, functools.partial(run.line, i, step)) for i in run.lines]
-    plan += [(1.0, functools.partial(run.end_line, i)) for i in run.lines]
-    return sorted(plan, key=lambda entry: entry[0]) + [(1.0, run.close)]
-
-
-def attend_kernel(group_pairs, pairs, specs, dp_size, tensor_size, *refs):
-    count = len(specs)
-    refs = list(refs)
-    q_ref, cos_ref, sin_ref, k_ref, v_ref = (refs.pop(0) for _ in range(5))
-    sources = [refs.pop(0) for _ in specs]
-    o_ref, q_out, lse_ref = (refs.pop(0) for _ in range(3))
-    outs = [refs.pop(0) for _ in specs]
-    k_left, v_turned = (refs.pop(0) for _ in range(2))
-    run = GatherRun(specs, dp_size, tensor_size, sources, outs, refs[:count], refs[count:])
-    pair = pl.program_id(0)
-    group = pair // group_pairs
-    rows = q_ref.shape[0]
+def attend_pair(pair, group_pairs, q_pre, cos_ref, sin_ref, kv_all, k_left, v_turned, outs):
+    context, queries_out, lse_ref = outs
+    rows = q_pre.shape[0]
+    kv_width = kv_all.shape[1] // 2
+    group = lax.div(pair, group_pairs)
     start = lax.axis_index("tensor") * rows
-    plan = gather_plan(run)
-    at_steps([entry for entry in plan if entry[0] < 1.0], pair, pairs)
-
-    @pl.when(pair % group_pairs == 0)
+    at = pl.ds(pl.multiple_of(pair * 128, 128), 128)
+
+    @pl.when(lax.rem(pair, group_pairs) == 0)
     def _():
-        odd = group % 2 == 1
-        k_left[...] = left_head(k_ref[...].astype(jnp.float32), odd).astype(jnp.bfloat16)
-        v_turned[...] = left_head(v_ref[...].astype(jnp.float32), odd).T[:HEAD_DIM].astype(
-            jnp.bfloat16
-        )
-
-    raw = q_ref[...]
+        odd = lax.rem(group, 2) == 1
+        lane = pl.multiple_of(lax.div(group, 2) * 128, 128)
+        keys = kv_all[:, pl.ds(lane, 128)].astype(jnp.float32)
+        values = kv_all[:, pl.ds(kv_width + lane, 128)].astype(jnp.float32)
+        k_left[...] = left_head(keys, odd).astype(jnp.bfloat16)
+        v_turned[...] = left_head(values, odd).T[:HEAD_DIM].astype(jnp.bfloat16)
+
+    raw = q_pre[:, at]
     turned = (raw * cos_ref[...] + swap_halves(raw) * sin_ref[...]).astype(jnp.bfloat16)
     turned = turned.astype(jnp.float32) * HEAD_DIM ** (-0.5)
-    q_out[...] = turned.astype(jnp.bfloat16)
+    queries_out[:, at] = turned.astype(jnp.bfloat16)
     open_at = allowed(k_left.shape[0], rows, start)
     contexts = []
     for head in (0, 1):
@@ -681,55 +568,228 @@
         top = jnp.max(scores, axis=0, keepdims=True)
         exponent = jnp.exp(scores - top)
         summed = jnp.sum(exponent, axis=0, keepdims=True)
-        context = product(v_turned[...], exponent.astype(jnp.bfloat16))
-        contexts.append(context * (1.0 / summed))
-        lse_ref[0, head, :] = (top + jnp.log(summed))[0]
-    o_ref[...] = jnp.concatenate(contexts, axis=0).T.astype(jnp.bfloat16)
-    at_steps([entry for entry in plan if entry[0] >= 1.0], pair, pairs)
-
-
-def attend(
-    q_pre, cosines, sines, keys_values, head_count, group_heads, specs, arrays, sizes, collective_id
-):
-    rows, width = q_pre.shape
-    length, both = keys_values.shape
-    pairs, group_pairs = head_count // 2, group_heads // 2
-    kv_blocks = both // 256
-    wide = pl.BlockSpec((rows, 128), lambda p: (0, p))
-    table = pl.BlockSpec((rows, 128), lambda p: (0, 0))
+        part = product(v_turned[...], exponent.astype(jnp.bfloat16))
+        contexts.append(part * (1.0 / summed))
+        lse_ref[pair, pl.ds(head, 1), :] = top + jnp.log(summed)
+    context[:, at] = jnp.concatenate(contexts, axis=0).T.astype(jnp.bfloat16)
+
+
+def front_kernel(specs, kv_spec, group_pairs, dp_size, tensor_size, *refs):
+    refs = list(refs)
+
+    def take(count):
+        return [refs.pop(0) for _ in range(count)]
+
+    count = len(specs)
+    tokens, cos_ref, sin_ref = take(3)
+    sources = take(count)
+    context, queries, lse_ref, normed, normed_two, middle, gain_rows, kv_all = take(8)
+    outs = take(count)
+    held = take(count)
+    weights, kv_weights, gain_blocks, q_pre, k_left, v_turned = take(6)
+    sems = take(5)
+    kv_sems = take(5)
+    (load_sem,) = take(1)
+    key_value, gains, query, out, gate, up, down, cot = range(count)
+    run = GatherRun(specs, dp_size, tensor_size, sources, outs, held, sems)
+    rows, width = tokens.shape
+    own_rows = pl.ds(pl.multiple_of(run.tensor * rows, rows), rows)
+    kv_run = GatherRun(
+        [kv_spec], dp_size, tensor_size, [kv_all.at[own_rows, :]], [kv_all], [None], kv_sems
+    )
+    kv_width = kv_all.shape[1] // 2
+    near = [1 << bit for bit in range(run.dp_bits - 1)]
+    far = [r for r in range(1, 1 << (run.dp_bits - 1)) if r not in near]
+    far.sort(key=lambda rank: rank.bit_count())
+    core = list(range(1 << (run.dp_bits - 1), 1 << run.dp_bits))
+
+    def hops(ranks, *units):
+        for unit in units:
+            for rank in ranks:
+                run.hop(unit, rank)
+
+    run.greet()
+    loads = [
+        pltpu.make_async_copy(source, target, run.own_sem.at[i])
+        for i, (source, target) in enumerate(zip(sources, held))
+    ]
+    for load in loads:
+        load.start()
+    first = (key_value, gains, query)
+    for i in first:
+        run.begin_line(i)
+    for i, load in enumerate(loads):
+        load.wait()
+        run.own(i).start()
+    run.end_line(gate)
+    hops([0], gate)
+    for step in range(1, tensor_size):
+        for i in first:
+            run.line(i, step)
+        if step == tensor_size // 2:
+            hops(near, gate)
+    for i in first:
+        run.end_line(i)
+    hops([0], *first)
+    run.begin_line(out)
+    hops(far, gate)
+    for step in range(1, tensor_size):
+        run.line(out, step)
+    run.begin_line(cot)
+    hops(near, key_value, gains)
+    hops(far, key_value, gains)
+    hops(near, query)
+    for i in (out, up, down):
+        run.end_line(i)
+    hops([0], out)
+    hops(core, key_value, gains)
+
+    kv_load = pltpu.make_async_copy(outs[key_value], kv_weights, load_sem.at[0])
+    kv_load.start()
+    gain_load = pltpu.make_async_copy(outs[gains], gain_blocks, load_sem.at[1])
+    gain_load.start()
+    gain_load.wait()
+    blocks = gain_blocks.shape[0] // 16
+    lanes = width // 128
+    per = blocks // lanes
+    for lane in range(lanes):
+        row = jnp.zeros((16, 128), jnp.float32)
+        for other in range(per):
+            at = (lane * per + other) * 16
+            row = row + gain_blocks[at : at + 16, :].astype(jnp.float32)
+        gain_rows[:, lane * 128 : (lane + 1) * 128] = row[:8]
+    slab = 16
+
+    def norm_first(step, carry):
+        at = pl.ds(pl.multiple_of(step * slab, slab), slab)
+        raw = tokens[at, :].astype(jnp.float32)
+        scale = lax.rsqrt(jnp.mean(raw * raw, axis=-1, keepdims=True) + epsilon)
+        normed[at, :] = (raw * scale * gain_rows[0:1, :]).astype(normed.dtype)
+        return carry
+
+    lax.fori_loop(0, rows // slab, norm_first, 0)
+    kv_load.wait()
+    own_kv = product(normed[...], kv_weights[...])
+    repeat = kv_width // cos_ref.shape[1]
+    own_keys = own_kv[:, :kv_width]
+    own_keys = own_keys * jnp.concatenate([cos_ref[...]] * repeat, axis=1) + swap_halves(
+        own_keys
+    ) * jnp.concatenate([sin_ref[...]] * repeat, axis=1)
+    kv_all[own_rows, :] = jnp.concatenate([own_keys, own_kv[:, kv_width:]], axis=1).astype(
+        kv_all.dtype
+    )
+    run.line(cot, 1)
+    kv_run.begin_line(0)
+    hops(far, query)
+    hops(core, query)
+    hops([0], up)
+    query_load = pltpu.make_async_copy(outs[query], weights, load_sem.at[0])
+    query_load.start()
+    query_load.wait()
+    tiles = max(4, tensor_size)
+    tile = width // tiles
+    for j in range(tiles):
+        columns = slice(j * tile, (j + 1) * tile)
+        q_pre[:, columns] = product(normed[...], weights[:, columns])
+        if 1 <= j < tensor_size:
+            kv_run.line(0, j)
+    assert tiles >= tensor_size
+    pairs = lse_ref.shape[0]
+    plan = [
+        (0.1, lambda: hops(near, out)),
+        (0.3, lambda: hops(far, out)),
+        (0.3, lambda: hops([0], down)),
+        (0.55, lambda: hops(near, up)),
+        (0.8, lambda: hops(far, up)),
+    ]
+    for step in range(2, tensor_size):
+        time = 0.05 + 0.6 * (step - 2) / max(1, tensor_size - 3)
+        plan.append((time, functools.partial(run.line, cot, step)))
+    plan.sort(key=lambda entry: entry[0])
+
+    def pair_step(pair, carry):
+        at_steps(plan, pair, pairs)
+        attend_pair(
+            pair,
+            group_pairs,
+            q_pre,
+            cos_ref,
+            sin_ref,
+            kv_all,
+            k_left,
+            v_turned,
+            (context, queries, lse_ref),
+        )
+        return carry
+
+    lax.fori_loop(0, pairs, pair_step, 0)
+    hops(core, out)
+    out_load = pltpu.make_async_copy(outs[out], weights, load_sem.at[0])
+    out_load.start()
+    hops(near, down)
+    out_load.wait()
+    for j in range(4):
+        columns = slice(j * (width // 4), (j + 1) * (width // 4))
+        middle[:, columns] = tokens[:, columns].astype(jnp.float32) + product(
+            context[...], weights[:, columns]
+        )
+
+    def norm_second(step, carry):
+        at = pl.ds(pl.multiple_of(step * slab, slab), slab)
+        raw = middle[at, :]
+        scale = lax.rsqrt(jnp.mean(raw * raw, axis=-1, keepdims=True) + epsilon)
+        normed_two[at, :] = (raw * scale * gain_rows[1:2, :]).astype(normed_two.dtype)
+        return carry
+
+    lax.fori_loop(0, rows // slab, norm_second, 0)
+    hops(far, down)
+    hops(core, gate, up, down)
+    run.end_line(cot)
+    run.close()
+    kv_run.close()
+
+
+def front(tokens, cosines, sines, arrays, specs, kv_spec, heads, group_heads, sizes, collective_id):
+    dp_size, tensor_size = sizes
+    rows, width = tokens.shape
+    length = rows * tensor_size
+    low, full = jnp.bfloat16, jnp.float32
     held, sems = gather_scratch(specs, arrays, *sizes)
+    _, kv_sems = gather_scratch([kv_spec], [], *sizes)
+    kv_both = specs[0].shape[1]
+    pairs = heads // 2
+    tokens_low = jax.ShapeDtypeStruct((rows, width), low)
     return pl.pallas_call(
-        functools.partial(attend_kernel, group_pairs, pairs, specs, *sizes),
-        grid=(pairs,),
+        functools.partial(front_kernel, specs, kv_spec, group_heads // 2, *sizes),
         out_shape=[
-            jax.ShapeDtypeStruct((rows, width), jnp.bfloat16),
-            jax.ShapeDtypeStruct((rows, width), jnp.bfloat16),
-            jax.ShapeDtypeStruct((pairs, 2, rows), jnp.float32),
+            tokens_low,
+            tokens_low,
+            jax.ShapeDtypeStruct((pairs, 2, rows), full),
+            tokens_low,
+            tokens_low,
+            jax.ShapeDtypeStruct((rows, width), full),
+            jax.ShapeDtypeStruct((8, width), full),
+            jax.ShapeDtypeStruct((length, kv_both), low),
         ]
         + gather_shapes(specs, arrays),
-        in_specs=[
-            wide,
-            table,
-            table,
-            pl.BlockSpec((length, 128), lambda p: (0, p // group_pairs // 2)),
-            pl.BlockSpec((length, 128), lambda p: (0, kv_blocks + p // group_pairs // 2)),
+        in_specs=[VMEM] * 3 + [ANY] * len(specs),
+        out_specs=[VMEM] * 8 + [ANY] * len(specs),
+        scratch_shapes=held
+        + [
+            pltpu.VMEM((width, width), low),
+            pltpu.VMEM((width, kv_both), low),
+            pltpu.VMEM(specs[1].shape, low),
+            pltpu.VMEM((rows, width), full),
+            pltpu.VMEM((length, 128), low),
+            pltpu.VMEM((HEAD_DIM, length), low),
         ]
-        + [ANY] * len(specs),
-        out_specs=[wide, wide, pl.BlockSpec((1, 2, rows), lambda p: (p, 0, 0))]
-        + [ANY] * len(specs),
-        scratch_shapes=[
-            pltpu.VMEM((length, 128), jnp.bfloat16),
-            pltpu.VMEM((HEAD_DIM, length), jnp.bfloat16),
-        ]
-        + held
-        + sems,
+        + sems
+        + kv_sems
+        + [pltpu.SemaphoreType.DMA((2,))],
         compiler_params=pltpu.CompilerParams(
             collective_id=collective_id, has_side_effects=True, vmem_limit_bytes=VMEM_LIMIT
         ),
-        cost_estimate=pl.CostEstimate(
-            flops=4 * rows * length * width, bytes_accessed=8 * rows * width, transcendentals=0
-        ),
-    )(q_pre, cosines, sines, keys_values, keys_values, *arrays)
+    )(tokens, cosines, sines, *arrays)
 
 
 def scatter_plan(run):
@@ -862,20 +922,18 @@
 
 
 def block_at(place, tensor, tensor_size):
-    last = tensor_size - 1
-    pairs = jnp.minimum(tensor, last - tensor)
-    near = lax.div(place + 1, 2)
-    paired = jnp.where(lax.rem(place, 2) == 1, tensor - near, tensor + near)
-    far = place - pairs
-    lone = jnp.where(tensor > last - tensor, tensor - far, tensor + far)
-    return jnp.where(place <= 2 * pairs, paired, lone)
+    above = tensor_size - 1 - tensor
+    up = jnp.where(place <= above, tensor + place, tensor - (place - above))
+    down = jnp.where(place <= tensor, tensor - place, place)
+    return jnp.where(tensor <= above, up, down)
 
 
 def mlp_kernel(
+    specs,
+    dp_size,
     tensor_size,
     normed_ref,
-    cot_low_ref,
-    cot_high_ref,
+    cot_ref,
     gate_ref,
     up_ref,
     down_ref,
@@ -883,7 +941,7 @@
     y_ref,
     d_gate_ref,
     d_up_ref,
-    d_down_ref,
+    down_sum,
     normed,
     cot,
     gate,
@@ -902,7 +960,11 @@
     b_send,
     b_recv,
     out_sem,
+    *scatter_refs,
 ):
+    run = ScatterRun(
+        specs, dp_size, tensor_size, [down], [down_sum], scatter_refs, in_place=True
+    )
     dp, tensor = lax.axis_index("dp"), lax.axis_index("tensor")
     rows, width = normed_ref.shape
     units = gate.shape[1]
@@ -914,14 +976,13 @@
                 (gate_ref, gate),
                 (up_ref, up),
                 (down_ref, down),
-                (cot_low_ref, cot.at[:, : cot_low_ref.shape[1]]),
-                (cot_high_ref, cot.at[:, cot_low_ref.shape[1] :]),
+                (cot_ref, cot),
             )
         )
     ]
     for load in loads:
         load.start()
-    greet((dp, tensor, tensor_size), False, True, 0)
+    greet((dp, tensor, tensor_size), False, True, run.dp_bits)
     has = [tensor + 1 < tensor_size, tensor > 0]
 
     def n_copy(block, way, source=None):
@@ -946,10 +1007,7 @@
                 n_copy(block, way).wait_recv()
                 pl.when(has[way])(n_copy(block, way).start)
 
-    def distance_at(place):
-        return jnp.abs(block_at(place, tensor, tensor_size) - tensor)
-
-    inner = (tensor > 0) & (tensor + 1 < tensor_size)
+    farthest = jnp.maximum(tensor, tensor_size - 1 - tensor)
 
     def b_copy(block, slot):
         return pltpu.make_async_remote_copy(
@@ -969,21 +1027,14 @@
 
     def chunk(place, carry):
         block = block_at(place, tensor, tensor_size)
-        fresh = (place >= 1) & (distance_at(place) != distance_at(place - 1))
-
-        @pl.when(fresh & jnp.logical_not((place >= 2) & inner))
+
+        @pl.when((place >= 1) & (place <= farthest))
         def _():
-            pump(distance_at(place))
+            pump(place)
 
         rows_in = normed[block]
         gate_pre = product(rows_in, gate[...])
         upward = product(rows_in, up[...])
-
-        @pl.when((place >= 1) & (place + 1 < tensor_size) & inner)
-        def _():
-            @pl.when(distance_at(place + 1) != distance_at(place))
-            def _():
-                pump(distance_at(place + 1))
 
         @pl.when(place == 0)
         def _():
@@ -1028,7 +1079,7 @@
 
     all_rows = tensor_size * rows
 
-    def weight_grad(left, right, out, out_hbm, sem):
+    def weight_grad(left, right, out):
         extent = left.shape[2]
         tile = 256 if extent % 256 == 0 else 128 if extent % 128 == 0 else extent
 
@@ -1039,11 +1090,15 @@
             return carry
 
         lax.fori_loop(0, extent // tile, body, 0)
-        pltpu.make_async_copy(out, out_hbm, sem).start()
-
-    weight_grad(hidden, cot, down, d_down_ref, out_sem.at[0])
-    weight_grad(normed, d_gate, gate, d_gate_ref, out_sem.at[1])
-    weight_grad(normed, d_up, up, d_up_ref, out_sem.at[2])
+
+    weight_grad(hidden, cot, down)
+    run.begin_unit(0)
+    weight_grad(normed, d_gate, gate)
+    pltpu.make_async_copy(gate, d_gate_ref, out_sem.at[0]).start()
+    run.step(0, 0)
+    weight_grad(normed, d_up, up)
+    pltpu.make_async_copy(up, d_up_ref, out_sem.at[1]).start()
+    run.step(0, 1)
 
     for other in range(tensor_size):
 
@@ -1062,9 +1117,11 @@
         return carry
 
     lax.fori_loop(0, rows // slab, add_slab, 0)
-    pltpu.make_async_copy(down, d_down_ref, out_sem.at[0]).wait()
-    pltpu.make_async_copy(gate, d_gate_ref, out_sem.at[1]).wait()
-    pltpu.make_async_copy(up, d_up_ref, out_sem.at[2]).wait()
+    for later in range(2, run.dp_bits + 1):
+        run.step(0, later)
+    run.close()
+    pltpu.make_async_copy(gate, d_gate_ref, out_sem.at[0]).wait()
+    pltpu.make_async_copy(up, d_up_ref, out_sem.at[1]).wait()
     for other in range(tensor_size):
 
         @pl.when(other != tensor)
@@ -1076,7 +1133,8 @@
             pl.when(sent)(n_copy(other, way).wait_send)
 
 
-def feed_forward(normed, cot_low, cot_high, gate, up, down, tensor_size, collective_id):
+def feed_forward(normed, cot_all, gate, up, down, specs, sizes, collective_id):
+    dp_size, tensor_size = sizes
     rows, width = normed.shape
     units = gate.shape[1]
     low = jnp.bfloat16
@@ -1084,16 +1142,16 @@
     inner = (tensor_size, rows, units)
     dma = pltpu.SemaphoreType.DMA
     return pl.pallas_call(
-        functools.partial(mlp_kernel, tensor_size),
+        functools.partial(mlp_kernel, specs, dp_size, tensor_size),
         out_shape=[
             jax.ShapeDtypeStruct((rows, width), jnp.float32),
             jax.ShapeDtypeStruct(tokens, low),
             jax.ShapeDtypeStruct(gate.shape, low),
             jax.ShapeDtypeStruct(up.shape, low),
-            jax.ShapeDtypeStruct(down.shape, low),
-        ],
-        in_specs=[ANY] * 6,
-        out_specs=[VMEM] + [ANY] * 4,
+        ]
+        + scatter_shapes(specs),
+        in_specs=[ANY] * 5,
+        out_specs=[VMEM] + [ANY] * 3 + [VMEM],
         scratch_shapes=[
             pltpu.VMEM(tokens, low),
             pltpu.VMEM(tokens, low),
@@ -1106,16 +1164,17 @@
             pltpu.VMEM((2, rows, width), low),
             pltpu.VMEM(tokens, low),
             pltpu.VMEM(tokens, low),
-            dma((6,)),
+            dma((5,)),
             dma((2, tensor_size)),
             dma((tensor_size,)),
             dma((2,)),
             dma((tensor_size,)),
             dma((tensor_size,)),
-            dma((3,)),
-        ],
+            dma((2,)),
+        ]
+        + scatter_scratch(specs, [down], dp_size, tensor_size, in_place=True),
         compiler_params=pltpu.CompilerParams(
-            collective_id=collective_id, has_side_effects=True, vmem_limit_bytes=60 * 2**20
+            collective_id=collective_id, has_side_effects=True, vmem_limit_bytes=63 * 2**20
         ),
         cost_estimate=pl.CostEstimate(
             flops=18 * tensor_size * rows * width * units,
@@ -1124,12 +1183,210 @@
         ),
     )(
         normed,
-        cot_low.reshape(tensor_size, -1, width),
-        cot_high.reshape(tensor_size, -1, width),
+        cot_all.reshape(tokens),
         gate,
         up,
         down,
     )
+
+
+def tail_kernel(specs, dp_size, tensor_size, *refs):
+    refs = list(refs)
+
+    def take(count):
+        return [refs.pop(0) for _ in range(count)]
+
+    sources = take(7)
+    blocks, wq_ref, cos_ref, sin_ref, gain_ref, second_ref = take(6)
+    tokens_out, out_sum, query_sum, kv_sum, gain_sum = take(5)
+    held = take(7)
+    context, middle_low, normed, dq, wkv, tokens, middle = held
+    o_grad, q_grad, kv_grad, gain_grad, wq_tile, kv_landing, kv_low, column_sum = take(8)
+    load_sem, tile_sem, ex_own, ex_send, ex_recv = take(5)
+    run = ScatterRun(
+        specs,
+        dp_size,
+        tensor_size,
+        [o_grad, q_grad, kv_grad, gain_grad],
+        [out_sum, query_sum, kv_sum, gain_sum],
+        refs,
+        in_place=True,
+    )
+    rows, width = tokens.shape
+    q_cols = q_grad.shape[2]
+    o_rows = o_grad.shape[1]
+    kv_width = kv_low.shape[1] // 2
+    loads = [
+        pltpu.make_async_copy(source, target, load_sem.at[i])
+        for i, (source, target) in enumerate(zip(sources, held))
+    ]
+    for load in loads:
+        load.start()
+
+    def tile_copy(j):
+        return pltpu.make_async_copy(
+            wq_ref.at[:, pl.ds(j * q_cols, q_cols)], wq_tile.at[j % 2], tile_sem.at[j % 2]
+        )
+
+    tile_copy(0).start()
+    exchange_run = ExchangeRun(tensor_size, blocks, kv_landing, ex_own, ex_send, ex_recv)
+    greet((run.dp, run.tensor, tensor_size), False, True, run.dp_bits)
+    exchange_run.begin()
+
+    def out_piece(j):
+        tile = min(256, o_rows)
+        for row in range(0, o_rows, tile):
+            o_grad[j, row : row + tile, :] = product_left(
+                context[:, j * o_rows + row : j * o_rows + row + tile], middle_low[...]
+            ).astype(o_grad.dtype)
+        run.begin_unit(j)
+
+    def query_piece(j):
+        grads = dq[:, j * q_cols : (j + 1) * q_cols]
+        tile = 512
+        for row in range(0, width, tile):
+            q_grad[j, row : row + tile, :] = product_left(
+                normed[:, row : row + tile], grads
+            ).astype(q_grad.dtype)
+        run.begin_unit(tensor_size + j)
+
+    def back_piece(j):
+        if j + 1 < tensor_size:
+            tile_copy(j + 1).start()
+        tile_copy(j).wait()
+        part = product_right(dq[:, j * q_cols : (j + 1) * q_cols], wq_tile[j % 2])
+        if j == 0:
+            tokens_out[...] = part
+        else:
+            tokens_out[...] += part
+
+    def kv_piece():
+        exchange_run.close()
+        total = kv_landing[0].astype(jnp.float32)
+        for other in range(1, tensor_size):
+            total = total + kv_landing[other].astype(jnp.float32)
+        grad_keys = total[:, :kv_width]
+        repeat = kv_width // cos_ref.shape[1]
+        cosines = jnp.concatenate([cos_ref[...]] * repeat, axis=1)
+        sines = jnp.concatenate([sin_ref[...]] * repeat, axis=1)
+        kv_low[:, :kv_width] = (grad_keys * cosines - swap_halves(grad_keys) * sines).astype(
+            kv_low.dtype
+        )
+        kv_low[:, kv_width:] = total[:, kv_width:].astype(kv_low.dtype)
+        for row in range(0, width, 512):
+            kv_grad[row : row + 512, :] = product_left(
+                normed[:, row : row + 512], kv_low[...]
+            ).astype(kv_grad.dtype)
+        run.begin_unit(2 * tensor_size)
+        tokens_out[...] += product_right(kv_low[...], wkv[...])
+
+    slab = 16
+
+    def finish(step, carry):
+        at = pl.ds(pl.multiple_of(step * slab, slab), slab)
+        raw = tokens[at, :].astype(jnp.float32)
+        scale = lax.rsqrt(jnp.mean(raw * raw, axis=-1, keepdims=True) + epsilon)
+        unit = raw * scale
+        grad = tokens_out[at, :]
+        gained = grad * unit
+        column_sum[...] += gained[:8] + gained[8:]
+        scaled = grad * gain_ref[...]
+        mean = jnp.mean(scaled * unit, axis=-1, keepdims=True)
+        tokens_out[at, :] = middle[at, :] + scale * (scaled - unit * mean)
+        return carry
+
+    def last_piece():
+        column_sum[...] = jnp.zeros_like(column_sum)
+        lax.fori_loop(0, rows // slab, finish, 0)
+        gain_grad[...] = jnp.zeros_like(gain_grad)
+        gain_grad[0:1, :] = jnp.sum(column_sum[...], axis=0, keepdims=True)
+        gain_grad[8:9, :] = second_ref[...]
+        run.begin_unit(2 * tensor_size + 1)
+
+    loads[0].wait()
+    loads[1].wait()
+    for j in range(tensor_size):
+        out_piece(j)
+        if 1 <= j <= 2:
+            run.step(j - 1, 0)
+    for load in loads[2:]:
+        load.wait()
+    count = len(run.units)
+    work = {j: [functools.partial(query_piece, j)] for j in range(tensor_size)}
+    room = max(1, tensor_size - 2)
+    for j in range(tensor_size):
+        work.setdefault(tensor_size + j * room // tensor_size, []).append(
+            functools.partial(back_piece, j)
+        )
+    work.setdefault(2 * tensor_size - 2, []).append(kv_piece)
+    work.setdefault(2 * tensor_size - 1, []).append(last_piece)
+    for tick in range(count + 1):
+        for piece in work.get(tick, []):
+            piece()
+        if tick < count:
+            run.step(tick, 1)
+        if tick + 2 < count:
+            run.step(tick + 2, 0)
+        if tick:
+            for stage in range(2, run.dp_bits + 1):
+                run.step(tick - 1, stage)
+    run.close()
+
+
+def tail(
+    context,
+    middle_low,
+    normed,
+    dq,
+    key_value,
+    tokens,
+    middle,
+    kv_blocks,
+    query,
+    cosines,
+    sines,
+    gain,
+    second,
+    specs,
+    sizes,
+    collective_id,
+):
+    dp_size, tensor_size = sizes
+    rows, width = tokens.shape
+    low, full = jnp.bfloat16, jnp.float32
+    o_spec, q_spec = specs[0], specs[1]
+    kv_both = key_value.shape[1]
+    dma = pltpu.SemaphoreType.DMA
+    arrays = [
+        jax.ShapeDtypeStruct((tensor_size, o_spec.shape[0], width), low),
+        jax.ShapeDtypeStruct((tensor_size, width, q_spec.shape[1]), low),
+        jax.ShapeDtypeStruct((width, kv_both), low),
+        jax.ShapeDtypeStruct((16, width), full),
+    ]
+    loaded = [context, middle_low, normed, dq, key_value, tokens, middle]
+    return pl.pallas_call(
+        functools.partial(tail_kernel, specs, dp_size, tensor_size),
+        out_shape=[jax.ShapeDtypeStruct((rows, width), full)] + scatter_shapes(specs),
+        in_specs=[ANY] * 9 + [VMEM] * 4,
+        out_specs=[VMEM] * (1 + len(specs)),
+        scratch_shapes=[pltpu.VMEM(array.shape, array.dtype) for array in loaded]
+        + [pltpu.VMEM(array.shape, array.dtype) for array in arrays]
+        + [
+            pltpu.VMEM((2, width, q_spec.shape[1]), low),
+            pltpu.VMEM(kv_blocks.shape, low),
+            pltpu.VMEM((rows, kv_both), low),
+            pltpu.VMEM((8, width), full),
+            dma((7,)),
+            dma((2,)),
+            dma,
+            dma((tensor_size,)),
+            dma((tensor_size,)),
+        ]
+        + scatter_scratch(specs, arrays, dp_size, tensor_size, in_place=True),
+        compiler_params=pltpu.CompilerParams(
+            collective_id=collective_id, has_side_effects=True, vmem_limit_bytes=60 * 2**20
+        ),
+    )(*loaded, kv_blocks, query, cosines, sines, gain, second)
 
 
 def rope_tables(rows, tensor):
@@ -1142,14 +1399,6 @@
         jnp.concatenate([cosines, cosines] * 2, axis=1),
         jnp.concatenate([-sines, sines] * 2, axis=1),
     )
-
-
-def turn_heads(values, cosines, sines):
-    rows, width = values.shape
-    parts = values.reshape(rows, width // HEAD_DIM, 2, HEAD_DIM // 2)
-    swapped = parts[:, :, ::-1, :].reshape(rows, width)
-    repeat = width // 128
-    return values * jnp.tile(cosines, (1, repeat)) + swapped * jnp.tile(sines, (1, repeat))
 
 
 def start_row(dp, size):
@@ -1181,11 +1430,14 @@
     kv_rows = w_key.shape[0]
     o_rows, o_cols = w_out.shape
     gain_part = attn_gain.shape[0]
-    call = functools.partial(gather, dp_size=dp_size, tensor_size=tensor_size)
 
     key_value = jnp.concatenate([w_key, w_value], axis=1)
-    gains = jnp.zeros((16, 128), jnp.bfloat16)
-    gains = gains.at[0, :gain_part].set(attn_gain).at[1, :gain_part].set(mlp_gain)
+    per = 128 // gain_part
+    spot = lax.rem(lax.axis_index("dp") * tensor_size + tensor_index, per)
+    rows_at = lax.broadcasted_iota(jnp.int32, (16, 128), 0)
+    here = lax.div(lax.broadcasted_iota(jnp.int32, (16, 128), 1), gain_part) == spot
+    gains = jnp.where(rows_at == 0, jnp.tile(attn_gain, per), jnp.tile(mlp_gain, per))
+    gains = jnp.where(here & (rows_at < 2), gains, jnp.zeros_like(gains))
     query_spec = Gather(
         (width, heads * HEAD_DIM),
         lambda ref, dp, t: ref.at[
@@ -1253,103 +1505,49 @@
         ],
         False,
     )
-    low_rows = rows // 4 * 3
-    cot_low_spec, cot_high_spec = row_spec((low_rows, width)), row_spec((rows - low_rows, width))
     sizes = (dp_size, tensor_size)
-    query_full, key_value_full, gains_full, gate_full, cot_low = call(
-        [query_spec, kv_spec, gain_spec, column_spec, cot_low_spec],
-        [w_query, key_value, gains, w_gate, cotangent[:low_rows]],
-        collective_id=1,
-        slow=(4,),
-    )
-    down_late, query_full = lax.optimization_barrier((w_down, query_full))
-    down_full = lax.all_gather(down_late, "dp", axis=1, tiled=True)
-    gains_full = gains_full.reshape(-1, 16, 128)[:, :2, :gain_part].astype(jnp.float32)
-    gain_first = gains_full[:, 0].reshape(width)
-    gain_second = gains_full[:, 1].reshape(width)
     cosines, sines = rope_tables(rows, tensor_index)
-
-    residual = tokens.astype(jnp.float32)
-    scale_first = lax.rsqrt(jnp.mean(residual * residual, axis=-1, keepdims=True) + epsilon)
-    unit_first = residual * scale_first
-    normed_first = (unit_first * gain_first).astype(jnp.bfloat16)
-    kv_pre = product(normed_first, key_value_full)
-    kv_own = jnp.concatenate(
-        [turn_heads(kv_pre[:, :kv_width], cosines, sines), kv_pre[:, kv_width:]], axis=1
-    ).astype(jnp.bfloat16)
-    query_pre = product(normed_first, query_full)
-    kv_all, out_full = call([row_spec(kv_own.shape), out_spec], [kv_own, w_out], collective_id=2)
-    context, queries, log_sums, up_full, cot_high = attend(
-        query_pre,
+    (
+        context,
+        queries,
+        log_sums,
+        normed_first,
+        normed_own,
+        middle,
+        gain_rows,
+        kv_all,
+        key_value_full,
+        _,
+        query_full,
+        out_full,
+        gate_full,
+        up_full,
+        down_full,
+        cot_all,
+    ) = front(
+        tokens,
         cosines,
         sines,
-        kv_all,
+        [key_value, gains, w_query, w_out, w_gate, w_up, w_down, cotangent],
+        [
+            kv_spec,
+            gain_spec,
+            query_spec,
+            out_spec,
+            column_spec,
+            column_spec,
+            down_spec,
+            row_spec(cotangent.shape),
+        ],
+        row_spec((rows, 2 * kv_width)),
         heads,
         group_heads,
-        [column_spec, cot_high_spec],
-        [w_up, cotangent[low_rows:]],
         sizes,
-        8,
-    )
-    middle = residual + product(context, out_full)
+        1,
+    )
+    gain_first, gain_second = gain_rows[0], gain_rows[1]
     scale_second = lax.rsqrt(jnp.mean(middle * middle, axis=-1, keepdims=True) + epsilon)
     unit_second = middle * scale_second
-    normed_own = (unit_second * gain_second).astype(jnp.bfloat16)
-    back_second, mlp_part, grad_gate_w, grad_up_w, grad_down_w = feed_forward(
-        normed_own, cot_low, cot_high, gate_full, up_full, down_full, tensor_size, 3
-    )
-    mlp_rows = lax.psum_scatter(
-        mlp_part.reshape(tensor_size * rows, width), "tensor", scatter_dimension=0, tiled=True
-    )
-    grad_gain_second = jnp.sum(back_second * unit_second, axis=0)
-    grad_middle = cotangent.astype(jnp.float32) + norm_back(
-        back_second, unit_second, scale_second, gain_second
-    )
-    middle_low = grad_middle.astype(jnp.bfloat16)
-    grad_context = product_right(middle_low, out_full).astype(jnp.bfloat16)
-    grad_out_w = product_left(context, middle_low).astype(jnp.bfloat16)
-    query_scatter = Scatter(
-        "own",
-        (q_rows, q_cols),
-        lambda ref, dp, half, j: ref.at[
-            pl.ds(pl.multiple_of(dp * q_rows + half * (q_rows // 2), q_rows // 2), q_rows // 2),
-            pl.ds(j * q_cols, q_cols),
-        ],
-        (q_rows // 2, q_cols),
-        lambda ref, half: ref.at[pl.ds(half * (q_rows // 2), q_rows // 2), :],
-    )
-    kv_scatter = Scatter(
-        "cut",
-        (kv_rows, 2 * kv_width),
-        lambda ref, dp, half, j: ref.at[
-            pl.ds(dp * tensor_size, tensor_size), :, pl.ds(half * kv_width, kv_width)
-        ],
-        (tensor_size, kv_rows, kv_width),
-        lambda ref, half: ref.at[:, pl.ds(half * kv_width, kv_width)],
-        lambda ref, j: ref.at[j],
-        (kv_rows, kv_width),
-    )
-    out_scatter = Scatter(
-        "own",
-        (o_rows, o_cols),
-        lambda ref, dp, half, j: ref.at[
-            pl.ds(j * o_rows + half * (o_rows // 2), o_rows // 2),
-            pl.ds(start_row(dp, o_cols), o_cols),
-        ],
-        (o_rows // 2, o_cols),
-        lambda ref, half: ref.at[pl.ds(half * (o_rows // 2), o_rows // 2), :],
-    )
-    gain_scatter = Scatter(
-        "cut",
-        (16, 128),
-        lambda ref, dp, half, j: ref.at[
-            pl.ds(dp * tensor_size, tensor_size), pl.ds(half * 8, 8), :
-        ],
-        (tensor_size, 8, 128),
-        lambda ref, half: ref.at[pl.ds(half * 8, 8), :],
-        lambda ref, j: ref.at[j],
-        (8, 128),
-    )
     column_scatter = Scatter(
         "dp",
         (up_rows, units),
@@ -1363,6 +1561,63 @@
         lambda ref, dp, half, j: down_spec.half(ref, dp, half),
         (units // 2, down_cols),
         lambda ref, half: ref.at[pl.ds(half * (units // 2), units // 2), :],
+    )
+    back_second, mlp_part, grad_gate_w, grad_up_w, sum_down = feed_forward(
+        normed_own, cot_all, gate_full, up_full, down_full, [down_scatter], sizes, 3
+    )
+    mlp_rows = lax.psum_scatter(
+        mlp_part.reshape(tensor_size * rows, width), "tensor", scatter_dimension=0, tiled=True
+    )
+    grad_gain_second = jnp.sum(back_second * unit_second, axis=0)
+    grad_middle = cotangent.astype(jnp.float32) + norm_back(
+        back_second, unit_second, scale_second, gain_second
+    )
+    middle_low = grad_middle.astype(jnp.bfloat16)
+    grad_context = product_right(middle_low, out_full).astype(jnp.bfloat16)
+    query_scatter = Scatter(
+        "own",
+        (q_rows, q_cols),
+        lambda ref, dp, half, j: ref.at[
+            j,
+            pl.ds(pl.multiple_of(dp * q_rows + half * (q_rows // 2), q_rows // 2), q_rows // 2),
+            :,
+        ],
+        (q_rows // 2, q_cols),
+        lambda ref, half: ref.at[pl.ds(half * (q_rows // 2), q_rows // 2), :],
+    )
+    kv_scatter = Scatter(
+        "cut",
+        (kv_rows, 2 * kv_width),
+        lambda ref, dp, half, j: ref.at[
+            pl.ds(start_row(dp, kv_all_rows), kv_all_rows), pl.ds(half * kv_width, kv_width)
+        ],
+        (kv_all_rows, kv_width),
+        lambda ref, half: ref.at[:, pl.ds(half * kv_width, kv_width)],
+        lambda ref, j: ref.at[pl.ds(j * kv_rows, kv_rows), :],
+        (kv_rows, kv_width),
+    )
+    out_scatter = Scatter(
+        "own",
+        (o_rows, o_cols),
+        lambda ref, dp, half, j: ref.at[
+            j,
+            pl.ds(half * (o_rows // 2), o_rows // 2),
+            pl.ds(start_row(dp, o_cols), o_cols),
+        ],
+        (o_rows // 2, o_cols),
+        lambda ref, half: ref.at[pl.ds(half * (o_rows // 2), o_rows // 2), :],
+    )
+    gain_cols = tensor_size * gain_part
+    gain_scatter = Scatter(
+        "cut",
+        (16, gain_cols),
+        lambda ref, dp, half, j: ref.at[
+            pl.ds(half * 8, 8), pl.ds(start_row(dp, gain_cols), gain_cols)
+        ],
+        (8, gain_cols),
+        lambda ref, half: ref.at[pl.ds(half * 8, 8), :],
+        lambda ref, j: ref,
+        (8, gain_cols),
     )
     grad_queries, grad_keys, grad_values, sum_gate, sum_up = attend_back(
         queries,
@@ -1379,49 +1634,36 @@
         7,
     )
     grad_kv = jnp.concatenate([grad_keys, grad_values], axis=1)
-    grad_kv_own, sum_out, sum_down = exchange(
+    grad_tokens, sum_out, sum_query, sum_kv, sum_gains = tail(
+        context,
+        middle_low,
+        normed_first,
+        grad_queries,
+        key_value_full,
+        tokens,
+        grad_middle,
         grad_kv.reshape(tensor_size, rows, 2 * kv_width),
-        [out_scatter, down_scatter],
-        [grad_out_w, grad_down_w],
+        query_full,
+        cosines,
+        sines,
+        gain_first.reshape(1, width),
+        grad_gain_second.reshape(1, width),
+        [out_scatter, query_scatter, kv_scatter, gain_scatter],
         sizes,
         5,
     )
-    grad_kv_own = jnp.concatenate(
-        [turn_heads(grad_kv_own[:, :kv_width], cosines, -sines), grad_kv_own[:, kv_width:]], axis=1
-    ).astype(jnp.bfloat16)
-    grad_query_w = product_left(normed_first, grad_queries).astype(jnp.bfloat16)
-    grad_kv_w = product_left(normed_first, grad_kv_own).astype(jnp.bfloat16)
-    back_first = product_right(grad_queries, query_full) + product_right(
-        grad_kv_own, key_value_full
-    )
-    grad_gain_first = jnp.sum(back_first * unit_first, axis=0)
-    grad_tokens = grad_middle + norm_back(back_first, unit_first, scale_first, gain_first)
-
-    grad_gains = jnp.zeros((dp_size * tensor_size, 16, 128), jnp.float32)
-    grad_gains = grad_gains.at[:, 0, :gain_part].set(grad_gain_first.reshape(-1, gain_part))
-    grad_gains = grad_gains.at[:, 8, :gain_part].set(grad_gain_second.reshape(-1, gain_part))
-    sum_query, sum_kv, sum_gains = scatter(
-        [query_scatter, kv_scatter, gain_scatter],
-        [
-            grad_query_w,
-            grad_kv_w.reshape(dp_size * tensor_size, kv_rows, 2 * kv_width),
-            grad_gains,
-        ],
-        dp_size,
-        tensor_size,
-        6,
-    )
+    sum_gains = lax.dynamic_slice_in_dim(sum_gains, tensor_index * gain_part, gain_part, 1)
     middle, mlp_rows, sum_query = lax.optimization_barrier((middle, mlp_rows, sum_query))
     output = (middle + mlp_rows.astype(jnp.float32)).astype(jnp.bfloat16)
     return (
         output,
         grad_tokens,
-        sum_gains[0, :gain_part],
+        sum_gains[0],
         sum_query,
         sum_kv[:, :kv_width],
         sum_kv[:, kv_width:],
         sum_out,
-        sum_gains[8, :gain_part],
+        sum_gains[8],
         sum_gate,
         sum_up,
         sum_down,

time: 690 us -> 552 us (0.80)
  Pallas kernels: 575 us -> 496 us
  matrix products: 46.1 us -> 3.33 us
  local copies, waits for them, and re-layouts: 27.6 us -> 17.9 us
    pallas_call x6 -> x3, Pallas kernels: 513 us -> 437 us  [the longest x1 180 us: front(): pl.pallas_call(functools.partial(front_kernel, specs, kv_spec, group_head...]
    dot_general x6 -> x0, matrix products: 30.2 us -> none  [the longest x3 15.6 us: product(): return jnp.dot(left, right, preferred_element_type=jnp.float32)]
    dot_general x3 -> x1, matrix products: 15.9 us -> 3.33 us  [product_right(): lax.dot_general(left, right, (((1,), (1,)), ((), ())), preferred_element_...]
    slice x9 -> x1, local copies, waits for them, and re-layouts: 9.17 us -> 1.53 us  [on_device(): gain_first, gain_second = (gain_rows[0], gain_rows[1])]
  transfers between devices with their start and end apart: 2 -> 1, of which waited for: 0 -> 0; matrix products, arithmetic and copies ran while one was open for 11% -> 2% of each run, Pallas kernels for 50% -> 32%
where the time goes in v4:
time: 552 us; the launch traced here: 544 us
  Pallas kernels  496 us (90%)
  local copies, waits for them, and re-layouts  17.9 us (3%)
  between operations  14.6 us (3%)
  other arithmetic  11.8 us (2%)
    pallas_call x1, Pallas kernels, front(): pl.pallas_call(functools.partial(front_kernel, specs, kv_spec, group_head...  180 us
    pallas_call x1, Pallas kernels, feed_forward(): pl.pallas_call(functools.partial(mlp_kernel, specs, dp_size, tensor_size)...  144 us
    pallas_call x1, Pallas kernels, tail(): pl.pallas_call(functools.partial(tail_kernel, specs, dp_size, tensor_size...  113 us
    pallas_call x1, Pallas kernels, attend_back(): pl.pallas_call(functools.partial(attend_back_kernel, group_pairs, pairs,...  59.1 us
    unnamed x28, local copies, waits for them, and re-layouts  12 us
  transfers between devices with their start and end apart: 1, of which 0 were waited for; matrix products, arithmetic and copies ran while one was open for 2% of the time, Pallas kernels for 32%

profile of v4, /device:TPU:25, one launch (start us, length us, event | category | flops | bytes accessed | tf_op | source)
XLA Modules:
  0.0 544.1 jit_solution(11302470601526036238)
XLA Ops:
  7.2 0.0 reduce-scatter.2.cloned.1.call-start
  7.3 0.7 tile.20
  7.9 0.1 tile.21
  8.0 0.7 tile.8
  8.7 0.1 tile.9
  8.8 0.5 fusion
  9.3 1.4 pad_maximum_fusion.3.refs_3_
  10.7 1.0 pad_maximum_fusion.1
  11.7 0.7 and_select_fusion.refs_4_
  12.4 180.2 %shard_map.194 = (bf16[256,2048]{1,0:T(8,128)(2,1)}, bf16[256,2048]{1,0:T(8,128)(2,1)}, f32[16,2,256]{2,1,0:T(2,128)}, bf16[256,2048]{1,0:T(8,128)(2,1)}, bf16[2...) custom-call(bf16[256,2048]{1,0:T(8,128)(2,1)} %refs_5_.3, ...), custom_call_target="tpu_custom_call" | custom-call | tf_op jit(solution)/shard_map/pallas_call | solution.py:762
  192.6 144.2 %shard_map.195 = (f32[256,2048]{1,0:T(8,128)}, bf16[4,256,2048]{2,1,0:T(8,128)(2,1)}, bf16[2048,1408]{1,0:T(8,128)(2,1)}, bf16[2048,1408]{1,0:T(8,128)(2,1)}, f32[1408,256]{1,0:T(8,128)}) custom-call(bf16[256,2048]{1,0:T(8,128)(2,1)} %get-tuple-element.45.normed_ref, bf16[4,256,2048]{2,1,0:T(8,128)(2,1)} %bitcast.16, ...), custom_call_target="tpu_custom_call" | custom-call | flops 53150220288 | bytes 23068672 | tf_op jit(solution)/shard_map/pallas_call | solution.py:1144
  336.8 0.0 copy-start
  336.8 0.0 reduce-scatter.2.cloned.1.call-update
  336.8 0.0 copy-start.1
  336.8 1.5 copy-done
  338.4 0.2 multiply_reduce_fusion.2
  338.6 1.5 fusion.3
  340.1 0.0 copy-done.1
  340.1 0.0 copy-start.2
  340.1 1.1 multiply_reduce_fusion
  341.3 0.1 copy-done.2
  341.4 0.0 copy-start.10
  341.4 1.9 fusion.1
  343.3 0.0 copy-start.3
  343.3 3.3 copy-done.10
  346.6 3.3 convolution_convert_fusion.refs_1_
  350.0 0.0 copy-done.3
  350.0 59.1 %shard_map.196 = (bf16[256,2048]{1,0:T(8,128)(2,1)}, bf16[1024,256]{1,0:T(8,128)(2,1)}, bf16[1024,256]{1,0:T(8,128)(2,1)}, f32[256,1408]{1,0:T(8,128)}, f32[256,1408]{1,0:T(8,128)}) custom-call(bf16[256,2048]{1,0:T(8,128)(2,1)} %get-tuple-element.55.refs_0_, bf16[256,2048]{1,0:T(8,128)(2,1)} %convolution_convert_fusion.refs_1_, ...), custom_call_target="tpu_custom_call" | custom-call | flops 5368709120 | bytes 4194304 | tf_op jit(solution)/shard_map/pallas_call | solution.py:887
  409.1 2.2 pad_maximum_fusion
  411.3 112.9 %shard_map.197 = (f32[256,2048]{1,0:T(8,128)}, f32[512,256]{1,0:T(8,128)}, f32[256,512]{1,0:T(8,128)}, f32[64,512]{1,0:T(8,128)}, f32[16,256]{1,0:T(8,128)}) custom-call(bf16[256,2048]{1,0:T(8,128)(2,1)} %get-tuple-element.51.refs_0_, bf16[256,2048]{1,0:T(8,128)(2,1)} %copy-done.3, bf16[256,2048]{1,0:T(8,128)(2,1)} %get-tuple-element.54.refs_2_, ...), custom_call_target="tpu_custom_call" | custom-call | tf_op jit(solution)/shard_map/pallas_call | solution.py:1367
  524.3 1.3 dynamic-slice_bitcast_fusion
  525.6 1.5 fusion.2
  527.1 0.0 reduce-scatter.2.cloned.1.call-done
  527.1 0.0 copy-start.4
  527.1 2.6 add_convert_fusion
  529.7 0.0 copy-done.4
  529.7 0.0 copy-start.9
  529.7 1.3 copy.29
  531.1 0.1 copy-done.9
  531.1 0.8 copy.30
  531.9 0.0 copy-done.8
  531.9 0.8 copy.31
  532.7 0.0 copy-done.7
  532.7 1.1 copy.32
  533.8 0.0 copy-done.6
  533.8 1.1 copy.33
  534.9 0.8 copy-done.5
  535.7 1.1 copy.34
  (10 shorter events, 0.0 us)
Async XLA Ops:
  7.2 519.9 %reduce-scatter.2.cloned.1.call-start = ((), (), s32[]{:S(2)}) async-start(), calls=%async_computation.1 | async-start | bytes 5242880 | tf_op jit(solution)/shard_map/reduce_scatter | solution.py:1568
  336.8 1.6 copy-start
  336.8 3.3 copy-start.1
  340.1 1.2 copy-start.2
  341.4 5.3 copy-start.10
  343.3 6.7 %copy-start.3 = (bf16[256,2048]{1,0:T(8,128)(2,1)}, bf16[256,2048]{1,0:T(8,128)(2,1)S(1)}, u32[]{:S(2)}) copy-start(bf16[256,2048]{1,0:T(8,128)(2,1)S(1)} %get-tuple-element.79.refs_1_) | copy-start | bytes 3145732
  527.1 2.6 copy-start.4
  529.7 1.4 copy-start.9
  529.7 2.2 copy-start.8
  531.1 1.6 copy-start.7
  531.9 1.9 copy-start.6
  533.8 1.9 copy-start.5
Sparse Core Ops, SparseCore 0:
  336.9 77.4 reduce-scatter.1

commit v5 on v4

--- a/solution.py
+++ b/solution.py
@@ -31,13 +31,6 @@
 def product_right(left, right):
     return lax.dot_general(
         left, right, (((1,), (1,)), ((), ())), preferred_element_type=jnp.float32
-    )
-
-
-def norm_back(grad_normed, unit_rows, scale_rows, gain):
-    scaled_grad = grad_normed * gain
-    return scale_rows * (
-        scaled_grad - unit_rows * jnp.mean(scaled_grad * unit_rows, axis=-1, keepdims=True)
     )
 
 
@@ -82,8 +75,9 @@
 
 
 class Gather:
-    def __init__(self, shape, slot, half=None, line=True):
+    def __init__(self, shape, slot, half=None, line=True, pieces=1):
         self.shape, self.slot, self.half, self.line = shape, slot, half, line
+        self.pieces = pieces
 
 
 class GatherRun:
@@ -95,8 +89,10 @@
         self.order = orders(self.dp_bits, True)
         self.hyper = [i for i, spec in enumerate(specs) if spec.half is not None]
         self.lines = [i for i, spec in enumerate(specs) if spec.line]
-        self.early = [n for n, i in enumerate(self.hyper) if not specs[i].line]
-        self.late = [n for n, i in enumerate(self.hyper) if specs[i].line]
+        self.base, total = {}, 0
+        for i in self.hyper:
+            self.base[i] = total
+            total += specs[i].pieces
         self.can = [self.tensor + 1 < tensor_size, self.tensor > 0]
 
     def greet(self):
@@ -126,23 +122,6 @@
         for way in (0, 1):
             pl.when(self.can[way])(self.z_copy(i, self.tensor, way, self.sources[i]).start)
 
-    def begin(self, slow=()):
-        loads = [
-            pltpu.make_async_copy(source, held, self.own_sem.at[i])
-            for i, (source, held) in enumerate(zip(self.sources, self.held))
-        ]
-        for load in loads:
-            load.start()
-        for i in self.lines:
-            if i not in slow:
-                self.begin_line(i)
-        for i, load in enumerate(loads):
-            load.wait()
-            self.own(i).start()
-        for n in self.early:
-            self.own(self.hyper[n]).wait()
-            self.hop(n, 0)
-
     def line(self, i, step):
         for way, block in ((0, self.tensor - step), (1, self.tensor + step)):
 
@@ -151,41 +130,54 @@
                 self.z_copy(i, block, way).wait_recv()
                 pl.when(self.can[way])(self.z_copy(i, block, way).start)
 
-    def part(self, n, half, rank):
-        i = self.hyper[n]
-        return self.specs[i].half(self.outs[i], masked(self.dp, self.order[half], rank), half)
-
-    def h_copy(self, n, half, rank, place):
+    def part(self, i, half, rank, piece):
+        place = masked(self.dp, self.order[half], rank)
+        return self.specs[i].half(self.outs[i], place, half, piece)
+
+    def h_copy(self, i, half, rank, place, piece):
+        n = self.base[i] + piece
         return pltpu.make_async_remote_copy(
-            src_ref=self.part(n, half, rank),
-            dst_ref=self.part(n, half, rank),
+            src_ref=self.part(i, half, rank, piece),
+            dst_ref=self.part(i, half, rank, piece),
             send_sem=self.h_send.at[n, half, rank, place],
             recv_sem=self.h_recv.at[n, half, rank | 1 << place],
             device_id=(flip(self.dp, self.order[half][place]), self.tensor),
             device_id_type=MESH,
         )
 
-    def hop(self, n, rank):
+    def hop(self, i, rank, piece=0):
+        n = self.base[i] + piece
         for half in (0, 1):
             if rank:
                 wait_part(
-                    self.part(n, half, rank),
+                    self.part(i, half, rank, piece),
                     self.h_recv.at[n, half, rank],
                     self.h_send.at[n, half, 0, 0],
                     (flip(self.dp, 0), self.tensor),
                 )
             for place in range(rank.bit_length(), self.dp_bits):
-                self.h_copy(n, half, rank, place).start()
+                self.h_copy(i, half, rank, place, piece).start()
+
+    def hop_from(self, i, rank, step):
+        if step == 0:
+            self.hop(i, rank, self.tensor)
+            return
+        for block in (self.tensor - step, self.tensor + step):
+
+            @pl.when((block >= 0) & (block < self.tensor_size))
+            def _():
+                self.hop(i, rank, block)
 
     def end_line(self, i):
         self.own(i).wait()
 
     def close(self):
         for rank in range(1 << self.dp_bits):
-            for n in range(len(self.hyper)):
-                for half in (0, 1):
-                    for place in range(rank.bit_length(), self.dp_bits):
-                        self.h_copy(n, half, rank, place).wait_send()
+            for i in self.hyper:
+                for piece in range(self.specs[i].pieces):
+                    for half in (0, 1):
+                        for place in range(rank.bit_length(), self.dp_bits):
+                            self.h_copy(i, half, rank, place, piece).wait_send()
         for i in self.lines:
             for block in range(self.tensor_size):
                 for way in (0, 1):
@@ -197,7 +189,7 @@
 
 def gather_scratch(specs, arrays, dp_size, tensor_size):
     count = len(specs)
-    hyper = max(1, sum(spec.half is not None for spec in specs))
+    hyper = max(1, sum(spec.pieces for spec in specs if spec.half is not None))
     dp_bits = dp_size.bit_length() - 1
     return [pltpu.VMEM(array.shape, array.dtype) for array in arrays], [
         pltpu.SemaphoreType.DMA((count,)),
@@ -238,12 +230,10 @@
 
         def body(step, carry):
             at = pl.ds(pl.multiple_of(step * slab, slab), slab)
-            total[at, :] = (
-                total[at, :].astype(jnp.float32) + extra[at, :].astype(jnp.float32)
-            ).astype(total.dtype)
+            total[at, :] = total[at, :] + extra[at, :]
             return carry
 
-        lax.fori_loop(0, rows // slab, body, 0, unroll=2 if (rows // slab) % 2 == 0 else 1)
+        lax.fori_loop(0, rows // slab, body, 0, unroll=4 if (rows // slab) % 4 == 0 else 1)
     else:
         for lead in range(shape[0]):
             add_into(total.at[lead], extra.at[lead])
@@ -408,18 +398,6 @@
     for i, spec in enumerate(specs):
         units += [(i, j) for j in range(tensor_size)] if spec.kind == "own" else [(i, None)]
     return units
-
-
-def scatter_kernel(specs, dp_size, tensor_size, *refs):
-    count = len(specs)
-    run = ScatterRun(
-        specs, dp_size, tensor_size, refs[:count], refs[count : 2 * count], refs[2 * count :]
-    )
-    run.greet()
-    run.begin()
-    for unit, stage in run.steps():
-        run.step(unit, stage)
-    run.close()
 
 
 def scatter_scratch(specs, arrays, dp_size, tensor_size, in_place=False):
@@ -452,20 +430,6 @@
     return [jax.ShapeDtypeStruct(spec.shape, jnp.float32) for spec in specs]
 
 
-def scatter(specs, arrays, dp_size, tensor_size, collective_id):
-    count = len(specs)
-    return pl.pallas_call(
-        functools.partial(scatter_kernel, specs, dp_size, tensor_size),
-        out_shape=scatter_shapes(specs),
-        in_specs=[ANY] * count,
-        out_specs=[VMEM] * count,
-        scratch_shapes=scatter_scratch(specs, arrays, dp_size, tensor_size),
-        compiler_params=pltpu.CompilerParams(
-            collective_id=collective_id, has_side_effects=True, vmem_limit_bytes=VMEM_LIMIT
-        ),
-    )(*arrays)
-
-
 class ExchangeRun:
     def __init__(self, tensor_size, source, out, own_sem, send, recv):
         self.tensor_size, self.source, self.out = tensor_size, source, out
@@ -574,7 +538,7 @@
     context[:, at] = jnp.concatenate(contexts, axis=0).T.astype(jnp.bfloat16)
 
 
-def front_kernel(specs, kv_spec, group_pairs, dp_size, tensor_size, *refs):
+def front_kernel(specs, kv_spec, n_spec, group_pairs, dp_size, tensor_size, *refs):
     refs = list(refs)
 
     def take(count):
@@ -583,14 +547,15 @@
     count = len(specs)
     tokens, cos_ref, sin_ref = take(3)
     sources = take(count)
-    context, queries, lse_ref, normed, normed_two, middle, gain_rows, kv_all = take(8)
+    context, queries, lse_ref, normed, middle, gain_rows, kv_all, normed_all = take(8)
     outs = take(count)
     held = take(count)
-    weights, kv_weights, gain_blocks, q_pre, k_left, v_turned = take(6)
+    weights, kv_weights, gain_blocks, q_pre, k_left, v_turned, normed_two = take(7)
     sems = take(5)
     kv_sems = take(5)
+    n_sems = take(5)
     (load_sem,) = take(1)
-    key_value, gains, query, out, gate, up, down, cot = range(count)
+    key_value, gains, query, out, gate, up, cot = range(count)
     run = GatherRun(specs, dp_size, tensor_size, sources, outs, held, sems)
     rows, width = tokens.shape
     own_rows = pl.ds(pl.multiple_of(run.tensor * rows, rows), rows)
@@ -603,10 +568,19 @@
     far.sort(key=lambda rank: rank.bit_count())
     core = list(range(1 << (run.dp_bits - 1), 1 << run.dp_bits))
 
+    n_run = GatherRun(
+        [n_spec], dp_size, tensor_size, [normed_two], [normed_all], [normed_two], n_sems
+    )
+
     def hops(ranks, *units):
         for unit in units:
             for rank in ranks:
                 run.hop(unit, rank)
+
+    def query_hops(ranks, *steps):
+        for step in steps:
+            for rank in ranks:
+                run.hop_from(query, rank, step)
 
     run.greet()
     loads = [
@@ -615,34 +589,32 @@
     ]
     for load in loads:
         load.start()
-    first = (key_value, gains, query)
-    for i in first:
+    small = (key_value, gains)
+    for i in (*small, query):
         run.begin_line(i)
-    for i, load in enumerate(loads):
-        load.wait()
+    for i in (query, key_value, gains, out, gate, up, cot):
+        loads[i].wait()
         run.own(i).start()
-    run.end_line(gate)
-    hops([0], gate)
+        if i == query:
+            run.end_line(query)
+            query_hops([0], 0)
     for step in range(1, tensor_size):
-        for i in first:
+        for i in small:
             run.line(i, step)
-        if step == tensor_size // 2:
-            hops(near, gate)
-    for i in first:
+    for i in small:
         run.end_line(i)
-    hops([0], *first)
+    hops([0], *small)
+    steps = range(1, tensor_size)
+    for step in steps:
+        run.line(query, step)
+        query_hops([0], step)
+        if step == max(1, tensor_size - 2):
+            hops(near, *small)
     run.begin_line(out)
-    hops(far, gate)
-    for step in range(1, tensor_size):
-        run.line(out, step)
     run.begin_line(cot)
-    hops(near, key_value, gains)
-    hops(far, key_value, gains)
-    hops(near, query)
-    for i in (out, up, down):
-        run.end_line(i)
-    hops([0], out)
-    hops(core, key_value, gains)
+    hops(far, *small)
+    hops(core, *small)
+    run.line(out, 1)
 
     kv_load = pltpu.make_async_copy(outs[key_value], kv_weights, load_sem.at[0])
     kv_load.start()
@@ -678,33 +650,41 @@
     kv_all[own_rows, :] = jnp.concatenate([own_keys, own_kv[:, kv_width:]], axis=1).astype(
         kv_all.dtype
     )
-    run.line(cot, 1)
     kv_run.begin_line(0)
-    hops(far, query)
-    hops(core, query)
-    hops([0], up)
+    query_hops(near, 0, *steps)
+    kv_run.line(0, 1)
+    query_hops(far, 0, *steps)
+    for step in steps[1:-1]:
+        run.line(out, step)
+        kv_run.line(0, step)
+    query_hops(core, 0, *steps)
     query_load = pltpu.make_async_copy(outs[query], weights, load_sem.at[0])
     query_load.start()
+    for step in steps[-1:]:
+        run.line(out, step)
+    for i in (out, gate, up):
+        run.end_line(i)
+    hops([0], out)
     query_load.wait()
-    tiles = max(4, tensor_size)
+    tiles = 4
     tile = width // tiles
     for j in range(tiles):
         columns = slice(j * tile, (j + 1) * tile)
         q_pre[:, columns] = product(normed[...], weights[:, columns])
-        if 1 <= j < tensor_size:
-            kv_run.line(0, j)
-    assert tiles >= tensor_size
+        if j == 1:
+            for step in steps[-1:]:
+                kv_run.line(0, step)
     pairs = lse_ref.shape[0]
     plan = [
-        (0.1, lambda: hops(near, out)),
-        (0.3, lambda: hops(far, out)),
-        (0.3, lambda: hops([0], down)),
-        (0.55, lambda: hops(near, up)),
-        (0.8, lambda: hops(far, up)),
+        (0.3, lambda: hops(near, out)),
+        (0.31, lambda: hops([0], gate)),
+        (0.75, lambda: hops(far, out)),
+        (0.88, lambda: hops(near, gate)),
+        (0.89, lambda: hops([0], up)),
     ]
-    for step in range(2, tensor_size):
-        time = 0.05 + 0.6 * (step - 2) / max(1, tensor_size - 3)
-        plan.append((time, functools.partial(run.line, cot, step)))
+    early = max(1, tensor_size - 2)
+    for step in steps[:early]:
+        plan.append((0.2 + 0.75 * (step - 1) / early, functools.partial(run.line, cot, step)))
     plan.sort(key=lambda entry: entry[0])
 
     def pair_step(pair, carry):
@@ -726,7 +706,6 @@
     hops(core, out)
     out_load = pltpu.make_async_copy(outs[out], weights, load_sem.at[0])
     out_load.start()
-    hops(near, down)
     out_load.wait()
     for j in range(4):
         columns = slice(j * (width // 4), (j + 1) * (width // 4))
@@ -742,38 +721,52 @@
         return carry
 
     lax.fori_loop(0, rows // slab, norm_second, 0)
-    hops(far, down)
-    hops(core, gate, up, down)
+    n_run.begin_line(0)
+    n_run.own(0).start()
+    hops(far, gate)
+    for step in steps[early:]:
+        run.line(cot, step)
+    hops(near, up)
+    hops(core, gate)
+    hops(far, up)
+    hops(core, up)
+    for way, block in ((0, run.tensor - 1), (1, run.tensor + 1)):
+        arrives = (block >= 0) & (block < tensor_size)
+        pl.when(arrives)(n_run.z_copy(0, block, way).wait_recv)
+        pl.when(run.can[way])(n_run.z_copy(0, run.tensor, way, normed_two).wait_send)
+    n_run.end_line(0)
     run.end_line(cot)
     run.close()
     kv_run.close()
 
 
-def front(tokens, cosines, sines, arrays, specs, kv_spec, heads, group_heads, sizes, collective_id):
+def front(
+    tokens, cosines, sines, arrays, specs, kv_spec, n_spec, heads, group_heads, sizes, collective_id
+):
     dp_size, tensor_size = sizes
     rows, width = tokens.shape
     length = rows * tensor_size
     low, full = jnp.bfloat16, jnp.float32
     held, sems = gather_scratch(specs, arrays, *sizes)
-    _, kv_sems = gather_scratch([kv_spec], [], *sizes)
+    _, line_sems = gather_scratch([kv_spec], [], *sizes)
     kv_both = specs[0].shape[1]
     pairs = heads // 2
     tokens_low = jax.ShapeDtypeStruct((rows, width), low)
     return pl.pallas_call(
-        functools.partial(front_kernel, specs, kv_spec, group_heads // 2, *sizes),
+        functools.partial(front_kernel, specs, kv_spec, n_spec, group_heads // 2, *sizes),
         out_shape=[
             tokens_low,
             tokens_low,
             jax.ShapeDtypeStruct((pairs, 2, rows), full),
             tokens_low,
-            tokens_low,
             jax.ShapeDtypeStruct((rows, width), full),
             jax.ShapeDtypeStruct((8, width), full),
             jax.ShapeDtypeStruct((length, kv_both), low),
+            jax.ShapeDtypeStruct((length, width), low),
         ]
         + gather_shapes(specs, arrays),
         in_specs=[VMEM] * 3 + [ANY] * len(specs),
-        out_specs=[VMEM] * 8 + [ANY] * len(specs),
+        out_specs=[VMEM] * 7 + [ANY] * (1 + len(specs)),
         scratch_shapes=held
         + [
             pltpu.VMEM((width, width), low),
@@ -782,9 +775,11 @@
             pltpu.VMEM((rows, width), full),
             pltpu.VMEM((length, 128), low),
             pltpu.VMEM((HEAD_DIM, length), low),
+            pltpu.VMEM((rows, width), low),
         ]
         + sems
-        + kv_sems
+        + line_sems
+        + line_sems
         + [pltpu.SemaphoreType.DMA((2,))],
         compiler_params=pltpu.CompilerParams(
             collective_id=collective_id, has_side_effects=True, vmem_limit_bytes=VMEM_LIMIT
@@ -794,19 +789,22 @@
 
 def scatter_plan(run):
     plan = [(0.0, run.greet), (0.0, run.begin)]
+    times = [(0.12, 0.08), (0.55, 0.3), (0.88, 0.12), (0.95, 0.05)]
     for unit, stage in run.steps():
-        time = 0.15 + 0.1 * unit if stage == 0 else 0.55 + 0.35 * unit if stage == 1 else 1.0
-        plan.append((min(time, 1.0), functools.partial(run.step, unit, stage)))
+        first, behind = times[min(stage, len(times) - 1)]
+        plan.append((min(first + behind * unit, 1.0), functools.partial(run.step, unit, stage)))
+    plan.sort(key=lambda entry: entry[0])
     return plan + [(1.0, run.close)]
 
 
 def attend_back_kernel(group_pairs, pairs, specs, dp_size, tensor_size, *refs):
     refs = list(refs)
-    q_ref, do_ref, lse_ref, cos_ref, sin_ref, k_ref, v_ref = (refs.pop(0) for _ in range(7))
+    q_ref, out_ref, lse_ref, cos_ref, sin_ref, k_ref, v_ref = (refs.pop(0) for _ in range(7))
+    back_ref, middle_ref, cot_ref, gain_ref = (refs.pop(0) for _ in range(4))
     sources = [refs.pop(0) for _ in specs]
-    dq_ref, dk_ref, dv_ref = (refs.pop(0) for _ in range(3))
+    dq_ref, dk_ref, dv_ref, grad_middle, middle_low, gain_sum = (refs.pop(0) for _ in range(6))
     outs = [refs.pop(0) for _ in specs]
-    k_left, v_left, k_turned, dk_sum, dv_sum = (refs.pop(0) for _ in range(5))
+    k_left, v_left, k_turned, dk_sum, dv_sum, column_sum = (refs.pop(0) for _ in range(6))
     run = ScatterRun(specs, dp_size, tensor_size, sources, outs, refs)
     plan = scatter_plan(run)
     at_steps([entry for entry in plan if entry[0] < 1.0], pl.program_id(0), pairs)
@@ -816,6 +814,31 @@
     rows = q_ref.shape[0]
     start = lax.axis_index("tensor") * rows
 
+    @pl.when(pair == 0)
+    def _():
+        slab = 16
+        column_sum[...] = jnp.zeros_like(column_sum)
+
+        def norm_slab(step, carry):
+            at = pl.ds(pl.multiple_of(step * slab, slab), slab)
+            raw = middle_ref[at, :]
+            scale = lax.rsqrt(jnp.mean(raw * raw, axis=-1, keepdims=True) + epsilon)
+            unit = raw * scale
+            grad = back_ref[at, :]
+            gained = grad * unit
+            column_sum[...] += gained[:8] + gained[8:]
+            scaled = grad * gain_ref[...]
+            mean = jnp.mean(scaled * unit, axis=-1, keepdims=True)
+            total = cot_ref[at, :].astype(jnp.float32) + scale * (scaled - unit * mean)
+            grad_middle[at, :] = total
+            middle_low[at, :] = total.astype(middle_low.dtype)
+            return carry
+
+        lax.fori_loop(0, rows // slab, norm_slab, 0)
+        gain_sum[...] = jnp.sum(column_sum[...], axis=0, keepdims=True)
+
+    grad_context = product_right(middle_low[...], out_ref[...])
+
     @pl.when(pair % group_pairs == 0)
     def _():
         left = left_head(k_ref[...].astype(jnp.float32), odd)
@@ -828,10 +851,10 @@
     open_at = allowed(k_left.shape[0], rows, start)
     grads = []
     for head in (0, 1):
-        queries, grad_out = q_ref[...], do_ref[...]
+        queries, grad_out = q_ref[...], grad_context.astype(jnp.bfloat16)
         if head == 1:
             queries = pltpu.roll(queries.astype(jnp.float32), HEAD_DIM, 1).astype(jnp.bfloat16)
-            grad_out = pltpu.roll(grad_out.astype(jnp.float32), HEAD_DIM, 1).astype(jnp.bfloat16)
+            grad_out = pltpu.roll(grad_context, HEAD_DIM, 1).astype(jnp.bfloat16)
         scores = product_right(k_left[...], queries)
         scores = jnp.where(open_at, scores, -1e30)
         softmaxed = jnp.exp(scores - lse_ref[0, head, :][None, :])
@@ -865,11 +888,15 @@
 
 def attend_back(
     queries,
-    grad_context,
+    out_full,
     lse,
     cosines,
     sines,
     keys_values,
+    back,
+    middle,
+    cotangent,
+    gain,
     head_count,
     group_heads,
     specs,
@@ -881,6 +908,7 @@
     length, both = keys_values.shape
     pairs, group_pairs = head_count // 2, group_heads // 2
     kv_blocks = both // 256
+    low, full = jnp.bfloat16, jnp.float32
     wide = pl.BlockSpec((rows, 128), lambda p: (0, p))
     table = pl.BlockSpec((rows, 128), lambda p: (0, 0))
     kv_out = pl.BlockSpec((length, 128), lambda p: (0, p // group_pairs // 2))
@@ -888,28 +916,33 @@
         functools.partial(attend_back_kernel, group_pairs, pairs, specs, *sizes),
         grid=(pairs,),
         out_shape=[
-            jax.ShapeDtypeStruct((rows, width), jnp.bfloat16),
-            jax.ShapeDtypeStruct((length, both // 2), jnp.bfloat16),
-            jax.ShapeDtypeStruct((length, both // 2), jnp.bfloat16),
+            jax.ShapeDtypeStruct((rows, width), low),
+            jax.ShapeDtypeStruct((length, both // 2), low),
+            jax.ShapeDtypeStruct((length, both // 2), low),
+            jax.ShapeDtypeStruct((rows, width), full),
+            jax.ShapeDtypeStruct((rows, width), low),
+            jax.ShapeDtypeStruct((1, width), full),
         ]
         + scatter_shapes(specs),
         in_specs=[
             wide,
-            wide,
+            pl.BlockSpec((128, width), lambda p: (p, 0)),
             pl.BlockSpec((1, 2, rows), lambda p: (p, 0, 0)),
             table,
             table,
             pl.BlockSpec((length, 128), lambda p: (0, p // group_pairs // 2)),
             pl.BlockSpec((length, 128), lambda p: (0, kv_blocks + p // group_pairs // 2)),
         ]
+        + [VMEM] * 4
         + [ANY] * len(specs),
-        out_specs=[wide, kv_out, kv_out] + [VMEM] * len(specs),
+        out_specs=[wide, kv_out, kv_out] + [VMEM] * (3 + len(specs)),
         scratch_shapes=[
-            pltpu.VMEM((length, 128), jnp.bfloat16),
-            pltpu.VMEM((length, 128), jnp.bfloat16),
-            pltpu.VMEM((HEAD_DIM, length), jnp.bfloat16),
-            pltpu.VMEM((length, 128), jnp.float32),
-            pltpu.VMEM((length, 128), jnp.float32),
+            pltpu.VMEM((length, 128), low),
+            pltpu.VMEM((length, 128), low),
+            pltpu.VMEM((HEAD_DIM, length), low),
+            pltpu.VMEM((length, 128), full),
+            pltpu.VMEM((length, 128), full),
+            pltpu.VMEM((8, width), full),
         ]
         + scatter_scratch(specs, arrays, *sizes),
         compiler_params=pltpu.CompilerParams(
@@ -918,17 +951,32 @@
         cost_estimate=pl.CostEstimate(
             flops=10 * rows * length * width, bytes_accessed=8 * rows * width, transcendentals=0
         ),
-    )(queries, grad_context, lse, cosines, sines, keys_values, keys_values, *arrays)
+    )(
+        queries,
+        out_full,
+        lse,
+        cosines,
+        sines,
+        keys_values,
+        keys_values,
+        back,
+        middle,
+        cotangent,
+        gain,
+        *arrays,
+    )
 
 
 def block_at(place, tensor, tensor_size):
     above = tensor_size - 1 - tensor
-    up = jnp.where(place <= above, tensor + place, tensor - (place - above))
-    down = jnp.where(place <= tensor, tensor - place, place)
-    return jnp.where(tensor <= above, up, down)
+    up = jnp.where(place < above, tensor + 1 + place, tensor - 1 - (place - above))
+    down = jnp.where(place < tensor, tensor - 1 - place, 1 + place)
+    other = jnp.where(tensor <= above, up, down)
+    return jnp.where(place == tensor_size - 1, tensor, other)
 
 
 def mlp_kernel(
+    gather_specs,
     specs,
     dp_size,
     tensor_size,
@@ -960,30 +1008,42 @@
     b_send,
     b_recv,
     out_sem,
-    *scatter_refs,
+    *more_refs,
 ):
     run = ScatterRun(
-        specs, dp_size, tensor_size, [down], [down_sum], scatter_refs, in_place=True
+        specs, dp_size, tensor_size, [down], [down_sum], more_refs[5:], in_place=True
+    )
+    down_run = GatherRun(
+        gather_specs, dp_size, tensor_size, [down_ref], [down], [down_ref], more_refs[:5]
     )
     dp, tensor = lax.axis_index("dp"), lax.axis_index("tensor")
-    rows, width = normed_ref.shape
+    _, rows, width = normed_ref.shape
     units = gate.shape[1]
     loads = [
         pltpu.make_async_copy(source, target, load_sem.at[i])
-        for i, (source, target) in enumerate(
-            (
-                (normed_ref, normed.at[tensor]),
-                (gate_ref, gate),
-                (up_ref, up),
-                (down_ref, down),
-                (cot_ref, cot),
-            )
+        for i, (source, target) in enumerate(((gate_ref, gate), (up_ref, up), (cot_ref, cot)))
+    ]
+    has = [tensor + 1 < tensor_size, tensor > 0]
+
+    def near_load(step):
+        block = tensor + step
+        return pltpu.make_async_copy(
+            normed_ref.at[block], normed.at[block], load_sem.at[4 + step]
         )
-    ]
+
+    def near_loads(act):
+        act(near_load(0))
+        for way, step in ((0, 1), (1, -1)):
+
+            @pl.when(has[way])
+            def _():
+                act(near_load(step))
+
+    near_loads(lambda load: load.start())
+    down_run.own(0).start()
     for load in loads:
         load.start()
     greet((dp, tensor, tensor_size), False, True, run.dp_bits)
-    has = [tensor + 1 < tensor_size, tensor > 0]
 
     def n_copy(block, way, source=None):
         return pltpu.make_async_remote_copy(
@@ -995,8 +1055,11 @@
             device_id_type=MESH,
         )
 
-    for way in (0, 1):
-        pl.when(has[way])(n_copy(tensor, way, normed_ref).start)
+    for way, step in ((0, -1), (1, 1)):
+        both = has[0] & has[1]
+        pl.when(both)(n_copy(tensor + step, way, normed_ref.at[tensor + step]).start)
+    down_run.end_line(0)
+    down_run.hop(0, 0)
     landing[tensor] = jnp.zeros((rows, width), landing.dtype)
 
     def pump(distance):
@@ -1008,6 +1071,11 @@
                 pl.when(has[way])(n_copy(block, way).start)
 
     farthest = jnp.maximum(tensor, tensor_size - 1 - tensor)
+    core_rank = 1 << (run.dp_bits - 1)
+    down_ranks = [
+        sorted(range(1, core_rank), key=lambda rank: rank.bit_count()),
+        range(core_rank, 2 * core_rank),
+    ]
 
     def b_copy(block, slot):
         return pltpu.make_async_remote_copy(
@@ -1022,24 +1090,29 @@
     def y_copy(block, slot):
         return pltpu.make_async_copy(y_stage.at[slot], y_ref.at[block], y_sem.at[slot])
 
-    for load in loads[:3]:
+    for load in loads:
         load.wait()
+    near_loads(lambda load: load.wait())
 
     def chunk(place, carry):
         block = block_at(place, tensor, tensor_size)
-
-        @pl.when((place >= 1) & (place <= farthest))
-        def _():
-            pump(place)
-
         rows_in = normed[block]
         gate_pre = product(rows_in, gate[...])
         upward = product(rows_in, up[...])
 
         @pl.when(place == 0)
         def _():
-            for load in loads[3:]:
-                load.wait()
+            for rank in down_ranks[0]:
+                down_run.hop(0, rank)
+
+        @pl.when(place + 2 <= farthest)
+        def _():
+            pump(place + 2)
+
+        @pl.when(place == 0)
+        def _():
+            for rank in down_ranks[1]:
+                down_run.hop(0, rank)
 
         sigmoid = 1.0 / (1.0 + jnp.exp(-gate_pre))
         silu = gate_pre * sigmoid
@@ -1091,6 +1164,7 @@
 
         lax.fori_loop(0, extent // tile, body, 0)
 
+    down_run.close()
     weight_grad(hidden, cot, down)
     run.begin_unit(0)
     weight_grad(normed, d_gate, gate)
@@ -1129,20 +1203,22 @@
             b_copy(other, tensor).wait_send()
 
         for way in (0, 1):
-            sent = has[way] & ((other <= tensor) if way == 0 else (other >= tensor))
+            sent = has[way] & ((other < tensor) if way == 0 else (other > tensor))
             pl.when(sent)(n_copy(other, way).wait_send)
 
 
-def feed_forward(normed, cot_all, gate, up, down, specs, sizes, collective_id):
+def feed_forward(
+    normed, cot_all, gate, up, down, gather_specs, specs, sizes, collective_id
+):
     dp_size, tensor_size = sizes
-    rows, width = normed.shape
+    rows, width = normed.shape[0] // tensor_size, normed.shape[1]
     units = gate.shape[1]
     low = jnp.bfloat16
     tokens = (tensor_size, rows, width)
     inner = (tensor_size, rows, units)
     dma = pltpu.SemaphoreType.DMA
     return pl.pallas_call(
-        functools.partial(mlp_kernel, specs, dp_size, tensor_size),
+        functools.partial(mlp_kernel, gather_specs, specs, dp_size, tensor_size),
         out_shape=[
             jax.ShapeDtypeStruct((rows, width), jnp.float32),
             jax.ShapeDtypeStruct(tokens, low),
@@ -1157,14 +1233,14 @@
             pltpu.VMEM(tokens, low),
             pltpu.VMEM(gate.shape, low),
             pltpu.VMEM(up.shape, low),
-            pltpu.VMEM(down.shape, low),
+            pltpu.VMEM(gather_specs[0].shape, low),
             pltpu.VMEM(inner, low),
             pltpu.VMEM(inner, low),
             pltpu.VMEM(inner, low),
             pltpu.VMEM((2, rows, width), low),
             pltpu.VMEM(tokens, low),
             pltpu.VMEM(tokens, low),
-            dma((5,)),
+            dma((6,)),
             dma((2, tensor_size)),
             dma((tensor_size,)),
             dma((2,)),
@@ -1172,6 +1248,7 @@
             dma((tensor_size,)),
             dma((2,)),
         ]
+        + gather_scratch(gather_specs, [], dp_size, tensor_size)[1]
         + scatter_scratch(specs, [down], dp_size, tensor_size, in_place=True),
         compiler_params=pltpu.CompilerParams(
             collective_id=collective_id, has_side_effects=True, vmem_limit_bytes=63 * 2**20
@@ -1182,7 +1259,7 @@
             transcendentals=0,
         ),
     )(
-        normed,
+        normed.reshape(tokens),
         cot_all.reshape(tokens),
         gate,
         up,
@@ -1197,12 +1274,13 @@
         return [refs.pop(0) for _ in range(count)]
 
     sources = take(7)
-    blocks, wq_ref, cos_ref, sin_ref, gain_ref, second_ref = take(6)
+    k_blocks, v_blocks, wq_ref, cos_ref, sin_ref, gain_ref, second_ref = take(7)
     tokens_out, out_sum, query_sum, kv_sum, gain_sum = take(5)
     held = take(7)
     context, middle_low, normed, dq, wkv, tokens, middle = held
-    o_grad, q_grad, kv_grad, gain_grad, wq_tile, kv_landing, kv_low, column_sum = take(8)
-    load_sem, tile_sem, ex_own, ex_send, ex_recv = take(5)
+    o_grad, q_grad, kv_grad, gain_grad, wq_tile, k_landing, v_landing, kv_low, column_sum = take(9)
+    load_sem, tile_sem = take(2)
+    k_sems, v_sems = take(3), take(3)
     run = ScatterRun(
         specs,
         dp_size,
@@ -1229,9 +1307,13 @@
         )
 
     tile_copy(0).start()
-    exchange_run = ExchangeRun(tensor_size, blocks, kv_landing, ex_own, ex_send, ex_recv)
+    exchanges = [
+        ExchangeRun(tensor_size, k_blocks, k_landing, *k_sems),
+        ExchangeRun(tensor_size, v_blocks, v_landing, *v_sems),
+    ]
     greet((run.dp, run.tensor, tensor_size), False, True, run.dp_bits)
-    exchange_run.begin()
+    for exchange in exchanges:
+        exchange.begin()
 
     def out_piece(j):
         tile = min(256, o_rows)
@@ -1261,18 +1343,20 @@
             tokens_out[...] += part
 
     def kv_piece():
-        exchange_run.close()
-        total = kv_landing[0].astype(jnp.float32)
+        for exchange in exchanges:
+            exchange.close()
+        grad_keys = k_landing[0].astype(jnp.float32)
+        grad_values = v_landing[0].astype(jnp.float32)
         for other in range(1, tensor_size):
-            total = total + kv_landing[other].astype(jnp.float32)
-        grad_keys = total[:, :kv_width]
+            grad_keys = grad_keys + k_landing[other].astype(jnp.float32)
+            grad_values = grad_values + v_landing[other].astype(jnp.float32)
         repeat = kv_width // cos_ref.shape[1]
         cosines = jnp.concatenate([cos_ref[...]] * repeat, axis=1)
         sines = jnp.concatenate([sin_ref[...]] * repeat, axis=1)
         kv_low[:, :kv_width] = (grad_keys * cosines - swap_halves(grad_keys) * sines).astype(
             kv_low.dtype
         )
-        kv_low[:, kv_width:] = total[:, kv_width:].astype(kv_low.dtype)
+        kv_low[:, kv_width:] = grad_values.astype(kv_low.dtype)
         for row in range(0, width, 512):
             kv_grad[row : row + 512, :] = product_left(
                 normed[:, row : row + 512], kv_low[...]
@@ -1341,7 +1425,8 @@
     key_value,
     tokens,
     middle,
-    kv_blocks,
+    k_blocks,
+    v_blocks,
     query,
     cosines,
     sines,
@@ -1367,26 +1452,25 @@
     return pl.pallas_call(
         functools.partial(tail_kernel, specs, dp_size, tensor_size),
         out_shape=[jax.ShapeDtypeStruct((rows, width), full)] + scatter_shapes(specs),
-        in_specs=[ANY] * 9 + [VMEM] * 4,
+        in_specs=[ANY] * 10 + [VMEM] * 4,
         out_specs=[VMEM] * (1 + len(specs)),
         scratch_shapes=[pltpu.VMEM(array.shape, array.dtype) for array in loaded]
         + [pltpu.VMEM(array.shape, array.dtype) for array in arrays]
         + [
             pltpu.VMEM((2, width, q_spec.shape[1]), low),
-            pltpu.VMEM(kv_blocks.shape, low),
+            pltpu.VMEM(k_blocks.shape, low),
+            pltpu.VMEM(v_blocks.shape, low),
             pltpu.VMEM((rows, kv_both), low),
             pltpu.VMEM((8, width), full),
             dma((7,)),
             dma((2,)),
-            dma,
-            dma((tensor_size,)),
-            dma((tensor_size,)),
         ]
+        + [dma, dma((tensor_size,)), dma((tensor_size,))] * 2
         + scatter_scratch(specs, arrays, dp_size, tensor_size, in_place=True),
         compiler_params=pltpu.CompilerParams(
             collective_id=collective_id, has_side_effects=True, vmem_limit_bytes=60 * 2**20
         ),
-    )(*loaded, kv_blocks, query, cosines, sines, gain, second)
+    )(*loaded, k_blocks, v_blocks, query, cosines, sines, gain, second)
 
 
 def rope_tables(rows, tensor):
@@ -1443,15 +1527,17 @@
         lambda ref, dp, t: ref.at[
             pl.ds(start_row(dp, q_rows), q_rows), pl.ds(start_row(t, q_cols), q_cols)
         ],
-        lambda ref, dp, half: ref.at[
-            pl.ds(pl.multiple_of(dp * q_rows + half * (q_rows // 2), q_rows // 2), q_rows // 2), :
+        lambda ref, dp, half, j: ref.at[
+            pl.ds(pl.multiple_of(dp * q_rows + half * (q_rows // 2), q_rows // 2), q_rows // 2),
+            pl.ds(start_row(j, q_cols), q_cols),
         ],
+        pieces=tensor_size,
     )
     kv_all_rows = kv_rows * tensor_size
     kv_spec = Gather(
         (width, 2 * kv_width),
         lambda ref, dp, t: ref.at[pl.ds(start_row(dp * tensor_size + t, kv_rows), kv_rows), :],
-        lambda ref, dp, half: ref.at[
+        lambda ref, dp, half, j: ref.at[
             pl.ds(
                 pl.multiple_of(dp * kv_all_rows + half * (kv_all_rows // 2), kv_all_rows // 2),
                 kv_all_rows // 2,
@@ -1462,7 +1548,7 @@
     gain_spec = Gather(
         (dp_size * tensor_size * 16, 128),
         lambda ref, dp, t: ref.at[pl.ds(start_row(dp * tensor_size + t, 16), 16), :],
-        lambda ref, dp, half: ref.at[
+        lambda ref, dp, half, j: ref.at[
             pl.ds(
                 pl.multiple_of((2 * dp + half) * tensor_size * 8, tensor_size * 8),
                 tensor_size * 8,
@@ -1475,7 +1561,7 @@
         lambda ref, dp, t: ref.at[
             pl.ds(start_row(t, o_rows), o_rows), pl.ds(start_row(dp, o_cols), o_cols)
         ],
-        lambda ref, dp, half: ref.at[
+        lambda ref, dp, half, j: ref.at[
             pl.ds(half * (heads * HEAD_DIM // 2), heads * HEAD_DIM // 2),
             pl.ds(start_row(dp, o_cols), o_cols),
         ],
@@ -1488,7 +1574,7 @@
     column_spec = Gather(
         (width, units),
         lambda ref, dp, t: ref.at[pl.ds(start_row(dp, up_rows), up_rows), :],
-        lambda ref, dp, half: ref.at[
+        lambda ref, dp, half, j: ref.at[
             pl.ds(
                 pl.multiple_of(dp * up_rows + half * (up_rows // 2), up_rows // 2), up_rows // 2
             ),
@@ -1500,7 +1586,7 @@
     down_spec = Gather(
         (units, width),
         lambda ref, dp, t: ref.at[:, pl.ds(start_row(dp, down_cols), down_cols)],
-        lambda ref, dp, half: ref.at[
+        lambda ref, dp, half, j: ref.at[
             pl.ds(half * (units // 2), units // 2), pl.ds(start_row(dp, down_cols), down_cols)
         ],
         False,
@@ -1512,23 +1598,22 @@
         queries,
         log_sums,
         normed_first,
-        normed_own,
         middle,
         gain_rows,
         kv_all,
+        normed_all,
         key_value_full,
         _,
         query_full,
         out_full,
         gate_full,
         up_full,
-        down_full,
         cot_all,
     ) = front(
         tokens,
         cosines,
         sines,
-        [key_value, gains, w_query, w_out, w_gate, w_up, w_down, cotangent],
+        [key_value, gains, w_query, w_out, w_gate, w_up, cotangent],
         [
             kv_spec,
             gain_spec,
@@ -1536,44 +1621,35 @@
             out_spec,
             column_spec,
             column_spec,
-            down_spec,
             row_spec(cotangent.shape),
         ],
         row_spec((rows, 2 * kv_width)),
+        row_spec((rows, width)),
         heads,
         group_heads,
         sizes,
         1,
     )
-    gain_first, gain_second = gain_rows[0], gain_rows[1]
-    scale_second = lax.rsqrt(jnp.mean(middle * middle, axis=-1, keepdims=True) + epsilon)
-    unit_second = middle * scale_second
     column_scatter = Scatter(
         "dp",
         (up_rows, units),
-        lambda ref, dp, half, j: column_spec.half(ref, dp, half),
+        column_spec.half,
         (up_rows // 2, units),
         lambda ref, half: ref.at[pl.ds(half * (up_rows // 2), up_rows // 2), :],
     )
     down_scatter = Scatter(
         "dp",
         (units, down_cols),
-        lambda ref, dp, half, j: down_spec.half(ref, dp, half),
+        down_spec.half,
         (units // 2, down_cols),
         lambda ref, half: ref.at[pl.ds(half * (units // 2), units // 2), :],
     )
     back_second, mlp_part, grad_gate_w, grad_up_w, sum_down = feed_forward(
-        normed_own, cot_all, gate_full, up_full, down_full, [down_scatter], sizes, 3
+        normed_all, cot_all, gate_full, up_full, w_down, [down_spec], [down_scatter], sizes, 3
     )
     mlp_rows = lax.psum_scatter(
         mlp_part.reshape(tensor_size * rows, width), "tensor", scatter_dimension=0, tiled=True
     )
-    grad_gain_second = jnp.sum(back_second * unit_second, axis=0)
-    grad_middle = cotangent.astype(jnp.float32) + norm_back(
-        back_second, unit_second, scale_second, gain_second
-    )
-    middle_low = grad_middle.astype(jnp.bfloat16)
-    grad_context = product_right(middle_low, out_full).astype(jnp.bfloat16)
     query_scatter = Scatter(
         "own",
         (q_rows, q_cols),
@@ -1619,13 +1695,26 @@
         lambda ref, j: ref,
         (8, gain_cols),
     )
-    grad_queries, grad_keys, grad_values, sum_gate, sum_up = attend_back(
+    (
+        grad_queries,
+        grad_keys,
+        grad_values,
+        grad_middle,
+        middle_low,
+        grad_gain_second,
+        sum_gate,
+        sum_up,
+    ) = attend_back(
         queries,
-        grad_context,
+        out_full,
         log_sums,
         cosines,
         sines,
         kv_all,
+        back_second,
+        middle,
+        cotangent,
+        gain_rows[1:2],
         heads,
         group_heads,
         [column_scatter, column_scatter],
@@ -1633,7 +1722,6 @@
         sizes,
         7,
     )
-    grad_kv = jnp.concatenate([grad_keys, grad_values], axis=1)
     grad_tokens, sum_out, sum_query, sum_kv, sum_gains = tail(
         context,
         middle_low,
@@ -1642,12 +1730,13 @@
         key_value_full,
         tokens,
         grad_middle,
-        grad_kv.reshape(tensor_size, rows, 2 * kv_width),
+        grad_keys.reshape(tensor_size, rows, kv_width),
+        grad_values.reshape(tensor_size, rows, kv_width),
         query_full,
         cosines,
         sines,
-        gain_first.reshape(1, width),
-        grad_gain_second.reshape(1, width),
+        gain_rows[0:1],
+        grad_gain_second,
         [out_scatter, query_scatter, kv_scatter, gain_scatter],
         sizes,
         5,

time: 552 us -> 526 us (0.953)
  Pallas kernels: 496 us -> 483 us
  other arithmetic: 11.8 us -> 6.24 us
    pallas_call x2, Pallas kernels: 324 us -> 306 us  [the longest x1 173 us: front(): pl.pallas_call(functools.partial(front_kernel, specs, kv_spec, n_spec, gr...]
    pallas_call x1, Pallas kernels: 59.1 us -> 65.8 us  [attend_back(): pl.pallas_call(functools.partial(attend_back_kernel, group_pairs, pairs,...]
    unnamed x28 -> x20, local copies, waits for them, and re-layouts: 12 us -> 7.06 us
  transfers between devices with their start and end apart: 1 -> 1, of which waited for: 0 -> 0; matrix products, arithmetic and copies ran while one was open for 2% -> 1% of each run, Pallas kernels for 32% -> 34%
where the time goes in v5:
time: 526 us; the launch traced here: 517 us
  Pallas kernels  483 us (92%)
  between operations  14.6 us (3%)
  local copies, waits for them, and re-layouts  12.9 us (2%)
  other arithmetic  6.24 us (1%)
    pallas_call x1, Pallas kernels, front(): pl.pallas_call(functools.partial(front_kernel, specs, kv_spec, n_spec, gr...  173 us
    pallas_call x1, Pallas kernels, feed_forward(): pl.pallas_call(functools.partial(mlp_kernel, gather_specs, specs, dp_size...  133 us
    pallas_call x1, Pallas kernels, tail(): pl.pallas_call(functools.partial(tail_kernel, specs, dp_size, tensor_size...  111 us
    pallas_call x1, Pallas kernels, attend_back(): pl.pallas_call(functools.partial(attend_back_kernel, group_pairs, pairs,...  65.8 us
  transfers between devices with their start and end apart: 1, of which 0 were waited for; matrix products, arithmetic and copies ran while one was open for 1% of the time, Pallas kernels for 34%

profile of v5, /device:TPU:25, one launch (start us, length us, event | category | flops | bytes accessed | tf_op | source)
XLA Modules:
  0.0 516.7 jit_solution(1402997047273401676)
XLA Ops:
  7.2 0.0 reduce-scatter.2.cloned.1.call-start
  7.3 0.7 tile.20
  7.9 0.1 tile.21
  8.0 0.7 tile.8
  8.7 0.1 tile.9
  8.8 0.5 fusion
  9.3 1.4 pad_maximum_fusion.2.refs_3_
  10.7 1.0 pad_maximum_fusion
  11.7 0.7 and_select_fusion.refs_4_
  12.4 173.1 %shard_map.194 = (bf16[256,2048]{1,0:T(8,128)(2,1)}, bf16[256,2048]{1,0:T(8,128)(2,1)}, f32[16,2,256]{2,1,0:T(2,128)}, bf16[256,2048]{1,0:T(8,128)(2,1)}, f32[25...) custom-call(bf16[256,2048]{1,0:T(8,128)(2,1)} %refs_5_.3, ...), custom_call_target="tpu_custom_call" | custom-call | tf_op jit(solution)/shard_map/pallas_call | solution.py:755
  185.4 132.9 %shard_map.195 = (f32[256,2048]{1,0:T(8,128)}, bf16[4,256,2048]{2,1,0:T(8,128)(2,1)}, bf16[2048,1408]{1,0:T(8,128)(2,1)}, bf16[2048,1408]{1,0:T(8,128)(2,1)}, f32[1408,256]{1,0:T(8,128)}) custom-call(bf16[4,256,2048]{2,1,0:T(8,128)(2,1)} %bitcast.12, bf16[4,256,2048]{2,1,0:T(8,128)(2,1)} %bitcast.13, bf16[2048,1408]{1,0:T(8,128)(2,1)} %get-tuple-element.49.gate_ref, ...), custom_call_target="tpu_custom_call" | custom-call | flops 53150220288 | bytes 23068672 | tf_op jit(solution)/shard_map/pallas_call | solution.py:1220
  318.3 0.0 reduce-scatter.2.cloned.1.call-update
  318.4 1.5 fusion.2
  319.9 65.8 %shard_map.196 = (bf16[256,2048]{1,0:T(8,128)(2,1)}, bf16[1024,256]{1,0:T(8,128)(2,1)}, bf16[1024,256]{1,0:T(8,128)(2,1)}, f32[256,2048]{1,0:T(8,128)}, bf16[256...) custom-call(bf16[256,2048]{1,0:T(8,128)(2,1)} %get-tuple-element.53.refs_0_, ...), custom_call_target="tpu_custom_call" | custom-call | flops 5368709120 | bytes 4194304 | tf_op jit(solution)/shard_map/pallas_call | solution.py:915
  385.7 0.0 copy-start
  385.7 111.2 %shard_map.197 = (f32[256,2048]{1,0:T(8,128)}, f32[512,256]{1,0:T(8,128)}, f32[256,512]{1,0:T(8,128)}, f32[64,512]{1,0:T(8,128)}, f32[16,256]{1,0:T(8,128)}) custom-call(bf16[256,2048]{1,0:T(8,128)(2,1)} %get-tuple-element.52.refs_0_, bf16[256,2048]{1,0:T(8,128)(2,1)} %get-tuple-element.61.refs_1_, bf16[256,2048]{1,0:T(8,128)(2,1)} %get-tuple-element.62.refs_2_, ...), custom_call_target="tpu_custom_call" | custom-call | tf_op jit(solution)/shard_map/pallas_call | solution.py:1452
  496.9 1.3 dynamic-slice_bitcast_fusion
  498.2 1.5 fusion.1
  499.7 0.0 reduce-scatter.2.cloned.1.call-done
  499.7 0.0 copy-done
  499.7 0.0 copy-start.1
  499.7 2.6 add_convert_fusion
  502.4 0.0 copy-done.1
  502.4 0.0 copy-start.6
  502.4 0.0 copy-start.5
  502.4 1.3 copy.29
  503.7 0.1 copy-done.6
  503.7 0.0 copy-start.4
  503.7 0.8 copy.30
  504.5 0.0 copy-done.5
  504.5 0.0 copy-start.3
  504.5 0.8 copy.31
  505.3 0.0 copy-done.4
  505.3 1.1 copy.32
  506.4 0.0 copy-done.3
  506.4 0.0 copy-start.2
  506.4 1.1 copy.33
  507.5 0.8 copy-done.2
  508.3 1.1 copy.34
  (4 shorter events, 0.0 us)
Async XLA Ops:
  7.2 492.5 %reduce-scatter.2.cloned.1.call-start = ((), (), s32[]{:S(2)}) async-start(), calls=%async_computation.1 | async-start | bytes 5242880 | tf_op jit(solution)/shard_map/reduce_scatter | solution.py:1650
  385.7 114.1 %copy-start = (f32[256,2048]{1,0:T(8,128)S(1)}, f32[256,2048]{1,0:T(8,128)}, u32[]{:S(2)}) copy-start(f32[256,2048]{1,0:T(8,128)} %get-tuple-element.71.refs_8_) | copy-start | bytes 6291460
  499.7 2.6 copy-start.1
  502.4 1.4 copy-start.6
  502.4 2.2 copy-start.5
  503.7 1.6 copy-start.4
  504.5 1.9 copy-start.3
  506.4 1.9 copy-start.2
Sparse Core Ops, SparseCore 0:
  318.5 77.7 reduce-scatter.1

commit v6 on v5

--- a/solution.py
+++ b/solution.py
@@ -674,17 +674,18 @@
         if j == 1:
             for step in steps[-1:]:
                 kv_run.line(0, step)
+            run.line(cot, 1)
     pairs = lse_ref.shape[0]
     plan = [
         (0.3, lambda: hops(near, out)),
         (0.31, lambda: hops([0], gate)),
         (0.75, lambda: hops(far, out)),
-        (0.88, lambda: hops(near, gate)),
         (0.89, lambda: hops([0], up)),
     ]
     early = max(1, tensor_size - 2)
-    for step in steps[:early]:
-        plan.append((0.2 + 0.75 * (step - 1) / early, functools.partial(run.line, cot, step)))
+    for step in steps[1:early]:
+        time = 0.52 + 0.4 * (step - 2) / early
+        plan.append((time, functools.partial(run.line, cot, step)))
     plan.sort(key=lambda entry: entry[0])
 
     def pair_step(pair, carry):
@@ -704,6 +705,7 @@
 
     lax.fori_loop(0, pairs, pair_step, 0)
     hops(core, out)
+    hops(near, gate)
     out_load = pltpu.make_async_copy(outs[out], weights, load_sem.at[0])
     out_load.start()
     out_load.wait()
@@ -799,7 +801,8 @@
 
 def attend_back_kernel(group_pairs, pairs, specs, dp_size, tensor_size, *refs):
     refs = list(refs)
-    q_ref, out_ref, lse_ref, cos_ref, sin_ref, k_ref, v_ref = (refs.pop(0) for _ in range(7))
+    q_ref, context_ref, out_ref = (refs.pop(0) for _ in range(3))
+    lse_ref, cos_ref, sin_ref, k_ref, v_ref = (refs.pop(0) for _ in range(5))
     back_ref, middle_ref, cot_ref, gain_ref = (refs.pop(0) for _ in range(4))
     sources = [refs.pop(0) for _ in specs]
     dq_ref, dk_ref, dv_ref, grad_middle, middle_low, gain_sum = (refs.pop(0) for _ in range(6))
@@ -838,6 +841,16 @@
         gain_sum[...] = jnp.sum(column_sum[...], axis=0, keepdims=True)
 
     grad_context = product_right(middle_low[...], out_ref[...])
+    grad_low = grad_context.astype(jnp.bfloat16)
+    heads_at = lax.broadcasted_iota(jnp.int32, (8, 128), 0)
+    own_lanes = lax.div(lanes_of((8, 128)), HEAD_DIM) == heads_at
+    mixed_sums = lax.dot_general(
+        jnp.where(own_lanes, 1.0, 0.0),
+        grad_low.astype(jnp.float32) * context_ref[...].astype(jnp.float32),
+        (((1,), (1,)), ((), ())),
+        precision=lax.Precision.HIGHEST,
+        preferred_element_type=jnp.float32,
+    )
 
     @pl.when(pair % group_pairs == 0)
     def _():
@@ -851,7 +864,7 @@
     open_at = allowed(k_left.shape[0], rows, start)
     grads = []
     for head in (0, 1):
-        queries, grad_out = q_ref[...], grad_context.astype(jnp.bfloat16)
+        queries, grad_out = q_ref[...], grad_low
         if head == 1:
             queries = pltpu.roll(queries.astype(jnp.float32), HEAD_DIM, 1).astype(jnp.bfloat16)
             grad_out = pltpu.roll(grad_context, HEAD_DIM, 1).astype(jnp.bfloat16)
@@ -859,9 +872,8 @@
         scores = jnp.where(open_at, scores, -1e30)
         softmaxed = jnp.exp(scores - lse_ref[0, head, :][None, :])
         grad_soft = product_right(v_left[...], grad_out)
-        mixed = softmaxed * grad_soft
-        mixed_sum = jnp.sum(mixed, axis=0, keepdims=True)
-        grad_scores = (mixed - softmaxed * mixed_sum).astype(jnp.bfloat16)
+        mixed_sum = mixed_sums[head : head + 1, :]
+        grad_scores = (softmaxed * (grad_soft - mixed_sum)).astype(jnp.bfloat16)
         dv_sum[...] += product(softmaxed.astype(jnp.bfloat16), grad_out)
         dk_sum[...] += product(grad_scores, queries)
         grads.append(product(k_turned[...], grad_scores))
@@ -888,6 +900,7 @@
 
 def attend_back(
     queries,
+    context,
     out_full,
     lse,
     cosines,
@@ -926,6 +939,7 @@
         + scatter_shapes(specs),
         in_specs=[
             wide,
+            wide,
             pl.BlockSpec((128, width), lambda p: (p, 0)),
             pl.BlockSpec((1, 2, rows), lambda p: (p, 0, 0)),
             table,
@@ -953,6 +967,7 @@
         ),
     )(
         queries,
+        context,
         out_full,
         lse,
         cosines,
@@ -1118,14 +1133,6 @@
         silu = gate_pre * sigmoid
         active = (silu * upward).astype(jnp.bfloat16)
         hidden[block] = active
-        slot = lax.rem(place, 2)
-
-        @pl.when(place >= 2)
-        def _():
-            y_copy(block, slot).wait()
-
-        y_stage[slot] = product(active, down[...]).astype(jnp.bfloat16)
-        y_copy(block, slot).start()
         grad_hidden = product_right(cot[block], down[...])
         low_gate = (
             grad_hidden * upward * sigmoid * (1.0 + gate_pre * (1.0 - sigmoid))
@@ -1143,6 +1150,15 @@
         def _():
             stage[block] = back.astype(stage.dtype)
             b_copy(block, tensor).start()
+
+        slot = lax.rem(place, 2)
+
+        @pl.when(place >= 2)
+        def _():
+            y_copy(block, slot).wait()
+
+        y_stage[slot] = product(active, down[...]).astype(jnp.bfloat16)
+        y_copy(block, slot).start()
 
         return carry
 
@@ -1475,14 +1491,12 @@
 
 def rope_tables(rows, tensor):
     halved = HEAD_DIM // 2
-    freqs = theta_base ** (-2.0 * jnp.arange(halved, dtype=jnp.float32) / HEAD_DIM)
+    lane = lax.rem(jnp.arange(128), HEAD_DIM)
+    turn = lax.rem(lane, halved).astype(jnp.float32)
+    freqs = theta_base ** (-2.0 * turn / HEAD_DIM)
     places = (tensor * rows + jnp.arange(rows)).astype(jnp.float32)
     angles = places[:, None] * freqs[None, :]
-    cosines, sines = jnp.cos(angles), jnp.sin(angles)
-    return (
-        jnp.concatenate([cosines, cosines] * 2, axis=1),
-        jnp.concatenate([-sines, sines] * 2, axis=1),
-    )
+    return jnp.cos(angles), jnp.where(lane < halved, -1.0, 1.0)[None, :] * jnp.sin(angles)
 
 
 def start_row(dp, size):
@@ -1706,6 +1720,7 @@
         sum_up,
     ) = attend_back(
         queries,
+        context,
         out_full,
         log_sums,
         cosines,

time: 526 us -> 521 us (level)
  no operation moved by 1% of the time
where the time goes in v6:
time: 521 us; the launch traced here: 512 us
  Pallas kernels  479 us (92%)
  between operations  14.6 us (3%)
  local copies, waits for them, and re-layouts  12.9 us (2%)
  other arithmetic  5.97 us (1%)
    pallas_call x1, Pallas kernels, front(): pl.pallas_call(functools.partial(front_kernel, specs, kv_spec, n_spec, gr...  173 us
    pallas_call x1, Pallas kernels, feed_forward(): pl.pallas_call(functools.partial(mlp_kernel, gather_specs, specs, dp_size...  131 us
    pallas_call x1, Pallas kernels, tail(): pl.pallas_call(functools.partial(tail_kernel, specs, dp_size, tensor_size...  111 us
    pallas_call x1, Pallas kernels, attend_back(): pl.pallas_call(functools.partial(attend_back_kernel, group_pairs, pairs,...  63.8 us
  transfers between devices with their start and end apart: 1, of which 0 were waited for; matrix products, arithmetic and copies ran while one was open for 1% of the time, Pallas kernels for 34%

profile of v6, /device:TPU:25, one launch (start us, length us, event | category | flops | bytes accessed | tf_op | source)
XLA Modules:
  0.0 512.4 jit_solution(17577580004546443024)
XLA Ops:
  7.2 0.0 reduce-scatter.2.cloned.1.call-start
  7.3 0.7 tile.20
  7.9 0.1 tile.21
  8.0 0.7 tile.8
  8.7 0.1 tile.9
  8.8 1.4 pad_maximum_fusion.refs_3_
  10.2 1.2 fusion
  11.4 0.7 and_select_fusion.refs_4_
  12.1 172.7 %shard_map.194 = (bf16[256,2048]{1,0:T(8,128)(2,1)}, bf16[256,2048]{1,0:T(8,128)(2,1)}, f32[16,2,256]{2,1,0:T(2,128)}, bf16[256,2048]{1,0:T(8,128)(2,1)}, f32[25...) custom-call(bf16[256,2048]{1,0:T(8,128)(2,1)} %refs_5_.3, ...), custom_call_target="tpu_custom_call" | custom-call | tf_op jit(solution)/shard_map/pallas_call | solution.py:757
  184.8 130.9 %shard_map.195 = (f32[256,2048]{1,0:T(8,128)}, bf16[4,256,2048]{2,1,0:T(8,128)(2,1)}, bf16[2048,1408]{1,0:T(8,128)(2,1)}, bf16[2048,1408]{1,0:T(8,128)(2,1)}, f32[1408,256]{1,0:T(8,128)}) custom-call(bf16[4,256,2048]{2,1,0:T(8,128)(2,1)} %bitcast.12, bf16[4,256,2048]{2,1,0:T(8,128)(2,1)} %bitcast.13, bf16[2048,1408]{1,0:T(8,128)(2,1)} %get-tuple-element.49.gate_ref, ...), custom_call_target="tpu_custom_call" | custom-call | flops 53150220288 | bytes 23068672 | tf_op jit(solution)/shard_map/pallas_call | solution.py:1236
  315.8 0.0 reduce-scatter.2.cloned.1.call-update
  315.8 1.5 fusion.6
  317.3 63.8 %shard_map.196 = (bf16[256,2048]{1,0:T(8,128)(2,1)}, bf16[1024,256]{1,0:T(8,128)(2,1)}, bf16[1024,256]{1,0:T(8,128)(2,1)}, f32[256,2048]{1,0:T(8,128)}, bf16[256...) custom-call(bf16[256,2048]{1,0:T(8,128)(2,1)} %get-tuple-element.53.refs_0_, ...), custom_call_target="tpu_custom_call" | custom-call | flops 5368709120 | bytes 4194304 | tf_op jit(solution)/shard_map/pallas_call | solution.py:928
  381.2 0.0 copy-start
  381.2 111.5 %shard_map.197 = (f32[256,2048]{1,0:T(8,128)}, f32[512,256]{1,0:T(8,128)}, f32[256,512]{1,0:T(8,128)}, f32[64,512]{1,0:T(8,128)}, f32[16,256]{1,0:T(8,128)}) custom-call(bf16[256,2048]{1,0:T(8,128)(2,1)} %get-tuple-element.52.refs_1_.refs_0_, bf16[256,2048]{1,0:T(8,128)(2,1)} %get-tuple-element.61.refs_1_, bf16[256,2048]{1,0:T(8,128)(2,1)} %get-tuple-element.62.refs_2_, ...), custom_call_target="tpu_custom_call" | custom-call | tf_op jit(solution)/shard_map/pallas_call | solution.py:1468
  492.6 1.3 dynamic-slice_bitcast_fusion
  493.9 1.5 fusion.5
  495.5 0.0 reduce-scatter.2.cloned.1.call-done
  495.5 0.0 copy-done
  495.5 0.0 copy-start.1
  495.5 2.6 add_convert_fusion
  498.1 0.0 copy-done.1
  498.1 0.0 copy-start.6
  498.1 0.0 copy-start.5
  498.1 1.3 copy.28
  499.4 0.1 copy-done.6
  499.5 0.0 copy-start.4
  499.5 0.8 copy.29
  500.3 0.0 copy-done.5
  500.3 0.0 copy-start.3
  500.3 0.8 copy.30
  501.1 0.0 copy-done.4
  501.1 1.1 copy.31
  502.2 0.0 copy-done.3
  502.2 0.0 copy-start.2
  502.2 1.1 copy.32
  503.3 0.8 copy-done.2
  504.1 1.1 copy.33
  (4 shorter events, 0.0 us)
Async XLA Ops:
  7.2 488.3 %reduce-scatter.2.cloned.1.call-start = ((), (), s32[]{:S(2)}) async-start(), calls=%async_computation.1 | async-start | bytes 5242880 | tf_op jit(solution)/shard_map/reduce_scatter | solution.py:1664
  381.2 114.3 %copy-start = (f32[256,2048]{1,0:T(8,128)S(1)}, f32[256,2048]{1,0:T(8,128)}, u32[]{:S(2)}) copy-start(f32[256,2048]{1,0:T(8,128)} %get-tuple-element.71.refs_9_) | copy-start | bytes 6291460
  495.5 2.6 copy-start.1
  498.1 1.4 copy-start.6
  498.1 2.2 copy-start.5
  499.5 1.6 copy-start.4
  500.3 1.9 copy-start.3
  502.2 1.9 copy-start.2
Sparse Core Ops, SparseCore 0:
  315.9 79.1 reduce-scatter.1

commit v7 on v6

--- a/solution.py
+++ b/solution.py
@@ -342,7 +342,7 @@
         for half in (0, 1):
             total = self.sum_at(unit, half, 0)
             if spec.kind == "dp":
-                spec.place(self.outs[i], half)[...] = total[...].astype(jnp.float32)
+                spec.place(self.outs[i], half)[...] = total[...]
                 continue
             for other in self.others(unit):
 
@@ -427,7 +427,10 @@
 
 
 def scatter_shapes(specs):
-    return [jax.ShapeDtypeStruct(spec.shape, jnp.float32) for spec in specs]
+    return [
+        jax.ShapeDtypeStruct(spec.shape, jnp.bfloat16 if spec.kind == "dp" else jnp.float32)
+        for spec in specs
+    ]
 
 
 class ExchangeRun:
@@ -1534,7 +1537,11 @@
     spot = lax.rem(lax.axis_index("dp") * tensor_size + tensor_index, per)
     rows_at = lax.broadcasted_iota(jnp.int32, (16, 128), 0)
     here = lax.div(lax.broadcasted_iota(jnp.int32, (16, 128), 1), gain_part) == spot
-    gains = jnp.where(rows_at == 0, jnp.tile(attn_gain, per), jnp.tile(mlp_gain, per))
+    wide = [
+        jnp.broadcast_to(gain.reshape(1, 1, -1), (16, per, gain_part)).reshape(16, 128)
+        for gain in (attn_gain, mlp_gain)
+    ]
+    gains = jnp.where(rows_at == 0, *wide)
     gains = jnp.where(here & (rows_at < 2), gains, jnp.zeros_like(gains))
     query_spec = Gather(
         (width, heads * HEAD_DIM),
@@ -1768,9 +1775,9 @@
         sum_kv[:, kv_width:],
         sum_out,
         sum_gains[8],
-        sum_gate,
-        sum_up,
-        sum_down,
+        sum_gate.astype(jnp.float32),
+        sum_up.astype(jnp.float32),
+        sum_down.astype(jnp.float32),
     )
 
 

time: 521 us -> 519 us (level)
  no operation moved by 1% of the time
where the time goes in v7:
time: 519 us; the launch traced here: 511 us
  Pallas kernels  478 us (92%)
  between operations  14.6 us (3%)
  other arithmetic  9.56 us (2%)
  local copies, waits for them, and re-layouts  8 us (2%)
    pallas_call x1, Pallas kernels, front(): pl.pallas_call(functools.partial(front_kernel, specs, kv_spec, n_spec, gr...  173 us
    pallas_call x1, Pallas kernels, feed_forward(): pl.pallas_call(functools.partial(mlp_kernel, gather_specs, specs, dp_size...  131 us
    pallas_call x1, Pallas kernels, tail(): pl.pallas_call(functools.partial(tail_kernel, specs, dp_size, tensor_size...  111 us
    pallas_call x1, Pallas kernels, attend_back(): pl.pallas_call(functools.partial(attend_back_kernel, group_pairs, pairs,...  63.5 us
  transfers between devices with their start and end apart: 1, of which 0 were waited for; matrix products, arithmetic and copies ran while one was open for 1% of the time, Pallas kernels for 34%

profile of v7, /device:TPU:25, one launch (start us, length us, event | category | flops | bytes accessed | tf_op | source)
XLA Modules:
  0.0 510.6 jit_solution(3647701478426794884)
XLA Ops:
  7.2 0.0 reduce-scatter.2.cloned.1.call-start
  7.3 0.7 broadcast_in_dim.34
  7.9 0.1 broadcast_in_dim.35
  8.0 0.7 broadcast_in_dim.37
  8.7 0.1 broadcast_in_dim.38
  8.8 1.4 pad_maximum_fusion.refs_3_
  10.2 1.2 fusion
  11.4 0.7 and_select_fusion.refs_4_
  12.1 172.8 %shard_map.194 = (bf16[256,2048]{1,0:T(8,128)(2,1)}, bf16[256,2048]{1,0:T(8,128)(2,1)}, f32[16,2,256]{2,1,0:T(2,128)}, bf16[256,2048]{1,0:T(8,128)(2,1)}, f32[25...) custom-call(bf16[256,2048]{1,0:T(8,128)(2,1)} %refs_5_.3, ...), custom_call_target="tpu_custom_call" | custom-call | tf_op jit(solution)/shard_map/pallas_call | solution.py:760
  184.8 130.7 %shard_map.195 = (f32[256,2048]{1,0:T(8,128)}, bf16[4,256,2048]{2,1,0:T(8,128)(2,1)}, bf16[2048,1408]{1,0:T(8,128)(2,1)}, bf16[2048,1408]{1,0:T(8,128)(2,1)}, bf16[1408,256]{1,0:T(8,128)(2,1)}) custom-call(bf16[4,256,2048]{2,1,0:T(8,128)(2,1)} %bitcast.12, bf16[4,256,2048]{2,1,0:T(8,128)(2,1)} %bitcast.13, bf16[2048,1408]{1,0:T(8,128)(2,1)} %get-tuple-element.49.gate_ref, ...), custom_call_target="tpu_custom_call" | custom-call | flops 53150220288 | bytes 23068672 | tf_op jit(solution)/shard_map/pallas_call | solution.py:1239
  315.6 0.0 reduce-scatter.2.cloned.1.call-update
  315.6 1.5 fusion.6
  317.1 63.5 %shard_map.196 = (bf16[256,2048]{1,0:T(8,128)(2,1)}, bf16[1024,256]{1,0:T(8,128)(2,1)}, bf16[1024,256]{1,0:T(8,128)(2,1)}, f32[256,2048]{1,0:T(8,128)}, bf16[256...) custom-call(bf16[256,2048]{1,0:T(8,128)(2,1)} %get-tuple-element.53.refs_0_, ...), custom_call_target="tpu_custom_call" | custom-call | flops 5368709120 | bytes 4194304 | tf_op jit(solution)/shard_map/pallas_call | solution.py:931
  380.6 0.0 copy-start.4
  380.6 111.4 %shard_map.197 = (f32[256,2048]{1,0:T(8,128)}, f32[512,256]{1,0:T(8,128)}, f32[256,512]{1,0:T(8,128)}, f32[64,512]{1,0:T(8,128)}, f32[16,256]{1,0:T(8,128)}) custom-call(bf16[256,2048]{1,0:T(8,128)(2,1)} %get-tuple-element.52.refs_1_.refs_0_, bf16[256,2048]{1,0:T(8,128)(2,1)} %get-tuple-element.61.refs_1_, bf16[256,2048]{1,0:T(8,128)(2,1)} %get-tuple-element.62.refs_2_, ...), custom_call_target="tpu_custom_call" | custom-call | tf_op jit(solution)/shard_map/pallas_call | solution.py:1471
  492.0 0.0 copy-start.3
  492.0 0.0 copy-done.4
  492.0 0.0 copy-start.2
  492.1 1.2 convert_element_type.33
  493.2 0.1 copy-done.3
  493.3 0.0 copy-start.7
  493.3 0.0 copy-start
  493.3 1.2 convert_element_type.34
  494.5 0.0 copy-done.2
  494.5 1.2 convert_element_type.35
  495.7 1.3 dynamic-slice_bitcast_fusion
  497.0 0.0 copy-done.7
  497.0 0.7 fusion.5
  497.7 0.0 reduce-scatter.2.cloned.1.call-done
  497.7 0.0 copy-done
  497.7 0.0 copy-start.1
  497.7 2.6 add_convert_fusion
  500.3 0.0 copy-done.1
  500.3 0.0 copy-start.6
  500.3 0.0 copy-start.5
  500.3 1.3 copy.25
  501.6 0.1 copy-done.6
  501.7 0.8 copy.26
  502.5 0.0 copy-done.5
  502.5 0.8 copy.27
  (4 shorter events, 0.0 us)
Async XLA Ops:
  7.2 490.5 %reduce-scatter.2.cloned.1.call-start = ((), (), s32[]{:S(2)}) async-start(), calls=%async_computation.1 | async-start | bytes 5242880 | tf_op jit(solution)/shard_map/reduce_scatter | solution.py:1671
  380.6 111.5 %copy-start.4 = (bf16[256,1408]{1,0:T(8,128)(2,1)S(1)}, bf16[256,1408]{1,0:T(8,128)(2,1)}, u32[]{:S(2)}) copy-start(bf16[256,1408]{1,0:T(8,128)(2,1)} %get-tuple-element.78) | copy-start | bytes 2162692
  492.0 1.3 copy-start.3
  492.0 2.5 copy-start.2
  493.3 3.7 copy-start.7
  493.3 4.3 copy-start
  497.7 2.6 copy-start.1
  500.3 1.4 copy-start.6
  500.3 2.2 copy-start.5
Sparse Core Ops, SparseCore 0:
  315.7 79.6 reduce-scatter.1
